TPU v7x, 128 devices: a whole 4x4x4 slice. The times are simulated.
128 devices in a mesh: row: 8 (over z, core), col: 16 (over y, x).
Axes of the slice: x: 4, y: 4, z: 4, core: 2. Of those that a mesh axis runs over, the one named last changes fastest.
Arguments:
- slab: float32 [16384, 8192], P(('row', 'col')), may hold values from -6 to 6
- block_mask: int32 [128, 64], P(('row', 'col')), may hold values 0 or 1
Outputs:
- band_gram: float32 [2048, 8192], P('row', 'col')
- factor: float32 [2048, 2048], P('row', 'col')
All inputs are finite; a program needn't handle non-finite values. No bound on the sum of `block_mask` on one device may be relied on, other than what follows from the above.
Results may differ from a plain program's by a relative error of at most 0.000073.
Values sent between devices are 32-bit elements; how exact they have to be, the bound alone decides.
No kernel may reach another device: no remote copies, remote signals or barrier semaphores. Data moves between devices by JAX's collectives and lax.ppermute only.
A program may use at most 192 MiB of HBM per device.

v0:
```python
import jax
import jax.numpy as jnp
from jax import lax
from jax.sharding import PartitionSpec as P

BLK = 128
SHIFT_NUM = 2


def shards(slab, block_mask):
    items = slab.shape[1]
    blocks = block_mask.shape[1]
    width = items // blocks
    keep = jnp.broadcast_to(block_mask.astype(jnp.float32)[:, :, None], (1, blocks, width)).reshape(
        1, items
    )
    dense = slab * keep
    ncols = lax.axis_size("col")
    nrows = lax.axis_size("row")
    local = lax.all_to_all(dense, "col", split_axis=1, concat_axis=0, tiled=True)
    band_cols = lax.all_gather(local[:, :BLK], "col", axis=1, tiled=True)
    partial_gram = jnp.dot(
        band_cols.T, local, precision=lax.Precision.HIGHEST, preferred_element_type=jnp.float32
    )
    total_users = local.shape[0] * nrows
    tile = lax.psum_scatter(partial_gram, "row", scatter_dimension=0, tiled=True) / total_users
    band_width = BLK * ncols
    strip = lax.all_gather(tile[:, :BLK], "col", axis=1, tiled=True)
    panel = lax.all_gather(strip, "row", axis=0, tiled=True)
    panel = panel + SHIFT_NUM / 4.0 * jnp.eye(band_width, dtype=jnp.float32)
    lower = jnp.linalg.cholesky(panel)
    row_count = band_width // nrows
    start_row = lax.axis_index("row") * row_count
    start_col = lax.axis_index("col") * BLK
    piece = lax.dynamic_slice(lower, (start_row, start_col), (row_count, BLK))
    return (tile, piece)


def solution(mesh):
    placed = (P(("row", "col"), None), P(("row", "col"), None))
    return jax.shard_map(
        shards,
        mesh=mesh,
        in_specs=placed,
        out_specs=(P("row", "col"), P("row", "col")),
        check_vma=False,
    )
```

profile of v0, /device:TPU:17, one launch (start us, length us, event | category | flops | bytes accessed | tf_op | source)
XLA Modules:
  0.0 931.0 jit_solution(5694570710533823759)
XLA Ops:
  7.2 5.6 copy.6
  18.5 54.6 %all_to_all.19 = f32[128,16,512]{0,2,1:T(8,128)} all-to-all(f32[128,16,512]{0,2,1:T(8,128)S(1)} %bitcast.91), channel_id=1, replica_groups=mesh['row'=8,'col'=16] {'col'}, dimensions={1} | all-to-all | bytes 8388608 | tf_op jit(solution)/shard_map/all_to_all | solution.py:20
  80.8 120.1 %all-gather.4.cloned.1.call-done = f32[2048,2048]{1,0:T(8,128)} async-done(((f32[2048,128]{1,0:T(8,128)}), f32[2048,2048]{1,0:T(8,128)}) %all-gather.4.cloned.1.call-update) | async-done | bytes 16777232 | tf_op jit(solution)/shard_map/all_gather | solution.py:21
  200.9 31.6 %fusion.109 = f32[2048,512]{1,0:T(8,128)} fusion(f32[2048,2048]{1,0:T(8,128)} %all-gather.4.cloned.1.call-done, f32[2048,512]{1,0:T(8,128)} %bitcast.94), kind=kOutput, calls=%fused_computation.176 | convolution fusion | flops 25769803776 | bytes 25165824 | tf_op jit(solution)/shard_map/dot_general | solution.py:22
  232.6 37.2 %reduce-scatter.2.cloned.1.call-done = f32[256,512]{1,0:T(8,128)} async-done(((f32[2048,512]{1,0:T(8,128)}), f32[256,512]{1,0:T(8,128)}) %reduce-scatter.2.cloned.1.call-update) | async-done | bytes 524304 | tf_op jit(solution)/shard_map/reduce_scatter | solution.py:26
  271.6 47.7 %all-gather.6.cloned.1.call-done = f32[256,2048]{1,0:T(8,128)} async-done(((f32[256,128]{1,0:T(8,128)}), f32[256,2048]{1,0:T(8,128)}) %all-gather.6.cloned.1.call-update) | async-done | bytes 2097168 | tf_op jit(solution)/shard_map/all_gather | solution.py:28
  319.3 89.0 %all-gather.8.cloned.1.call-done = f32[2048,2048]{1,0:T(8,128)} async-done(((f32[256,2048]{1,0:T(8,128)}), f32[2048,2048]{1,0:T(8,128)}) %all-gather.8.cloned.1.call-update) | async-done | bytes 16777232 | tf_op jit(solution)/shard_map/all_gather | solution.py:29
  408.3 12.4 %select_add_fusion = f32[2048,2048]{1,0:T(8,128)} fusion(f32[2048,2048]{1,0:T(8,128)} %all-gather.8.cloned.1.call-done), kind=kLoop, calls=%fused_computation.2 | loop fusion | flops 12582912 | bytes 33554432 | tf_op jit(solution)/shard_map/add | solution.py:30
  420.8 17.6 %copy.8 = f32[2048,2048]{0,1:T(8,128)} copy(f32[2048,2048]{1,0:T(8,128)} %select_add_fusion) | data formatting | bytes 33554432 | tf_op jit(solution)/shard_map/add | solution.py:30
  438.4 12.4 %fusion = f32[2048,2048]{1,0:T(8,128)S(1)} fusion(f32[2048,2048]{0,1:T(8,128)} %copy.8, f32[2048,2048]{1,0:T(8,128)} %all-gather.8.cloned.1.call-done), kind=kLoop, calls=%fused_computation.1 | loop fusion | flops 20971520 | bytes 50331648 | tf_op jit(solution)/shard_map/jit(cholesky)/div | solution.py:31
  450.8 5.7 copy-done
  456.5 11.7 %cholesky.456 = f32[128,128]{1,0:T(8,128)S(1)} custom-call(f32[128,128]{1,0:T(8,128)S(1)} %cholesky.1201), custom_call_target="Cholesky" | custom-call | tf_op jit(solution)/shard_map/jit(cholesky)/cholesky | solution.py:31
  468.2 9.8 %custom-call.123 = f32[1,128,128]{1,2,0:T(8,128)S(1)} custom-call(f32[1,128,128]{2,1,0:T(8,128)S(1)} %get-tuple-element.47), custom_call_target="InvertDiagBlocksLowerTriangular" | custom-call | tf_op jit(solution)/shard_map/jit(cholesky)/cholesky | solution.py:31
  478.1 7.8 cholesky.486
  491.2 11.9 %cholesky.479 = f32[128,128]{1,0:T(8,128)S(1)} custom-call(f32[128,128]{1,0:T(8,128)S(1)} %cholesky.1205), custom_call_target="Cholesky" | custom-call | tf_op jit(solution)/shard_map/jit(cholesky)/cholesky | solution.py:31
  503.7 9.8 %custom-call.124 = f32[1,128,128]{1,2,0:T(8,128)S(1)} custom-call(f32[1,128,128]{2,1,0:T(8,128)S(1)} %get-tuple-element.44), custom_call_target="InvertDiagBlocksLowerTriangular" | custom-call | tf_op jit(solution)/shard_map/jit(cholesky)/cholesky | solution.py:31
  518.8 11.7 %cholesky.502 = f32[128,128]{1,0:T(8,128)S(1)} custom-call(f32[128,128]{1,0:T(8,128)S(1)} %cholesky.1210), custom_call_target="Cholesky" | custom-call | tf_op jit(solution)/shard_map/jit(cholesky)/cholesky | solution.py:31
  531.9 9.8 %custom-call.125 = f32[1,128,128]{1,2,0:T(8,128)S(1)} custom-call(f32[1,128,128]{2,1,0:T(8,128)S(1)} %get-tuple-element.41), custom_call_target="InvertDiagBlocksLowerTriangular" | custom-call | tf_op jit(solution)/shard_map/jit(cholesky)/cholesky | solution.py:31
  548.0 11.7 %cholesky.523 = f32[128,128]{1,0:T(8,128)S(1)} custom-call(f32[128,128]{1,0:T(8,128)S(1)} %cholesky.1215), custom_call_target="Cholesky" | custom-call | tf_op jit(solution)/shard_map/jit(cholesky)/cholesky | solution.py:31
  561.0 9.8 %custom-call.126 = f32[1,128,128]{1,2,0:T(8,128)S(1)} custom-call(f32[1,128,128]{2,1,0:T(8,128)S(1)} %get-tuple-element.38), custom_call_target="InvertDiagBlocksLowerTriangular" | custom-call | tf_op jit(solution)/shard_map/jit(cholesky)/cholesky | solution.py:31
  577.8 11.7 %cholesky.960 = f32[128,128]{1,0:T(8,128)S(1)} custom-call(f32[128,128]{1,0:T(8,128)S(1)} %cholesky.1220), custom_call_target="Cholesky" | custom-call | tf_op jit(solution)/shard_map/jit(cholesky)/cholesky | solution.py:31
  590.8 9.8 %custom-call.127 = f32[1,128,128]{1,2,0:T(8,128)S(1)} custom-call(f32[1,128,128]{2,1,0:T(8,128)S(1)} %get-tuple-element.35), custom_call_target="InvertDiagBlocksLowerTriangular" | custom-call | tf_op jit(solution)/shard_map/jit(cholesky)/cholesky | solution.py:31
  607.7 11.9 %cholesky.980 = f32[128,128]{1,0:T(8,128)S(1)} custom-call(f32[128,128]{1,0:T(8,128)S(1)} %cholesky.1225), custom_call_target="Cholesky" | custom-call | tf_op jit(solution)/shard_map/jit(cholesky)/cholesky | solution.py:31
  620.9 9.8 %custom-call.128 = f32[1,128,128]{1,2,0:T(8,128)S(1)} custom-call(f32[1,128,128]{2,1,0:T(8,128)S(1)} %get-tuple-element.32), custom_call_target="InvertDiagBlocksLowerTriangular" | custom-call | tf_op jit(solution)/shard_map/jit(cholesky)/cholesky | solution.py:31
  632.2 5.6 fusion.26
  637.9 11.7 %cholesky.1000 = f32[128,128]{1,0:T(8,128)S(1)} custom-call(f32[128,128]{1,0:T(8,128)S(1)} %cholesky.1230), custom_call_target="Cholesky" | custom-call | tf_op jit(solution)/shard_map/jit(cholesky)/cholesky | solution.py:31
  650.9 10.0 %custom-call.129 = f32[1,128,128]{1,2,0:T(8,128)S(1)} custom-call(f32[1,128,128]{2,1,0:T(8,128)S(1)} %get-tuple-element.29), custom_call_target="InvertDiagBlocksLowerTriangular" | custom-call | tf_op jit(solution)/shard_map/jit(cholesky)/cholesky | solution.py:31
  662.4 6.0 fusion.23
  668.4 11.7 %cholesky.1020 = f32[128,128]{1,0:T(8,128)S(1)} custom-call(f32[128,128]{1,0:T(8,128)S(1)} %cholesky.1235), custom_call_target="Cholesky" | custom-call | tf_op jit(solution)/shard_map/jit(cholesky)/cholesky | solution.py:31
  681.4 10.2 %custom-call.130 = f32[1,128,128]{1,2,0:T(8,128)S(1)} custom-call(f32[1,128,128]{2,1,0:T(8,128)S(1)} %get-tuple-element.26), custom_call_target="InvertDiagBlocksLowerTriangular" | custom-call | tf_op jit(solution)/shard_map/jit(cholesky)/cholesky | solution.py:31
  693.0 5.9 fusion.41
  698.9 11.7 %cholesky.1040 = f32[128,128]{1,0:T(8,128)S(1)} custom-call(f32[128,128]{1,0:T(8,128)S(1)} %cholesky.1240), custom_call_target="Cholesky" | custom-call | tf_op jit(solution)/shard_map/jit(cholesky)/cholesky | solution.py:31
  711.9 9.8 %custom-call.131 = f32[1,128,128]{1,2,0:T(8,128)S(1)} custom-call(f32[1,128,128]{2,1,0:T(8,128)S(1)} %get-tuple-element.23), custom_call_target="InvertDiagBlocksLowerTriangular" | custom-call | tf_op jit(solution)/shard_map/jit(cholesky)/cholesky | solution.py:31
  723.0 6.1 fusion.44
  729.1 11.7 %cholesky.1060 = f32[128,128]{1,0:T(8,128)S(1)} custom-call(f32[128,128]{1,0:T(8,128)S(1)} %cholesky.1245), custom_call_target="Cholesky" | custom-call | tf_op jit(solution)/shard_map/jit(cholesky)/cholesky | solution.py:31
  742.1 9.8 %custom-call.132 = f32[1,128,128]{1,2,0:T(8,128)S(1)} custom-call(f32[1,128,128]{2,1,0:T(8,128)S(1)} %get-tuple-element.20), custom_call_target="InvertDiagBlocksLowerTriangular" | custom-call | tf_op jit(solution)/shard_map/jit(cholesky)/cholesky | solution.py:31
  753.2 5.8 fusion.47
  759.0 11.7 %cholesky.1080 = f32[128,128]{1,0:T(8,128)S(1)} custom-call(f32[128,128]{1,0:T(8,128)S(1)} %cholesky.1250), custom_call_target="Cholesky" | custom-call | tf_op jit(solution)/shard_map/jit(cholesky)/cholesky | solution.py:31
  772.0 9.8 %custom-call.133 = f32[1,128,128]{1,2,0:T(8,128)S(1)} custom-call(f32[1,128,128]{2,1,0:T(8,128)S(1)} %get-tuple-element.17), custom_call_target="InvertDiagBlocksLowerTriangular" | custom-call | tf_op jit(solution)/shard_map/jit(cholesky)/cholesky | solution.py:31
  788.3 12.1 %cholesky.1100 = f32[128,128]{1,0:T(8,128)S(1)} custom-call(f32[128,128]{1,0:T(8,128)S(1)} %cholesky.1255), custom_call_target="Cholesky" | custom-call | tf_op jit(solution)/shard_map/jit(cholesky)/cholesky | solution.py:31
  801.6 9.8 %custom-call.134 = f32[1,128,128]{1,2,0:T(8,128)S(1)} custom-call(f32[1,128,128]{2,1,0:T(8,128)S(1)} %get-tuple-element.14), custom_call_target="InvertDiagBlocksLowerTriangular" | custom-call | tf_op jit(solution)/shard_map/jit(cholesky)/cholesky | solution.py:31
  817.3 11.7 %cholesky.1120 = f32[128,128]{1,0:T(8,128)S(1)} custom-call(f32[128,128]{1,0:T(8,128)S(1)} %cholesky.1260), custom_call_target="Cholesky" | custom-call | tf_op jit(solution)/shard_map/jit(cholesky)/cholesky | solution.py:31
  830.3 9.9 %custom-call.135 = f32[1,128,128]{1,2,0:T(8,128)S(1)} custom-call(f32[1,128,128]{2,1,0:T(8,128)S(1)} %get-tuple-element.11), custom_call_target="InvertDiagBlocksLowerTriangular" | custom-call | tf_op jit(solution)/shard_map/jit(cholesky)/cholesky | solution.py:31
  845.5 11.7 %cholesky.1140 = f32[128,128]{1,0:T(8,128)S(1)} custom-call(f32[128,128]{1,0:T(8,128)S(1)} %cholesky.1265), custom_call_target="Cholesky" | custom-call | tf_op jit(solution)/shard_map/jit(cholesky)/cholesky | solution.py:31
  858.5 9.8 %custom-call.136 = f32[1,128,128]{1,2,0:T(8,128)S(1)} custom-call(f32[1,128,128]{2,1,0:T(8,128)S(1)} %get-tuple-element.8), custom_call_target="InvertDiagBlocksLowerTriangular" | custom-call | tf_op jit(solution)/shard_map/jit(cholesky)/cholesky | solution.py:31
  872.6 11.9 %cholesky.1160 = f32[128,128]{1,0:T(8,128)S(1)} custom-call(f32[128,128]{1,0:T(8,128)S(1)} %cholesky.1270), custom_call_target="Cholesky" | custom-call | tf_op jit(solution)/shard_map/jit(cholesky)/cholesky | solution.py:31
  885.8 9.8 %custom-call.137 = f32[1,128,128]{1,2,0:T(8,128)S(1)} custom-call(f32[1,128,128]{2,1,0:T(8,128)S(1)} %get-tuple-element.5), custom_call_target="InvertDiagBlocksLowerTriangular" | custom-call | tf_op jit(solution)/shard_map/jit(cholesky)/cholesky | solution.py:31
  899.1 11.7 %cholesky.1178 = f32[128,128]{1,0:T(8,128)S(1)} custom-call(f32[128,128]{1,0:T(8,128)S(1)} %convolution_subtract_fusion.2), custom_call_target="Cholesky" | custom-call | tf_op jit(solution)/shard_map/jit(cholesky)/cholesky | solution.py:31
  (90 shorter events, 99.8 us)
Async XLA Ops:
  7.2 193.7 %all-gather.4.cloned.1.call-start = ((), (), s32[]{:S(2)}) async-start(), calls=%async_computation.2 | async-start | bytes 17825792 | tf_op jit(solution)/shard_map/all_gather | solution.py:21
  80.7 189.0 %reduce-scatter.2.cloned.1.call-start = ((), (), s32[]{:S(2)}) async-start(), calls=%async_computation.3 | async-start | bytes 4718592 | tf_op jit(solution)/shard_map/reduce_scatter | solution.py:26
  232.5 86.8 %all-gather.6.cloned.1.call-start = ((), (), s32[]{:S(2)}) async-start(), calls=%async_computation.4 | async-start | bytes 2228224 | tf_op jit(solution)/shard_map/all_gather | solution.py:28
  270.8 150.0 %copy-start.1 = (f32[256,512]{1,0:T(8,128)}, f32[256,512]{1,0:T(8,128)S(1)}, u32[]{:S(2)}) copy-start(f32[256,512]{1,0:T(8,128)S(1)} %broadcast_multiply_fusion.1) | copy-start | bytes 1572868
  271.6 136.7 %all-gather.8.cloned.1.call-start = ((), (), s32[]{:S(2)}) async-start(), calls=%async_computation.5 | async-start | bytes 18874368 | tf_op jit(solution)/shard_map/all_gather | solution.py:29
  450.8 5.7 copy-start
Sparse Core Ops, SparseCore 0:
  80.9 119.9 all-gather.3
  232.6 37.0 reduce-scatter.1
  272.4 46.8 all-gather.5
  320.9 87.4 all-gather.7
where the time goes:
time: 941 us; the launch traced here: 931 us
  other arithmetic  389 us (41%)
  waiting for transfers between devices  294 us (31%)
  matrix products  124 us (13%)
  blocking collectives  54.6 us (6%)
  local copies, waits for them, and re-layouts  45.3 us (5%)
  between operations  24.1 us (3%)
    another operation x62, other arithmetic, shards(): lower = jnp.linalg.cholesky(panel)  356 us
    all_gather x1, waiting for transfers between devices, shards(): band_cols = lax.all_gather(local[:, :BLK], 'col', axis=1, tiled=True)  120 us
    another operation x30, matrix products, shards(): lower = jnp.linalg.cholesky(panel)  92.4 us
    all_gather x1, waiting for transfers between devices, shards(): panel = lax.all_gather(strip, 'row', axis=0, tiled=True)  89 us
    all_to_all x1, blocking collectives, shards(): lax.all_to_all(dense, 'col', split_axis=1, concat_axis=0, tiled=True)  54.6 us
    all_gather x1, waiting for transfers between devices, shards(): strip = lax.all_gather(tile[:, :BLK], 'col', axis=1, tiled=True)  47.7 us
    reduce_scatter x1, waiting for transfers between devices, shards(): lax.psum_scatter(partial_gram, 'row', scatter_dimension=0, tiled=True)  37.2 us
    dot_general x1, matrix products, shards(): jnp.dot(band_cols.T, local, precision=lax.Precision.HIGHEST, preferred_el...  31.6 us
  transfers between devices with their start and end apart: 4, of which 4 were waited for; matrix products, arithmetic and copies ran while one was open for 0% of the time, Pallas kernels for 0%

commit v1 on v0

--- a/solution.py
+++ b/solution.py
@@ -1,10 +1,148 @@
+import functools
+
 import jax
 import jax.numpy as jnp
 from jax import lax
+from jax.experimental import pallas as pl
+from jax.experimental.pallas import tpu as pltpu
 from jax.sharding import PartitionSpec as P
 
 BLK = 128
 SHIFT_NUM = 2
+
+def diag128(F):
+    S = (8, 128)
+    lane = lax.broadcasted_iota(jnp.int32, S, 1)
+    subl = lax.broadcasted_iota(jnp.int32, S, 0)
+    F = list(F)
+    Ws = []
+    onehot = [jnp.where(subl == k, 1.0, 0.0) for k in range(8)]
+    n = len(F)
+    for t in range(n):
+        b = 8 * t
+        C = {s: [jnp.broadcast_to(F[s][:, b + k:b + k + 1], S) for k in range(8)] for s in range(t, n)}
+        inblk = (lane >= b) & (lane < b + 8)
+        X = jnp.where(inblk, jnp.where(lane - b == subl, 1.0, 0.0), F[t])
+        D = C[t]
+        G = jnp.zeros(S, jnp.float32)
+        for k in range(8):
+            d = jnp.broadcast_to(D[k][k:k + 1], S)
+            rs = lax.rsqrt(d)
+            inv = rs * rs
+            g = D[k] - onehot[k]
+            xk = jnp.broadcast_to(X[k:k + 1], S)
+            G = jnp.where(subl == k, xk * rs, G)
+            X = X - g * (xk * inv)
+            for m in range(k + 1, 8):
+                r = jnp.broadcast_to(D[m][k:k + 1], S)
+                D[m] = D[m] - g * (r * inv)
+        Ws.append(jnp.where(lane < b + 8, G, 0.0))
+        V = [jnp.broadcast_to(X[k:k + 1], S) for k in range(8)]
+        for s in range(t + 1, n):
+            f = jnp.where(inblk, 0.0, F[s])
+            for k in range(8):
+                f = f - C[s][k] * V[k]
+            F[s] = f
+    return Ws
+
+def split(x, n):
+    parts = []
+    for i in range(n):
+        h = x.astype(jnp.bfloat16)
+        parts.append(h)
+        if i + 1 < n:
+            x = x - h.astype(jnp.float32)
+    return parts
+
+PAIRS = {2: [(0, 0), (0, 1), (1, 0)], 3: [(0, 0), (0, 1), (1, 0), (0, 2), (1, 1), (2, 0)]}
+
+def dot_nt(a, b):
+    pairs = PAIRS[len(a)]
+    x = jnp.concatenate([a[i] for i, _ in pairs], axis=1)
+    y = jnp.concatenate([b[j] for _, j in pairs], axis=1)
+    return lax.dot_general(x, y, (((1,), (1,)), ((), ())), preferred_element_type=jnp.float32)
+
+BT = 512
+
+def chol_kernel(nparts, place_ref, a_ref, out_ref, *scratch):
+    Ls = scratch[:nparts]
+    P, W = scratch[nparts:]
+    n = a_ref.shape[0]
+    r = place_ref[0]
+    c = place_ref[1]
+
+    def zero(i, _):
+        for L in Ls:
+            L[pl.ds(i * 128, 128), :] = jnp.zeros((128, n), L.dtype)
+        return 0
+    lax.fori_loop(0, n // 128, zero, 0)
+    out_ref[...] = jnp.zeros(out_ref.shape, jnp.float32)
+
+    def column(jj, _):
+        J2 = jj // 2
+        h = jj % 2
+        base = pl.multiple_of(J2 * 256, 256)
+        here = pl.multiple_of(jj * 128, 128)
+        first = base // BT
+
+        @pl.when(h == 0)
+        def _():
+            def rows(i, _):
+                at = pl.ds(pl.multiple_of(i * BT, BT), BT)
+                P[at, :] = a_ref[at, pl.ds(base, 256)]
+                def depth(q, _):
+                    ks = pl.ds(pl.multiple_of(q * 512, 512), 512)
+                    P[at, :] -= dot_nt([L[at, ks] for L in Ls], [L[pl.ds(base, 256), ks] for L in Ls])
+                    return 0
+                lax.fori_loop(0, (base + 511) // 512, depth, 0)
+                return 0
+            lax.fori_loop(first, n // BT, rows, 0)
+
+        @pl.when(h == 1)
+        def _():
+            prev = pl.ds(pl.multiple_of(here - 128, 128), 128)
+            def rows(i, _):
+                at = pl.ds(pl.multiple_of(i * BT, BT), BT)
+                P[at, 128:] -= dot_nt([L[at, prev] for L in Ls], [L[pl.ds(here, 128), prev] for L in Ls])
+                return 0
+            lax.fori_loop(first, n // BT, rows, 0)
+            P[:, :128] = P[:, 128:]
+
+        ws = diag128([P[pl.ds(pl.multiple_of(here + 8 * s, 8), 8), :128] for s in range(16)])
+        for s in range(16):
+            W[8 * s:8 * s + 8, :] = ws[s]
+        w = split(W[...], 3)
+
+        def rows(i, _):
+            at = pl.ds(pl.multiple_of(i * BT, BT), BT)
+            l = dot_nt(split(P[at, :128], 3), w)
+            for L, part in zip(Ls, split(l, nparts)):
+                L[at, pl.ds(here, 128)] = part
+            P[at, :128] = l
+            return 0
+        lax.fori_loop(first, n // BT, rows, 0)
+
+        @pl.when(jj == c)
+        def _():
+            rows = out_ref.shape[0]
+            mine = P[pl.ds(pl.multiple_of(r * rows, rows), rows), :128]
+            row = lax.broadcasted_iota(jnp.int32, mine.shape, 0) + r * rows
+            col = lax.broadcasted_iota(jnp.int32, mine.shape, 1) + here
+            out_ref[...] = jnp.where(row >= col, mine, 0.0)
+        return 0
+    lax.fori_loop(0, n // 128, column, 0)
+
+def chol_piece(panel, place, rows, nparts=3):
+    n = panel.shape[0]
+    return pl.pallas_call(
+        functools.partial(chol_kernel, nparts),
+        out_shape=jax.ShapeDtypeStruct((rows, 128), jnp.float32),
+        in_specs=[pl.BlockSpec(memory_space=pltpu.SMEM), pl.BlockSpec(memory_space=pltpu.VMEM)],
+        out_specs=pl.BlockSpec(memory_space=pltpu.VMEM),
+        scratch_shapes=[pltpu.VMEM((n, n), jnp.bfloat16)] * nparts + [pltpu.VMEM((n, 256), jnp.float32), pltpu.VMEM((128, 128), jnp.float32)],
+        compiler_params=pltpu.CompilerParams(vmem_limit_bytes=56 * 2**20),
+        name="factor",
+    )(place, panel)
 
 
 def shards(slab, block_mask):
@@ -28,11 +166,9 @@
     strip = lax.all_gather(tile[:, :BLK], "col", axis=1, tiled=True)
     panel = lax.all_gather(strip, "row", axis=0, tiled=True)
     panel = panel + SHIFT_NUM / 4.0 * jnp.eye(band_width, dtype=jnp.float32)
-    lower = jnp.linalg.cholesky(panel)
     row_count = band_width // nrows
-    start_row = lax.axis_index("row") * row_count
-    start_col = lax.axis_index("col") * BLK
-    piece = lax.dynamic_slice(lower, (start_row, start_col), (row_count, BLK))
+    place = jnp.stack([lax.axis_index("row"), lax.axis_index("col")]).astype(jnp.int32)
+    piece = chol_piece(panel, place, row_count)
     return (tile, piece)
 
 

time: 941 us -> 564 us (0.60)
  other arithmetic: 389 us -> 19.1 us
  Pallas kernels: 0 us -> 135 us
  matrix products: 124 us -> 31.6 us
  local copies, waits for them, and re-layouts: 45.3 us -> 14.1 us
  between operations: 24.1 us -> 13.8 us
    another operation x62 -> x1, other arithmetic: 356 us -> 0.59 us  [shards(): jnp.stack([lax.axis_index('row'), lax.axis_index('col')]).astype(jnp.int32)]
    pallas_call x0 -> x1, Pallas kernels: none -> 135 us  [chol_piece(): pl.pallas_call(functools.partial(chol_kernel, nparts), out_shape=jax.Shap...]
    another operation x30 -> x0, matrix products: 92.4 us -> none  [shards(): lower = jnp.linalg.cholesky(panel)]
    add x1 -> x0, local copies, waits for them, and re-layouts: 17.6 us -> none  [shards(): panel = panel + SHIFT_NUM / 4.0 * jnp.eye(band_width, dtype=jnp.float32)]
    div x1 -> x0, other arithmetic: 12.4 us -> none  [shards(): lower = jnp.linalg.cholesky(panel)]
where the time goes in v1:
time: 564 us; the launch traced here: 562 us
  waiting for transfers between devices  293 us (52%)
  Pallas kernels  135 us (24%)
  blocking collectives  54.6 us (10%)
  matrix products  31.6 us (6%)
  other arithmetic  19.1 us (3%)
  local copies, waits for them, and re-layouts  14.1 us (2%)
  between operations  13.8 us (2%)
    pallas_call x1, Pallas kernels, chol_piece(): pl.pallas_call(functools.partial(chol_kernel, nparts), out_shape=jax.Shap...  135 us
    all_gather x1, waiting for transfers between devices, shards(): band_cols = lax.all_gather(local[:, :BLK], 'col', axis=1, tiled=True)  120 us
    all_gather x1, waiting for transfers between devices, shards(): panel = lax.all_gather(strip, 'row', axis=0, tiled=True)  88.4 us
    all_to_all x1, blocking collectives, shards(): lax.all_to_all(dense, 'col', split_axis=1, concat_axis=0, tiled=True)  54.6 us
    all_gather x1, waiting for transfers between devices, shards(): strip = lax.all_gather(tile[:, :BLK], 'col', axis=1, tiled=True)  47.5 us
    reduce_scatter x1, waiting for transfers between devices, shards(): lax.psum_scatter(partial_gram, 'row', scatter_dimension=0, tiled=True)  37.1 us
    dot_general x1, matrix products, shards(): jnp.dot(band_cols.T, local, precision=lax.Precision.HIGHEST, preferred_el...  31.6 us
    add x1, other arithmetic, shards(): panel = panel + SHIFT_NUM / 4.0 * jnp.eye(band_width, dtype=jnp.float32)  12.5 us
  transfers between devices with their start and end apart: 4, of which 4 were waited for; matrix products, arithmetic and copies ran while one was open for 0% of the time, Pallas kernels for 0%

profile of v1, /device:TPU:17, one launch (start us, length us, event | category | flops | bytes accessed | tf_op | source)
XLA Modules:
  0.0 562.1 jit_solution(7165547012286770824)
XLA Ops:
  7.2 0.0 copy-start.1
  7.2 0.0 all-gather.4.cloned.1.call-start
  7.2 5.6 copy.4
  12.8 0.0 copy-done.1
  12.8 0.1 broadcast_bitcast_fusion
  12.9 5.0 broadcast_multiply_fusion
  17.9 54.6 %all_to_all.19 = f32[128,16,512]{0,2,1:T(8,128)} all-to-all(f32[128,16,512]{0,2,1:T(8,128)S(1)} %bitcast.11), channel_id=1, replica_groups=mesh['row'=8,'col'=16] {'col'}, dimensions={1} | all-to-all | bytes 8388608 | tf_op jit(solution)/shard_map/all_to_all | solution.py:158
  72.5 5.4 copy.5
  77.9 2.3 slice.8
  80.1 0.0 all-gather.4.cloned.1.call-update
  80.1 0.0 reduce-scatter.2.cloned.1.call-start
  80.2 120.1 %all-gather.4.cloned.1.call-done = f32[2048,2048]{1,0:T(8,128)} async-done(((f32[2048,128]{1,0:T(8,128)}), f32[2048,2048]{1,0:T(8,128)}) %all-gather.4.cloned.1.call-update) | async-done | bytes 16777232 | tf_op jit(solution)/shard_map/all_gather | solution.py:159
  200.3 31.6 %fusion = f32[2048,512]{1,0:T(8,128)} fusion(f32[2048,2048]{1,0:T(8,128)} %all-gather.4.cloned.1.call-done, f32[2048,512]{1,0:T(8,128)} %bitcast.14), kind=kOutput, calls=%fused_computation.7 | convolution fusion | flops 25769803776 | bytes 25165824 | tf_op jit(solution)/shard_map/dot_general | solution.py:160
  231.9 0.0 reduce-scatter.2.cloned.1.call-update
  232.0 0.0 all-gather.6.cloned.1.call-start
  232.0 37.1 %reduce-scatter.2.cloned.1.call-done = f32[256,512]{1,0:T(8,128)} async-done(((f32[2048,512]{1,0:T(8,128)}), f32[256,512]{1,0:T(8,128)}) %reduce-scatter.2.cloned.1.call-update) | async-done | bytes 524304 | tf_op jit(solution)/shard_map/reduce_scatter | solution.py:164
  269.1 1.1 broadcast_multiply_fusion.1
  270.2 0.0 copy-start
  270.2 0.7 slice.9
  271.0 0.0 all-gather.6.cloned.1.call-update
  271.0 0.2 all-gather.8.cloned.1.call-start
  271.2 47.5 %all-gather.6.cloned.1.call-done = f32[256,2048]{1,0:T(8,128)} async-done(((f32[256,128]{1,0:T(8,128)}), f32[256,2048]{1,0:T(8,128)}) %all-gather.6.cloned.1.call-update) | async-done | bytes 2097168 | tf_op jit(solution)/shard_map/all_gather | solution.py:166
  318.7 0.0 all-gather.8.cloned.1.call-update
  318.8 0.6 pad_add_fusion.place_ref
  319.4 88.4 %all-gather.8.cloned.1.call-done = f32[2048,2048]{1,0:T(8,128)} async-done(((f32[256,2048]{1,0:T(8,128)}), f32[2048,2048]{1,0:T(8,128)}) %all-gather.8.cloned.1.call-update) | async-done | bytes 16777232 | tf_op jit(solution)/shard_map/all_gather | solution.py:167
  407.8 12.5 %select_add_fusion.a_ref = f32[2048,2048]{1,0:T(8,128)} fusion(f32[2048,2048]{1,0:T(8,128)} %all-gather.8.cloned.1.call-done), kind=kLoop, calls=%fused_computation | loop fusion | flops 12582912 | bytes 33554432 | tf_op jit(solution)/shard_map/add | solution.py:168
  420.2 0.0 copy-done
  420.2 135.4 %factor.1 = f32[256,128]{1,0:T(8,128)} custom-call(s32[2]{0:T(128)} %pad_add_fusion.place_ref, f32[2048,2048]{1,0:T(8,128)} %select_add_fusion.a_ref), custom_call_target="tpu_custom_call" | custom-call | tf_op jit(solution)/shard_map/factor/pallas_call | solution.py:137
  (1 shorter events, 0.0 us)
Async XLA Ops:
  7.2 5.7 %copy-start.1 = (s32[1,64]{1,0:T(1,128)S(1)}, s32[1,64]{1,0:T(1,128)}, u32[]{:S(2)}) copy-start(s32[1,64]{1,0:T(1,128)} %param.3) | copy-start | bytes 772
  7.2 193.1 %all-gather.4.cloned.1.call-start = ((), (), s32[]{:S(2)}) async-start(), calls=%async_computation.2 | async-start | bytes 17825792 | tf_op jit(solution)/shard_map/all_gather | solution.py:159
  80.1 189.0 %reduce-scatter.2.cloned.1.call-start = ((), (), s32[]{:S(2)}) async-start(), calls=%async_computation.3 | async-start | bytes 4718592 | tf_op jit(solution)/shard_map/reduce_scatter | solution.py:164
  232.0 86.8 %all-gather.6.cloned.1.call-start = ((), (), s32[]{:S(2)}) async-start(), calls=%async_computation.4 | async-start | bytes 2228224 | tf_op jit(solution)/shard_map/all_gather | solution.py:166
  270.2 150.0 %copy-start = (f32[256,512]{1,0:T(8,128)}, f32[256,512]{1,0:T(8,128)S(1)}, u32[]{:S(2)}) copy-start(f32[256,512]{1,0:T(8,128)S(1)} %broadcast_multiply_fusion.1) | copy-start | bytes 1572868
  271.0 136.8 %all-gather.8.cloned.1.call-start = ((), (), s32[]{:S(2)}) async-start(), calls=%async_computation.5 | async-start | bytes 18874368 | tf_op jit(solution)/shard_map/all_gather | solution.py:167
Sparse Core Ops, SparseCore 0:
  80.3 119.9 all-gather.3
  232.1 37.0 reduce-scatter.1
  271.8 46.8 all-gather.5
  320.3 87.4 all-gather.7

commit v2 on v1

--- a/solution.py
+++ b/solution.py
@@ -9,6 +9,7 @@
 
 BLK = 128
 SHIFT_NUM = 2
+
 
 def diag128(F):
     S = (8, 128)
@@ -64,19 +65,55 @@
 
 BT = 512
 
-def chol_kernel(nparts, place_ref, a_ref, out_ref, *scratch):
+
+def chol_kernel(nparts, place_ref, packed_ref, band_ref, out_ref, a_ref, *scratch):
     Ls = scratch[:nparts]
-    P, W = scratch[nparts:]
+    P, W, sems = scratch[nparts:]
     n = a_ref.shape[0]
+    nb = n // BLK
     r = place_ref[0]
     c = place_ref[1]
+
+    copies = []
+    for i in range(nb):
+        src = min(i, nb - 1 - i)
+        first = 0 if 2 * i >= nb else BLK * (nb - i)
+        copies.append(
+            pltpu.make_async_copy(
+                packed_ref.at[pl.ds(BLK * src, BLK), pl.ds(first, BLK * (i + 1))],
+                a_ref.at[pl.ds(BLK * i, BLK), pl.ds(0, BLK * (i + 1))],
+                sems.at[i],
+            )
+        )
+    for copy in copies:
+        copy.start()
 
     def zero(i, _):
         for L in Ls:
             L[pl.ds(i * 128, 128), :] = jnp.zeros((128, n), L.dtype)
         return 0
-    lax.fori_loop(0, n // 128, zero, 0)
+
+    lax.fori_loop(0, nb, zero, 0)
     out_ref[...] = jnp.zeros(out_ref.shape, jnp.float32)
+    for copy in copies:
+        copy.wait()
+
+    for q in range(2):
+        i = 2 * r + q
+        rows_i = pl.multiple_of(i * BLK, BLK)
+        cols_c = pl.multiple_of(c * BLK, BLK)
+
+        @pl.when(c <= i)
+        def _():
+            band_ref[q * BLK:(q + 1) * BLK, :] = a_ref[pl.ds(rows_i, BLK), pl.ds(cols_c, BLK)]
+
+        @pl.when(c > i)
+        def _():
+            band_ref[q * BLK:(q + 1) * BLK, :] = a_ref[pl.ds(cols_c, BLK), pl.ds(rows_i, BLK)].T
+
+    row_of = lax.broadcasted_iota(jnp.int32, (BLK, BLK), 0)
+    col_of = lax.broadcasted_iota(jnp.int32, (BLK, BLK), 1)
+    shift = jnp.where(row_of == col_of, SHIFT_NUM / 4.0, 0.0)
 
     def column(jj, _):
         J2 = jj // 2
@@ -90,24 +127,29 @@
             def rows(i, _):
                 at = pl.ds(pl.multiple_of(i * BT, BT), BT)
                 P[at, :] = a_ref[at, pl.ds(base, 256)]
+
                 def depth(q, _):
                     ks = pl.ds(pl.multiple_of(q * 512, 512), 512)
                     P[at, :] -= dot_nt([L[at, ks] for L in Ls], [L[pl.ds(base, 256), ks] for L in Ls])
                     return 0
+
                 lax.fori_loop(0, (base + 511) // 512, depth, 0)
                 return 0
+
             lax.fori_loop(first, n // BT, rows, 0)
 
         @pl.when(h == 1)
         def _():
             prev = pl.ds(pl.multiple_of(here - 128, 128), 128)
+
             def rows(i, _):
                 at = pl.ds(pl.multiple_of(i * BT, BT), BT)
-                P[at, 128:] -= dot_nt([L[at, prev] for L in Ls], [L[pl.ds(here, 128), prev] for L in Ls])
+                P[at, :128] = P[at, 128:] - dot_nt([L[at, prev] for L in Ls], [L[pl.ds(here, 128), prev] for L in Ls])
                 return 0
+
             lax.fori_loop(first, n // BT, rows, 0)
-            P[:, :128] = P[:, 128:]
-
+
+        P[pl.ds(here, BLK), :BLK] += shift
         ws = diag128([P[pl.ds(pl.multiple_of(here + 8 * s, 8), 8), :128] for s in range(16)])
         for s in range(16):
             W[8 * s:8 * s + 8, :] = ws[s]
@@ -120,6 +162,7 @@
                 L[at, pl.ds(here, 128)] = part
             P[at, :128] = l
             return 0
+
         lax.fori_loop(first, n // BT, rows, 0)
 
         @pl.when(jj == c)
@@ -129,47 +172,105 @@
             row = lax.broadcasted_iota(jnp.int32, mine.shape, 0) + r * rows
             col = lax.broadcasted_iota(jnp.int32, mine.shape, 1) + here
             out_ref[...] = jnp.where(row >= col, mine, 0.0)
+
         return 0
-    lax.fori_loop(0, n // 128, column, 0)
-
-def chol_piece(panel, place, rows, nparts=3):
-    n = panel.shape[0]
+
+    lax.fori_loop(0, nb, column, 0)
+
+
+def chol_piece(packed, place, n, rows, nparts=3):
+    nb = n // BLK
+    flat = jax.ShapeDtypeStruct((rows, BLK), jnp.float32)
+    vmem = pl.BlockSpec(memory_space=pltpu.VMEM)
     return pl.pallas_call(
         functools.partial(chol_kernel, nparts),
-        out_shape=jax.ShapeDtypeStruct((rows, 128), jnp.float32),
-        in_specs=[pl.BlockSpec(memory_space=pltpu.SMEM), pl.BlockSpec(memory_space=pltpu.VMEM)],
-        out_specs=pl.BlockSpec(memory_space=pltpu.VMEM),
-        scratch_shapes=[pltpu.VMEM((n, n), jnp.bfloat16)] * nparts + [pltpu.VMEM((n, 256), jnp.float32), pltpu.VMEM((128, 128), jnp.float32)],
+        out_shape=(flat, flat),
+        in_specs=[pl.BlockSpec(memory_space=pltpu.SMEM), pl.BlockSpec(memory_space=pl.ANY)],
+        out_specs=(vmem, vmem),
+        scratch_shapes=[pltpu.VMEM((n, n), jnp.float32)]
+        + [pltpu.VMEM((n, n), jnp.bfloat16)] * nparts
+        + [pltpu.VMEM((n, 256), jnp.float32), pltpu.VMEM((BLK, BLK), jnp.float32), pltpu.SemaphoreType.DMA((nb,))],
         compiler_params=pltpu.CompilerParams(vmem_limit_bytes=56 * 2**20),
+        cost_estimate=pl.CostEstimate(flops=2 * n * n * n, bytes_accessed=300 * 2**20, transcendentals=n),
         name="factor",
-    )(place, panel)
+    )(place, packed)
+
+
+def mask_kernel(keep_ref, slab_ref, band_ref, rest_ref):
+    c = pl.program_id(0)
+    per = slab_ref.shape[1] // BLK
+    for b in range(per):
+        part = slab_ref[:, b * BLK:(b + 1) * BLK] * keep_ref[0, c * per + b].astype(jnp.float32)
+        if b == 0:
+            band_ref[...] = part
+        else:
+            rest_ref[0, :, (b - 1) * BLK:b * BLK] = part
+
+
+def mask_and_sort(slab, block_mask, ncols, nrows):
+    users, items = slab.shape
+    width = items // ncols
+    other = width - BLK
+    pair = ncols // nrows
+    return pl.pallas_call(
+        mask_kernel,
+        grid=(ncols,),
+        out_shape=(
+            jax.ShapeDtypeStruct((users, BLK * ncols), jnp.float32),
+            jax.ShapeDtypeStruct((nrows, users, pair * other), jnp.float32),
+        ),
+        in_specs=[pl.BlockSpec(memory_space=pltpu.SMEM), pl.BlockSpec((users, width), lambda c: (0, c))],
+        out_specs=(
+            pl.BlockSpec((users, BLK), lambda c: (0, c)),
+            pl.BlockSpec((1, users, other), lambda c: (c // pair, 0, c % pair)),
+        ),
+        name="mask",
+    )(block_mask, slab)
 
 
 def shards(slab, block_mask):
-    items = slab.shape[1]
-    blocks = block_mask.shape[1]
-    width = items // blocks
-    keep = jnp.broadcast_to(block_mask.astype(jnp.float32)[:, :, None], (1, blocks, width)).reshape(
-        1, items
-    )
-    dense = slab * keep
     ncols = lax.axis_size("col")
     nrows = lax.axis_size("row")
-    local = lax.all_to_all(dense, "col", split_axis=1, concat_axis=0, tiled=True)
-    band_cols = lax.all_gather(local[:, :BLK], "col", axis=1, tiled=True)
-    partial_gram = jnp.dot(
-        band_cols.T, local, precision=lax.Precision.HIGHEST, preferred_element_type=jnp.float32
-    )
-    total_users = local.shape[0] * nrows
-    tile = lax.psum_scatter(partial_gram, "row", scatter_dimension=0, tiled=True) / total_users
-    band_width = BLK * ncols
-    strip = lax.all_gather(tile[:, :BLK], "col", axis=1, tiled=True)
-    panel = lax.all_gather(strip, "row", axis=0, tiled=True)
-    panel = panel + SHIFT_NUM / 4.0 * jnp.eye(band_width, dtype=jnp.float32)
-    row_count = band_width // nrows
-    place = jnp.stack([lax.axis_index("row"), lax.axis_index("col")]).astype(jnp.int32)
-    piece = chol_piece(panel, place, row_count)
-    return (tile, piece)
+    r = lax.axis_index("row")
+    c = lax.axis_index("col")
+    pair = ncols // nrows
+    total_users = slab.shape[0] * ncols * nrows
+    high = dict(precision=lax.Precision.HIGH, preferred_element_type=jnp.float32)
+    over_users = (((0,), (0,)), ((), ()))
+
+    band, rest = mask_and_sort(slab, block_mask, ncols, nrows)
+    bands = lax.all_gather(band, "row", axis=0, tiled=True)
+
+    upper = lax.dynamic_slice_in_dim(bands, BLK * r, BLK, 1)
+    lower = lax.dynamic_slice_in_dim(bands, BLK * (ncols - 1 - r), BLK, 1)
+    both = lax.dot_general(jnp.concatenate([lower, upper], axis=1), bands, over_users, **high)
+    padded = jnp.concatenate([jnp.zeros((BLK, BLK * ncols), jnp.float32), both[BLK:]], axis=1)
+    moved = lax.dynamic_slice_in_dim(padded, BLK * r, BLK * (ncols + 1), 1)
+    long = jnp.concatenate([both[:BLK], jnp.zeros((BLK, BLK), jnp.float32)], axis=1)
+    lane = lax.broadcasted_iota(jnp.int32, moved.shape, 1)
+    packed = jnp.where(lane < BLK * (ncols - r), long, moved)
+    pieces = lax.all_to_all(packed, "col", split_axis=0, concat_axis=0, tiled=True)
+    mine = jnp.sum(pieces.reshape(ncols, BLK // ncols, -1), axis=0) / total_users
+    mine, rest = lax.optimization_barrier((mine, rest))
+    panel = lax.all_gather(mine, ("row", "col"), axis=0, tiled=True)
+
+    others = lax.all_to_all(rest, "row", split_axis=0, concat_axis=0, tiled=True)
+    others = others.reshape(-1, others.shape[-1])
+    partial = lax.dot_general(bands, others, over_users, **high)
+    strip = lax.psum_scatter(partial, "col", scatter_dimension=0, tiled=True) / total_users
+    half = strip.shape[1] // pair
+    odd = c % 2
+    own = lax.dynamic_slice_in_dim(strip, half * odd, half, 1)
+    far = lax.dynamic_slice_in_dim(strip, half * (1 - odd), half, 1)
+    at = [(i, j) for i in range(nrows) for j in range(ncols)]
+    to = lambda i, j: i * ncols + j
+    own = lax.ppermute(own, ("row", "col"), [(to(i, j), to(j // 2, 2 * i + j % 2)) for i, j in at])
+    far = lax.ppermute(far, ("row", "col"), [(to(i, j), to(j // 2, 2 * i + 1 - j % 2)) for i, j in at])
+    items = jnp.where(odd == 0, jnp.concatenate([own, far]), jnp.concatenate([far, own]))
+
+    place = jnp.stack([r, c]).astype(jnp.int32)
+    block, piece = chol_piece(panel, place, BLK * ncols, BLK * pair)
+    return (jnp.concatenate([block, items], axis=1), piece)
 
 
 def solution(mesh):

time: 564 us -> 461 us (0.82)
  waiting for transfers between devices: 293 us -> 199 us
  other arithmetic: 19.1 us -> 4.26 us
  local copies, waits for them, and re-layouts: 14.1 us -> 1.45 us
  blocking collectives: 54.6 us -> 64.8 us
  matrix products: 31.6 us -> 22 us
  starting transfers between devices: 0.34 us -> 9.43 us
  Pallas kernels: 135 us -> 143 us
    all_gather x3 -> x2, waiting for transfers between devices: 256 us -> 106 us  [the longest x1 53.7 us: shards(): panel = lax.all_gather(mine, ('row', 'col'), axis=0, tiled=True)]
    reduce_scatter x1, waiting for transfers between devices: 37.1 us -> 77.2 us  [shards(): lax.psum_scatter(partial, 'col', scatter_dimension=0, tiled=True)]
    ppermute x0 -> x2, waiting for transfers between devices: none -> 15 us  [the longest x1 7.8 us: shards(): lax.ppermute(far, ('row', 'col'), [(to(i, j), to(j // 2, 2 * i + 1 - j %...]
    add x1 -> x0, other arithmetic: 12.5 us -> none  [shards(): panel = panel + SHIFT_NUM / 4.0 * jnp.eye(band_width, dtype=jnp.float32)]
    all_to_all x1 -> x2, blocking collectives: 54.6 us -> 64.8 us  [the longest x1 42.9 us: shards(): lax.all_to_all(rest, 'row', split_axis=0, concat_axis=0, tiled=True)]
    dot_general x1 -> x2, matrix products: 31.6 us -> 22 us  [the longest x1 15.7 us: shards(): partial = lax.dot_general(bands, others, over_users, **high)]
    ppermute x0 -> x2, starting transfers between devices: none -> 9.3 us  [the longest x1 8.88 us: shards(): lax.ppermute(own, ('row', 'col'), [(to(i, j), to(j // 2, 2 * i + j % 2))...]
    pallas_call x1 -> x2, Pallas kernels: 135 us -> 143 us  [the longest x1 133 us: chol_piece(): pl.pallas_call(functools.partial(chol_kernel, nparts), out_shape=(flat, f...]
  transfers between devices with their start and end apart: 4 -> 5, of which waited for: 4 -> 5; matrix products, arithmetic and copies ran while one was open for 0% -> 0% of each run, Pallas kernels for 0% -> 0%
where the time goes in v2:
time: 461 us; the launch traced here: 458 us
  waiting for transfers between devices  199 us (43%)
  Pallas kernels  143 us (31%)
  blocking collectives  64.8 us (14%)
  matrix products  22 us (5%)
  between operations  13.8 us (3%)
  starting transfers between devices  9.43 us (2%)
    pallas_call x1, Pallas kernels, chol_piece(): pl.pallas_call(functools.partial(chol_kernel, nparts), out_shape=(flat, f...  133 us
    reduce_scatter x1, waiting for transfers between devices, shards(): lax.psum_scatter(partial, 'col', scatter_dimension=0, tiled=True)  77.2 us
    all_gather x1, waiting for transfers between devices, shards(): panel = lax.all_gather(mine, ('row', 'col'), axis=0, tiled=True)  53.7 us
    all_gather x1, waiting for transfers between devices, shards(): bands = lax.all_gather(band, 'row', axis=0, tiled=True)  52.6 us
    all_to_all x1, blocking collectives, shards(): lax.all_to_all(rest, 'row', split_axis=0, concat_axis=0, tiled=True)  42.9 us
    all_to_all x1, blocking collectives, shards(): lax.all_to_all(packed, 'col', split_axis=0, concat_axis=0, tiled=True)  21.8 us
    dot_general x1, matrix products, shards(): partial = lax.dot_general(bands, others, over_users, **high)  15.7 us
    pallas_call x1, Pallas kernels, mask_and_sort(): pl.pallas_call(mask_kernel, grid=(ncols,), out_shape=(jax.ShapeDtypeStruc...  10.4 us
  transfers between devices with their start and end apart: 5, of which 5 were waited for; matrix products, arithmetic and copies ran while one was open for 0% of the time, Pallas kernels for 0%

profile of v2, /device:TPU:17, one launch (start us, length us, event | category | flops | bytes accessed | tf_op | source)
XLA Modules:
  0.0 457.9 jit_solution(7090733183197931959)
XLA Ops:
  7.2 0.0 all-gather.3.cloned.1.call-start
  7.2 10.4 %mask.1 = (f32[128,2048]{1,0:T(8,128)}, f32[8,128,768]{2,1,0:T(8,128)}) custom-call(s32[1,64]{1,0:T(1,128)} %keep_ref.1, f32[128,8192]{1,0:T(8,128)} %slab_ref.1), custom_call_target="tpu_custom_call" | custom-call | tf_op jit(solution)/shard_map/mask/pallas_call | solution.py:215
  17.6 0.0 all-gather.3.cloned.1.call-update
  17.6 0.0 reduce-scatter.2.cloned.1.call-start
  17.7 52.6 %all-gather.3.cloned.1.call-done = f32[1024,2048]{1,0:T(8,128)} async-done(((f32[128,2048]{1,0:T(8,128)}), f32[1024,2048]{1,0:T(8,128)}) %all-gather.3.cloned.1.call-update) | async-done | bytes 8388624 | tf_op jit(solution)/shard_map/all_gather | solution.py:242
  70.3 1.3 constant_dynamic-slice_fusion.3
  71.6 6.3 %fusion.2 = f32[256,2048]{1,0:T(8,128)S(1)} fusion(f32[1024,2048]{1,0:T(8,128)} %all-gather.3.cloned.1.call-done, f32[1024,128]{1,0:T(8,128)S(1)} %get-tuple-element.15, f32[1024,128]{1,0:T(8,128)S(1)} %get-tuple-element.14), kind=kOutput, calls=%fused_computation.3 | convolution fusion | flops 3221487616 | bytes 11534336 | tf_op jit(solution)/shard_map/dot_general | solution.py:246
  77.8 0.1 fusion.7
  78.0 0.2 fusion.1
  78.2 21.8 %all_to_all.14 = f32[16,8,2176]{2,1,0:T(8,128)S(1)} all-to-all(f32[16,8,2176]{2,1,0:T(8,128)S(1)} %fusion.1), channel_id=1, replica_groups=mesh['row'=8,'col'=16] {'col'}, dimensions={0} | all-to-all | bytes 2228224 | tf_op jit(solution)/shard_map/all_to_all | solution.py:252
  100.0 0.1 reduce_sum.9
  100.0 0.6 broadcast_multiply_fusion.1
  100.7 42.9 %all_to_all.15 = f32[8,128,768]{2,1,0:T(8,128)S(1)} all-to-all(f32[8,128,768]{2,1,0:T(8,128)} %get-tuple-element.12), channel_id=1, replica_groups=mesh['row'=8,'col'=16] {'row'}, dimensions={0} | all-to-all | bytes 6291456 | tf_op jit(solution)/shard_map/all_to_all | solution.py:257
  143.6 15.7 %fusion.8 = f32[2048,768]{1,0:T(8,128)} fusion(f32[1024,2048]{1,0:T(8,128)} %all-gather.3.cloned.1.call-done, f32[1024,768]{1,0:T(8,128)S(1)} %bitcast.8), kind=kOutput, calls=%fused_computation.19 | convolution fusion | flops 9663676416 | bytes 17825792 | tf_op jit(solution)/shard_map/dot_general | solution.py:259
  159.3 0.0 reduce-scatter.2.cloned.1.call-update
  159.4 0.0 all-gather.5.cloned.1.call-start
  159.4 0.7 all-gather.5.cloned.1.call-update
  160.1 77.2 %reduce-scatter.2.cloned.1.call-done = f32[128,768]{1,0:T(8,128)} async-done(((f32[2048,768]{1,0:T(8,128)}), f32[128,768]{1,0:T(8,128)}) %reduce-scatter.2.cloned.1.call-update) | async-done | bytes 393232 | tf_op jit(solution)/shard_map/reduce_scatter | solution.py:260
  237.3 1.0 broadcast_multiply_fusion
  238.4 8.9 %collective-permute-start = (f32[128,384]{1,0:T(8,128)S(1)}, f32[128,384]{1,0:T(8,128)S(1)}, u32[]{:S(2)}, u32[]{:S(2)}) collective-permute-start(f32[128,384]{1,0:T(8,128)S(1)} %get-tuple-element.18), channel_id=1, source_target_pairs={{0,0},{1,1},{2,16},{3,17},{4,32},{5,33},{6,48},{7,49},{8,64},{9,65... | collective-permute-start | bytes 589832 | tf_op jit(solution)/shard_map/ppermute | solution.py:267
  247.3 0.4 collective-permute-start.1
  247.7 0.6 pad_add_fusion.place_ref
  248.3 7.3 %collective-permute-done = f32[128,384]{1,0:T(8,128)S(1)} collective-permute-done((f32[128,384]{1,0:T(8,128)S(1)}, f32[128,384]{1,0:T(8,128)S(1)}, u32[]{:S(2)}, u32[]{:S(2)}) %collective-permute-start) | collective-permute-done | bytes 196640 | tf_op jit(solution)/shard_map/ppermute | solution.py:267
  255.6 7.8 %collective-permute-done.1 = f32[128,384]{1,0:T(8,128)S(1)} collective-permute-done((f32[128,384]{1,0:T(8,128)S(1)}, f32[128,384]{1,0:T(8,128)S(1)}, u32[]{:S(2)}, u32[]{:S(2)}) %collective-permute-start.1) | collective-permute-done | bytes 196640 | tf_op jit(solution)/shard_map/ppermute | solution.py:268
  263.4 53.7 %all-gather.5.cloned.1.call-done.packed_ref = f32[1024,2176]{1,0:T(8,128)} async-done(((f32[8,2176]{1,0:T(8,128)}), f32[1024,2176]{1,0:T(8,128)}) %all-gather.5.cloned.1.call-update) | async-done | bytes 8912912 | tf_op jit(solution)/shard_map/all_gather | solution.py:255
  317.1 132.5 %factor.1 = (f32[256,128]{1,0:T(8,128)}, f32[256,128]{1,0:T(8,128)}) custom-call(s32[2]{0:T(128)} %pad_add_fusion.place_ref, f32[1024,2176]{1,0:T(8,128)} %all-gather.5.cloned.1.call-done.packed_ref), custom_call_target="tpu_custom_call" | custom-call | flops 17179869184 | bytes 314572800 | tf_op jit(solution)/shard_map/factor/pallas_call | solution.py:185
  449.6 1.8 pad_maximum_fusion
  (3 shorter events, 0.1 us)
Async XLA Ops:
  7.2 63.1 %all-gather.3.cloned.1.call-start = ((), (), s32[]{:S(2)}) async-start(), calls=%async_computation.3 | async-start | bytes 9437184 | tf_op jit(solution)/shard_map/all_gather | solution.py:242
  17.6 219.7 %reduce-scatter.2.cloned.1.call-start = ((), (), s32[]{:S(2)}) async-start(), calls=%async_computation.5 | async-start | bytes 6684672 | tf_op jit(solution)/shard_map/reduce_scatter | solution.py:260
  159.4 157.7 %all-gather.5.cloned.1.call-start = ((), (), s32[]{:S(2)}) async-start(), calls=%async_computation.4 | async-start | bytes 8982528 | tf_op jit(solution)/shard_map/all_gather | solution.py:255
  238.4 17.2 %collective-permute-start = (f32[128,384]{1,0:T(8,128)S(1)}, f32[128,384]{1,0:T(8,128)S(1)}, u32[]{:S(2)}, u32[]{:S(2)}) collective-permute-start(f32[128,384]{1,0:T(8,128)S(1)} %get-tuple-element.18), channel_id=1, source_target_pairs={{0,0},{1,1},{2,16},{3,17},{4,32},{5,33},{6,48},{7,49},{8,64},{9,65... | collective-permute-start | bytes 589832 | tf_op jit(solution)/shard_map/ppermute | solution.py:267
  247.3 16.1 %collective-permute-start.1 = (f32[128,384]{1,0:T(8,128)S(1)}, f32[128,384]{1,0:T(8,128)S(1)}, u32[]{:S(2)}, u32[]{:S(2)}) collective-permute-start(f32[128,384]{1,0:T(8,128)S(1)} %get-tuple-element.19), channel_id=1, source_target_pairs={{0,1},{1,0},{2,17},{3,16},{4,33},{5,32},{6,49},{7,48},{8,65},{9,64... | collective-permute-start | bytes 589832 | tf_op jit(solution)/shard_map/ppermute | solution.py:268
Sparse Core Ops, SparseCore 0:
  17.7 52.5 all-gather.2
  159.5 77.8 reduce-scatter.1
  240.9 76.1 all-gather.4

commit v3 on v2

--- a/solution.py
+++ b/solution.py
@@ -196,35 +196,47 @@
     )(place, packed)
 
 
-def mask_kernel(keep_ref, slab_ref, band_ref, rest_ref):
-    c = pl.program_id(0)
-    per = slab_ref.shape[1] // BLK
-    for b in range(per):
-        part = slab_ref[:, b * BLK:(b + 1) * BLK] * keep_ref[0, c * per + b].astype(jnp.float32)
-        if b == 0:
-            band_ref[...] = part
-        else:
-            rest_ref[0, :, (b - 1) * BLK:b * BLK] = part
-
-
-def mask_and_sort(slab, block_mask, ncols, nrows):
+def band_kernel(keep_ref, slab_ref, band_ref):
+    band_ref[...] = slab_ref[...] * keep_ref[0, pl.program_id(0) * keep_ref.shape[1] // pl.num_programs(0)].astype(jnp.float32)
+
+
+def band_columns(slab, block_mask, ncols):
     users, items = slab.shape
-    width = items // ncols
-    other = width - BLK
+    step = items // ncols // BLK
+    return pl.pallas_call(
+        band_kernel,
+        grid=(ncols,),
+        out_shape=jax.ShapeDtypeStruct((users, BLK * ncols), jnp.float32),
+        in_specs=[pl.BlockSpec(memory_space=pltpu.SMEM), pl.BlockSpec((users, BLK), lambda c: (0, c * step))],
+        out_specs=pl.BlockSpec((users, BLK), lambda c: (0, c)),
+        name="mask_band",
+    )(block_mask, slab)
+
+
+def rest_kernel(pair, keep_ref, slab_ref, rest_ref):
+    g = pl.program_id(0)
+    blocks = slab_ref.shape[1] // BLK
+    per = blocks // pair
+    to = 0
+    for b in range(blocks):
+        if b % per:
+            keep = keep_ref[0, g * blocks + b].astype(jnp.float32)
+            rest_ref[0, :, to:to + BLK] = slab_ref[:, b * BLK:(b + 1) * BLK] * keep
+            to += BLK
+
+
+def other_columns(slab, block_mask, ncols, nrows):
+    users, items = slab.shape
     pair = ncols // nrows
+    other = items // nrows - pair * BLK
     return pl.pallas_call(
-        mask_kernel,
-        grid=(ncols,),
-        out_shape=(
-            jax.ShapeDtypeStruct((users, BLK * ncols), jnp.float32),
-            jax.ShapeDtypeStruct((nrows, users, pair * other), jnp.float32),
-        ),
-        in_specs=[pl.BlockSpec(memory_space=pltpu.SMEM), pl.BlockSpec((users, width), lambda c: (0, c))],
-        out_specs=(
-            pl.BlockSpec((users, BLK), lambda c: (0, c)),
-            pl.BlockSpec((1, users, other), lambda c: (c // pair, 0, c % pair)),
-        ),
-        name="mask",
+        functools.partial(rest_kernel, pair),
+        grid=(nrows,),
+        out_shape=jax.ShapeDtypeStruct((nrows, users, other), jnp.float32),
+        in_specs=[pl.BlockSpec(memory_space=pltpu.SMEM), pl.BlockSpec((users, items // nrows), lambda g: (0, g))],
+        out_specs=pl.BlockSpec((1, users, other), lambda g: (g, 0, 0)),
+        cost_estimate=pl.CostEstimate(flops=users * items, bytes_accessed=8 * users * items, transcendentals=0),
+        name="mask_rest",
     )(block_mask, slab)
 
 
@@ -238,7 +250,8 @@
     high = dict(precision=lax.Precision.HIGH, preferred_element_type=jnp.float32)
     over_users = (((0,), (0,)), ((), ()))
 
-    band, rest = mask_and_sort(slab, block_mask, ncols, nrows)
+    band = band_columns(slab, block_mask, ncols)
+    rest = other_columns(slab, block_mask, ncols, nrows)
     bands = lax.all_gather(band, "row", axis=0, tiled=True)
 
     upper = lax.dynamic_slice_in_dim(bands, BLK * r, BLK, 1)
@@ -257,7 +270,12 @@
     others = lax.all_to_all(rest, "row", split_axis=0, concat_axis=0, tiled=True)
     others = others.reshape(-1, others.shape[-1])
     partial = lax.dot_general(bands, others, over_users, **high)
-    strip = lax.psum_scatter(partial, "col", scatter_dimension=0, tiled=True) / total_users
+    panel, partial = lax.optimization_barrier((panel, partial))
+    strip = lax.psum_scatter(partial, "col", scatter_dimension=0, tiled=True)
+
+    place = jnp.stack([r, c]).astype(jnp.int32)
+    block, piece = chol_piece(panel, place, BLK * ncols, BLK * pair)
+    strip, block, piece = lax.optimization_barrier((strip, block, piece))
     half = strip.shape[1] // pair
     odd = c % 2
     own = lax.dynamic_slice_in_dim(strip, half * odd, half, 1)
@@ -266,10 +284,7 @@
     to = lambda i, j: i * ncols + j
     own = lax.ppermute(own, ("row", "col"), [(to(i, j), to(j // 2, 2 * i + j % 2)) for i, j in at])
     far = lax.ppermute(far, ("row", "col"), [(to(i, j), to(j // 2, 2 * i + 1 - j % 2)) for i, j in at])
-    items = jnp.where(odd == 0, jnp.concatenate([own, far]), jnp.concatenate([far, own]))
-
-    place = jnp.stack([r, c]).astype(jnp.int32)
-    block, piece = chol_piece(panel, place, BLK * ncols, BLK * pair)
+    items = jnp.where(odd == 0, jnp.concatenate([own, far]), jnp.concatenate([far, own])) / total_users
     return (jnp.concatenate([block, items], axis=1), piece)
 
 

time: 461 us -> 343 us (0.74)
  waiting for transfers between devices: 199 us -> 86.1 us
  blocking collectives: 64.8 us -> 47.3 us
  starting transfers between devices: 9.43 us -> 16.7 us
  Pallas kernels: 143 us -> 148 us
    reduce_scatter x1, waiting for transfers between devices: 77.2 us -> 0.02 us  [shards(): strip = lax.psum_scatter(partial, 'col', scatter_dimension=0, tiled=True)]
    all_gather x1, waiting for transfers between devices: 53.7 us -> 11.2 us  [shards(): panel = lax.all_gather(mine, ('row', 'col'), axis=0, tiled=True)]
    all_to_all x1 -> x0, blocking collectives: 21.8 us -> none  [shards(): lax.all_to_all(packed, 'col', split_axis=0, concat_axis=0, tiled=True)]
    all_to_all x0 -> x1, waiting for transfers between devices: none -> 8.61 us  [shards(): lax.all_to_all(packed, 'col', split_axis=0, concat_axis=0, tiled=True)]
    all_to_all x0 -> x1, starting transfers between devices: none -> 6.68 us  [shards(): lax.all_to_all(packed, 'col', split_axis=0, concat_axis=0, tiled=True)]
    pallas_call x1 -> x2, Pallas kernels: 10.4 us -> 15.4 us  [the longest x1 9.01 us: band_columns(): pl.pallas_call(band_kernel, grid=(ncols,), out_shape=jax.ShapeDtypeStruct...]
  transfers between devices with their start and end apart: 5 -> 6, of which waited for: 5 -> 5; matrix products, arithmetic and copies ran while one was open for 0% -> 5% of each run, Pallas kernels for 0% -> 41%
where the time goes in v3:
time: 343 us; the launch traced here: 341 us
  Pallas kernels  148 us (43%)
  waiting for transfers between devices  86.1 us (25%)
  blocking collectives  47.3 us (14%)
  matrix products  22 us (6%)
  starting transfers between devices  16.7 us (5%)
  between operations  13.8 us (4%)
  other arithmetic  4.28 us (1%)
    pallas_call x1, Pallas kernels, chol_piece(): pl.pallas_call(functools.partial(chol_kernel, nparts), out_shape=(flat, f...  133 us
    all_gather x1, waiting for transfers between devices, shards(): bands = lax.all_gather(band, 'row', axis=0, tiled=True)  52.7 us
    all_to_all x1, blocking collectives, shards(): lax.all_to_all(rest, 'row', split_axis=0, concat_axis=0, tiled=True)  47.3 us
    dot_general x1, matrix products, shards(): partial = lax.dot_general(bands, others, over_users, **high)  15.7 us
    all_gather x1, waiting for transfers between devices, shards(): panel = lax.all_gather(mine, ('row', 'col'), axis=0, tiled=True)  11.2 us
    ppermute x1, waiting for transfers between devices, shards(): lax.ppermute(own, ('row', 'col'), [(to(i, j), to(j // 2, 2 * i + j % 2))...  9.77 us
    pallas_call x1, Pallas kernels, band_columns(): pl.pallas_call(band_kernel, grid=(ncols,), out_shape=jax.ShapeDtypeStruct...  9.01 us
    all_to_all x1, waiting for transfers between devices, shards(): lax.all_to_all(packed, 'col', split_axis=0, concat_axis=0, tiled=True)  8.61 us
  transfers between devices with their start and end apart: 6, of which 5 were waited for; matrix products, arithmetic and copies ran while one was open for 5% of the time, Pallas kernels for 41%

profile of v3, /device:TPU:17, one launch (start us, length us, event | category | flops | bytes accessed | tf_op | source)
XLA Modules:
  0.0 340.6 jit_solution(13977279634014813500)
XLA Ops:
  7.2 0.0 all-gather.3.cloned.1.call-start
  7.2 9.0 %mask_band.1 = f32[128,2048]{1,0:T(8,128)} custom-call(s32[1,64]{1,0:T(1,128)} %keep_ref.3, f32[128,8192]{1,0:T(8,128)} %slab_ref.3), custom_call_target="tpu_custom_call" | custom-call | tf_op jit(solution)/shard_map/mask_band/pallas_call | solution.py:206
  16.2 0.0 all-gather.3.cloned.1.call-update
  16.3 52.7 %all-gather.3.cloned.1.call-done = f32[1024,2048]{1,0:T(8,128)} async-done(((f32[128,2048]{1,0:T(8,128)}), f32[1024,2048]{1,0:T(8,128)}) %all-gather.3.cloned.1.call-update) | async-done | bytes 8388624 | tf_op jit(solution)/shard_map/all_gather | solution.py:255
  69.0 1.3 constant_dynamic-slice_fusion.3
  70.2 6.2 %fusion.2 = f32[256,2048]{1,0:T(8,128)S(1)} fusion(f32[1024,2048]{1,0:T(8,128)} %all-gather.3.cloned.1.call-done, f32[1024,128]{1,0:T(8,128)S(1)} %get-tuple-element.21, f32[1024,128]{1,0:T(8,128)S(1)} %get-tuple-element.20), kind=kOutput, calls=%fused_computation.3 | convolution fusion | flops 3221487616 | bytes 11534336 | tf_op jit(solution)/shard_map/dot_general | solution.py:259
  76.5 0.1 fusion.8
  76.6 1.1 fusion.1
  77.8 6.7 %all-to-all-start = ((f32[16,8,2176]{2,1,0:T(8,128)}), f32[16,8,2176]{2,1,0:T(8,128)S(1)}, u32[]{:S(2)}, u32[]{:S(2)}) async-start(f32[16,8,2176]{2,1,0:T(8,128)} %fusion.1), calls=%async_computation | async-start | bytes 2228224 | tf_op jit(solution)/shard_map/all_to_all | solution.py:265
  84.4 0.0 all-gather.5.cloned.1.call-start
  84.5 6.4 %mask_rest.1 = f32[8,128,768]{2,1,0:T(8,128)} custom-call(s32[1,64]{1,0:T(1,128)} %keep_ref.3, f32[128,8192]{1,0:T(8,128)} %slab_ref.3), custom_call_target="tpu_custom_call" | custom-call | flops 1048576 | bytes 8388608 | tf_op jit(solution)/shard_map/mask_rest/pallas_call | solution.py:232
  90.9 8.6 %all-to-all-done = f32[16,8,2176]{2,1,0:T(8,128)S(1)} async-done(((f32[16,8,2176]{2,1,0:T(8,128)}), f32[16,8,2176]{2,1,0:T(8,128)S(1)}, u32[]{:S(2)}, u32[]{:S(2)}) %all-to-all-start) | async-done | bytes 1114144 | tf_op jit(solution)/shard_map/all_to_all | solution.py:265
  99.5 0.1 reduce_sum.9
  99.6 0.6 broadcast_multiply_fusion
  100.2 0.0 all-gather.5.cloned.1.call-update
  100.2 0.0 reduce-scatter.2.cloned.1.call-start
  100.3 47.3 %all_to_all.14 = f32[8,128,768]{2,1,0:T(8,128)S(1)} all-to-all(f32[8,128,768]{2,1,0:T(8,128)} %mask_rest.1), channel_id=1, replica_groups=mesh['row'=8,'col'=16] {'row'}, dimensions={0} | all-to-all | bytes 6291456 | tf_op jit(solution)/shard_map/all_to_all | solution.py:270
  147.6 15.7 %fusion.9 = f32[2048,768]{1,0:T(8,128)} fusion(f32[1024,2048]{1,0:T(8,128)} %all-gather.3.cloned.1.call-done, f32[1024,768]{1,0:T(8,128)S(1)} %bitcast.8), kind=kOutput, calls=%fused_computation.19 | convolution fusion | flops 9663676416 | bytes 17825792 | tf_op jit(solution)/shard_map/dot_general | solution.py:272
  163.3 11.2 %all-gather.5.cloned.1.call-done.packed_ref = f32[1024,2176]{1,0:T(8,128)} async-done(((f32[8,2176]{1,0:T(8,128)}), f32[1024,2176]{1,0:T(8,128)}) %all-gather.5.cloned.1.call-update) | async-done | bytes 8912912 | tf_op jit(solution)/shard_map/all_gather | solution.py:268
  174.5 0.0 reduce-scatter.2.cloned.1.call-update
  174.6 0.7 pad_add_fusion.place_ref
  175.2 132.5 %factor.1 = (f32[256,128]{1,0:T(8,128)}, f32[256,128]{1,0:T(8,128)}) custom-call(s32[2]{0:T(128)} %pad_add_fusion.place_ref, f32[1024,2176]{1,0:T(8,128)} %all-gather.5.cloned.1.call-done.packed_ref), custom_call_target="tpu_custom_call" | custom-call | flops 17179869184 | bytes 314572800 | tf_op jit(solution)/shard_map/factor/pallas_call | solution.py:185
  307.8 0.0 reduce-scatter.2.cloned.1.call-done
  307.8 1.1 constant_dynamic-slice_fusion.1
  308.9 5.5 %collective-permute-start = (f32[128,384]{1,0:T(8,128)S(1)}, f32[128,384]{1,0:T(8,128)S(1)}, u32[]{:S(2)}, u32[]{:S(2)}) collective-permute-start(f32[128,384]{1,0:T(8,128)S(1)} %get-tuple-element.24), channel_id=1, source_target_pairs={{0,0},{1,1},{2,16},{3,17},{4,32},{5,33},{6,48},{7,49},{8,64},{9,65... | collective-permute-start | bytes 589832 | tf_op jit(solution)/shard_map/ppermute | solution.py:285
  314.4 4.4 %collective-permute-start.1 = (f32[128,384]{1,0:T(8,128)S(1)}, f32[128,384]{1,0:T(8,128)S(1)}, u32[]{:S(2)}, u32[]{:S(2)}) collective-permute-start(f32[128,384]{1,0:T(8,128)S(1)} %get-tuple-element.25), channel_id=1, source_target_pairs={{0,1},{1,0},{2,17},{3,16},{4,33},{5,32},{6,49},{7,48},{8,65},{9,64... | collective-permute-start | bytes 589832 | tf_op jit(solution)/shard_map/ppermute | solution.py:286
  318.8 9.8 %collective-permute-done = f32[128,384]{1,0:T(8,128)S(1)} collective-permute-done((f32[128,384]{1,0:T(8,128)S(1)}, f32[128,384]{1,0:T(8,128)S(1)}, u32[]{:S(2)}, u32[]{:S(2)}) %collective-permute-start) | collective-permute-done | bytes 196640 | tf_op jit(solution)/shard_map/ppermute | solution.py:285
  328.6 3.7 %collective-permute-done.1 = f32[128,384]{1,0:T(8,128)S(1)} collective-permute-done((f32[128,384]{1,0:T(8,128)S(1)}, f32[128,384]{1,0:T(8,128)S(1)}, u32[]{:S(2)}, u32[]{:S(2)}) %collective-permute-start.1) | collective-permute-done | bytes 196640 | tf_op jit(solution)/shard_map/ppermute | solution.py:286
  332.3 1.8 pad_maximum_fusion
  (2 shorter events, 0.0 us)
Async XLA Ops:
  7.2 61.8 %all-gather.3.cloned.1.call-start = ((), (), s32[]{:S(2)}) async-start(), calls=%async_computation.3 | async-start | bytes 9437184 | tf_op jit(solution)/shard_map/all_gather | solution.py:255
  77.8 21.8 %all-to-all-start = ((f32[16,8,2176]{2,1,0:T(8,128)}), f32[16,8,2176]{2,1,0:T(8,128)S(1)}, u32[]{:S(2)}, u32[]{:S(2)}) async-start(f32[16,8,2176]{2,1,0:T(8,128)} %fusion.1), calls=%async_computation | async-start | bytes 2228224 | tf_op jit(solution)/shard_map/all_to_all | solution.py:265
  84.4 90.1 %all-gather.5.cloned.1.call-start = ((), (), s32[]{:S(2)}) async-start(), calls=%async_computation.4 | async-start | bytes 8982528 | tf_op jit(solution)/shard_map/all_gather | solution.py:268
  100.2 207.6 %reduce-scatter.2.cloned.1.call-start = ((), (), s32[]{:S(2)}) async-start(), calls=%async_computation.5 | async-start | bytes 6684672 | tf_op jit(solution)/shard_map/reduce_scatter | solution.py:274
  308.9 19.7 %collective-permute-start = (f32[128,384]{1,0:T(8,128)S(1)}, f32[128,384]{1,0:T(8,128)S(1)}, u32[]{:S(2)}, u32[]{:S(2)}) collective-permute-start(f32[128,384]{1,0:T(8,128)S(1)} %get-tuple-element.24), channel_id=1, source_target_pairs={{0,0},{1,1},{2,16},{3,17},{4,32},{5,33},{6,48},{7,49},{8,64},{9,65... | collective-permute-start | bytes 589832 | tf_op jit(solution)/shard_map/ppermute | solution.py:285
  314.4 17.9 %collective-permute-start.1 = (f32[128,384]{1,0:T(8,128)S(1)}, f32[128,384]{1,0:T(8,128)S(1)}, u32[]{:S(2)}, u32[]{:S(2)}) collective-permute-start(f32[128,384]{1,0:T(8,128)S(1)} %get-tuple-element.25), channel_id=1, source_target_pairs={{0,1},{1,0},{2,17},{3,16},{4,33},{5,32},{6,49},{7,48},{8,65},{9,64... | collective-permute-start | bytes 589832 | tf_op jit(solution)/shard_map/ppermute | solution.py:286
Sparse Core Ops, SparseCore 0:
  16.4 52.5 all-gather.2
  100.4 74.1 all-gather.4
  178.0 78.1 reduce-scatter.1

commit v4 on v3

--- a/solution.py
+++ b/solution.py
@@ -11,7 +11,7 @@
 SHIFT_NUM = 2
 
 
-def diag128(F):
+def diag128(F, beside=lambda t: None):
     S = (8, 128)
     lane = lax.broadcasted_iota(jnp.int32, S, 1)
     subl = lax.broadcasted_iota(jnp.int32, S, 0)
@@ -19,12 +19,20 @@
     Ws = []
     onehot = [jnp.where(subl == k, 1.0, 0.0) for k in range(8)]
     n = len(F)
+    spread = lambda x, at: [jnp.broadcast_to(x[:, at + k:at + k + 1], S) for k in range(8)]
+    D = spread(F[0], 0)
     for t in range(n):
         b = 8 * t
-        C = {s: [jnp.broadcast_to(F[s][:, b + k:b + k + 1], S) for k in range(8)] for s in range(t, n)}
         inblk = (lane >= b) & (lane < b + 8)
         X = jnp.where(inblk, jnp.where(lane - b == subl, 1.0, 0.0), F[t])
-        D = C[t]
+        if t + 1 < n:
+            first = spread(F[t + 1], b)
+            B = list(first)
+            N = spread(F[t + 1], b + 8)
+        C = {}
+        for k in range(8):
+            for s in range(t + 2, n):
+                C[s, k] = jnp.broadcast_to(F[s][:, b + k:b + k + 1], S)
         G = jnp.zeros(S, jnp.float32)
         for k in range(8):
             d = jnp.broadcast_to(D[k][k:k + 1], S)
@@ -35,16 +43,25 @@
             G = jnp.where(subl == k, xk * rs, G)
             X = X - g * (xk * inv)
             for m in range(k + 1, 8):
-                r = jnp.broadcast_to(D[m][k:k + 1], S)
-                D[m] = D[m] - g * (r * inv)
+                f = jnp.broadcast_to(D[m][k:k + 1], S) * inv
+                D[m] = D[m] - g * f
+                if t + 1 < n:
+                    B[m] = B[m] - B[k] * f
+            if t + 1 < n:
+                y = B[k] * inv
+                N = [N[m] - B[k] * jnp.broadcast_to(y[m:m + 1], S) for m in range(8)]
         Ws.append(jnp.where(lane < b + 8, G, 0.0))
-        V = [jnp.broadcast_to(X[k:k + 1], S) for k in range(8)]
-        for s in range(t + 1, n):
-            f = jnp.where(inblk, 0.0, F[s])
-            for k in range(8):
-                f = f - C[s][k] * V[k]
-            F[s] = f
+        if t + 1 < n:
+            V = [jnp.broadcast_to(X[k:k + 1], S) for k in range(8)]
+            for s in range(t + 1, n):
+                f = jnp.where(inblk, 0.0, F[s])
+                for k in range(8):
+                    f = f - (first[k] if s == t + 1 else C[s, k]) * V[k]
+                F[s] = f
+            D = N
+        beside(t)
     return Ws
+
 
 def split(x, n):
     parts = []
@@ -68,9 +85,10 @@
 
 def chol_kernel(nparts, place_ref, packed_ref, band_ref, out_ref, a_ref, *scratch):
     Ls = scratch[:nparts]
-    P, W, sems = scratch[nparts:]
+    P, Q, W, sems = scratch[nparts:]
     n = a_ref.shape[0]
     nb = n // BLK
+    np2 = n // 256
     r = place_ref[0]
     c = place_ref[1]
 
@@ -89,11 +107,13 @@
         copy.start()
 
     def zero(i, _):
+        at = pl.ds(pl.multiple_of(i * 256, 256), 256)
         for L in Ls:
-            L[pl.ds(i * 128, 128), :] = jnp.zeros((128, n), L.dtype)
+            L[at, :] = jnp.zeros((256, n), L.dtype)
+        Q[at, :] = jnp.zeros((256, 256), jnp.float32)
         return 0
 
-    lax.fori_loop(0, nb, zero, 0)
+    lax.fori_loop(0, np2, zero, 0)
     out_ref[...] = jnp.zeros(out_ref.shape, jnp.float32)
     for copy in copies:
         copy.wait()
@@ -122,39 +142,52 @@
         here = pl.multiple_of(jj * 128, 128)
         first = base // BT
 
-        @pl.when(h == 0)
+        @pl.when(jj == 0)
         def _():
             def rows(i, _):
                 at = pl.ds(pl.multiple_of(i * BT, BT), BT)
-                P[at, :] = a_ref[at, pl.ds(base, 256)]
-
-                def depth(q, _):
-                    ks = pl.ds(pl.multiple_of(q * 512, 512), 512)
-                    P[at, :] -= dot_nt([L[at, ks] for L in Ls], [L[pl.ds(base, 256), ks] for L in Ls])
-                    return 0
-
-                lax.fori_loop(0, (base + 511) // 512, depth, 0)
+                P[at, :] = a_ref[at, :256]
                 return 0
-
+            lax.fori_loop(0, n // BT, rows, 0)
+
+        @pl.when((h == 0) & (jj > 0))
+        def _():
+            ks = pl.ds(pl.multiple_of(base - 256, 256), 256)
+            def rows(i, _):
+                at = pl.ds(pl.multiple_of(i * BT, BT), BT)
+                P[at, :] = a_ref[at, pl.ds(base, 256)] + Q[at, :] - dot_nt([L[at, ks] for L in Ls], [L[pl.ds(base, 256), ks] for L in Ls])
+                Q[at, :] = jnp.zeros((BT, 256), jnp.float32)
+                return 0
             lax.fori_loop(first, n // BT, rows, 0)
 
         @pl.when(h == 1)
         def _():
             prev = pl.ds(pl.multiple_of(here - 128, 128), 128)
-
             def rows(i, _):
                 at = pl.ds(pl.multiple_of(i * BT, BT), BT)
                 P[at, :128] = P[at, 128:] - dot_nt([L[at, prev] for L in Ls], [L[pl.ds(here, 128), prev] for L in Ls])
                 return 0
-
             lax.fori_loop(first, n // BT, rows, 0)
 
+        units = (np2 // 2 * (np2 // 2 - 1) + 1) // 2
+        later = jnp.minimum(J2 + 1, np2 - 1)
+        deep = jnp.maximum(J2, 1)
+        def unit(u):
+            at = units * h + u
+            real = at < J2 * (np2 - 1 - J2)
+            i = J2 + 1 + at // deep
+            src = pl.multiple_of(jnp.where(real, i, 0) * 256, 256)
+            dst = pl.multiple_of(jnp.where(real, i, np2) * 256, 256)
+            ks = pl.ds(pl.multiple_of(jnp.where(real, at % deep, 0) * 256, 256), 256)
+            Q[pl.ds(dst, 256), :] -= dot_nt([L[pl.ds(src, 256), ks] for L in Ls], [L[pl.ds(pl.multiple_of(later * 256, 256), 256), ks] for L in Ls])
+        def beside(t):
+            if t % 2 == 0 and t // 2 < units:
+                unit(t // 2)
         P[pl.ds(here, BLK), :BLK] += shift
-        ws = diag128([P[pl.ds(pl.multiple_of(here + 8 * s, 8), 8), :128] for s in range(16)])
+        ws = diag128([P[pl.ds(pl.multiple_of(here + 8 * s, 8), 8), :128] for s in range(16)], beside)
         for s in range(16):
             W[8 * s:8 * s + 8, :] = ws[s]
         w = split(W[...], 3)
-
         def rows(i, _):
             at = pl.ds(pl.multiple_of(i * BT, BT), BT)
             l = dot_nt(split(P[at, :128], 3), w)
@@ -162,7 +195,6 @@
                 L[at, pl.ds(here, 128)] = part
             P[at, :128] = l
             return 0
-
         lax.fori_loop(first, n // BT, rows, 0)
 
         @pl.when(jj == c)
@@ -172,10 +204,8 @@
             row = lax.broadcasted_iota(jnp.int32, mine.shape, 0) + r * rows
             col = lax.broadcasted_iota(jnp.int32, mine.shape, 1) + here
             out_ref[...] = jnp.where(row >= col, mine, 0.0)
-
         return 0
-
-    lax.fori_loop(0, nb, column, 0)
+    lax.fori_loop(0, n // 128, column, 0)
 
 
 def chol_piece(packed, place, n, rows, nparts=3):
@@ -189,26 +219,36 @@
         out_specs=(vmem, vmem),
         scratch_shapes=[pltpu.VMEM((n, n), jnp.float32)]
         + [pltpu.VMEM((n, n), jnp.bfloat16)] * nparts
-        + [pltpu.VMEM((n, 256), jnp.float32), pltpu.VMEM((BLK, BLK), jnp.float32), pltpu.SemaphoreType.DMA((nb,))],
+        + [pltpu.VMEM((n, 256), jnp.float32), pltpu.VMEM((n + 256, 256), jnp.float32), pltpu.VMEM((BLK, BLK), jnp.float32), pltpu.SemaphoreType.DMA((nb,))],
         compiler_params=pltpu.CompilerParams(vmem_limit_bytes=56 * 2**20),
         cost_estimate=pl.CostEstimate(flops=2 * n * n * n, bytes_accessed=300 * 2**20, transcendentals=n),
         name="factor",
     )(place, packed)
 
 
-def band_kernel(keep_ref, slab_ref, band_ref):
-    band_ref[...] = slab_ref[...] * keep_ref[0, pl.program_id(0) * keep_ref.shape[1] // pl.num_programs(0)].astype(jnp.float32)
+def band_kernel(keep_ref, slab_ref, band_ref, got, sems):
+    ncols = band_ref.shape[1] // BLK
+    step = slab_ref.shape[1] // ncols
+    copies = [
+        pltpu.make_async_copy(slab_ref.at[:, pl.ds(c * step, BLK)], got.at[:, pl.ds(c * BLK, BLK)], sems.at[c])
+        for c in range(ncols)
+    ]
+    for copy in copies:
+        copy.start()
+    for c, copy in enumerate(copies):
+        copy.wait()
+        at = slice(c * BLK, (c + 1) * BLK)
+        band_ref[:, at] = got[:, at] * keep_ref[0, c * step // BLK].astype(jnp.float32)
 
 
 def band_columns(slab, block_mask, ncols):
-    users, items = slab.shape
-    step = items // ncols // BLK
+    users = slab.shape[0]
     return pl.pallas_call(
         band_kernel,
-        grid=(ncols,),
         out_shape=jax.ShapeDtypeStruct((users, BLK * ncols), jnp.float32),
-        in_specs=[pl.BlockSpec(memory_space=pltpu.SMEM), pl.BlockSpec((users, BLK), lambda c: (0, c * step))],
-        out_specs=pl.BlockSpec((users, BLK), lambda c: (0, c)),
+        in_specs=[pl.BlockSpec(memory_space=pltpu.SMEM), pl.BlockSpec(memory_space=pl.ANY)],
+        out_specs=pl.BlockSpec(memory_space=pltpu.VMEM),
+        scratch_shapes=[pltpu.VMEM((users, BLK * ncols), jnp.float32), pltpu.SemaphoreType.DMA((ncols,))],
         name="mask_band",
     )(block_mask, slab)
 

time: 343 us -> 298 us (0.87)
  Pallas kernels: 148 us -> 104 us
    pallas_call x1, Pallas kernels: 133 us -> 94.2 us  [chol_piece(): pl.pallas_call(functools.partial(chol_kernel, nparts), out_shape=(flat, f...]
    pallas_call x1, Pallas kernels: 9.01 us -> 3.04 us  [band_columns(): pl.pallas_call(band_kernel, out_shape=jax.ShapeDtypeStruct((users, BLK *...]
  transfers between devices with their start and end apart: 6 -> 6, of which waited for: 5 -> 5; matrix products, arithmetic and copies ran while one was open for 5% -> 6% of each run, Pallas kernels for 41% -> 34%
where the time goes in v4:
time: 298 us; the launch traced here: 296 us
  Pallas kernels  104 us (35%)
  waiting for transfers between devices  86 us (29%)
  blocking collectives  47.3 us (16%)
  matrix products  22 us (7%)
  starting transfers between devices  16.7 us (6%)
  between operations  13.8 us (5%)
  other arithmetic  4.28 us (1%)
    pallas_call x1, Pallas kernels, chol_piece(): pl.pallas_call(functools.partial(chol_kernel, nparts), out_shape=(flat, f...  94.2 us
    all_gather x1, waiting for transfers between devices, shards(): bands = lax.all_gather(band, 'row', axis=0, tiled=True)  52.7 us
    all_to_all x1, blocking collectives, shards(): lax.all_to_all(rest, 'row', split_axis=0, concat_axis=0, tiled=True)  47.3 us
    dot_general x1, matrix products, shards(): partial = lax.dot_general(bands, others, over_users, **high)  15.7 us
    all_gather x1, waiting for transfers between devices, shards(): panel = lax.all_gather(mine, ('row', 'col'), axis=0, tiled=True)  11.2 us
    ppermute x1, waiting for transfers between devices, shards(): lax.ppermute(own, ('row', 'col'), [(to(i, j), to(j // 2, 2 * i + j % 2))...  9.88 us
    all_to_all x1, waiting for transfers between devices, shards(): lax.all_to_all(packed, 'col', split_axis=0, concat_axis=0, tiled=True)  8.61 us
    all_to_all x1, starting transfers between devices, shards(): lax.all_to_all(packed, 'col', split_axis=0, concat_axis=0, tiled=True)  6.68 us
  transfers between devices with their start and end apart: 6, of which 5 were waited for; matrix products, arithmetic and copies ran while one was open for 6% of the time, Pallas kernels for 34%

profile of v4, /device:TPU:17, one launch (start us, length us, event | category | flops | bytes accessed | tf_op | source)
XLA Modules:
  0.0 296.2 jit_solution(8147969051849820108)
XLA Ops:
  7.2 0.0 all-gather.3.cloned.1.call-start
  7.2 3.0 %mask_band.1 = f32[128,2048]{1,0:T(8,128)} custom-call(s32[1,64]{1,0:T(1,128)} %keep_ref.3, f32[128,8192]{1,0:T(8,128)} %slab_ref.3), custom_call_target="tpu_custom_call" | custom-call | tf_op jit(solution)/shard_map/mask_band/pallas_call | solution.py:246
  10.3 0.0 all-gather.3.cloned.1.call-update
  10.3 52.7 %all-gather.3.cloned.1.call-done = f32[1024,2048]{1,0:T(8,128)} async-done(((f32[128,2048]{1,0:T(8,128)}), f32[1024,2048]{1,0:T(8,128)}) %all-gather.3.cloned.1.call-update) | async-done | bytes 8388624 | tf_op jit(solution)/shard_map/all_gather | solution.py:295
  63.0 1.3 constant_dynamic-slice_fusion.3
  64.3 6.2 %fusion.2 = f32[256,2048]{1,0:T(8,128)S(1)} fusion(f32[1024,2048]{1,0:T(8,128)} %all-gather.3.cloned.1.call-done, f32[1024,128]{1,0:T(8,128)S(1)} %get-tuple-element.21, f32[1024,128]{1,0:T(8,128)S(1)} %get-tuple-element.20), kind=kOutput, calls=%fused_computation.3 | convolution fusion | flops 3221487616 | bytes 11534336 | tf_op jit(solution)/shard_map/dot_general | solution.py:299
  70.5 0.1 fusion.8
  70.7 1.1 fusion.1
  71.8 6.7 %all-to-all-start = ((f32[16,8,2176]{2,1,0:T(8,128)}), f32[16,8,2176]{2,1,0:T(8,128)S(1)}, u32[]{:S(2)}, u32[]{:S(2)}) async-start(f32[16,8,2176]{2,1,0:T(8,128)} %fusion.1), calls=%async_computation | async-start | bytes 2228224 | tf_op jit(solution)/shard_map/all_to_all | solution.py:305
  78.5 0.0 all-gather.5.cloned.1.call-start
  78.5 6.4 %mask_rest.1 = f32[8,128,768]{2,1,0:T(8,128)} custom-call(s32[1,64]{1,0:T(1,128)} %keep_ref.3, f32[128,8192]{1,0:T(8,128)} %slab_ref.3), custom_call_target="tpu_custom_call" | custom-call | flops 1048576 | bytes 8388608 | tf_op jit(solution)/shard_map/mask_rest/pallas_call | solution.py:272
  85.0 8.6 %all-to-all-done = f32[16,8,2176]{2,1,0:T(8,128)S(1)} async-done(((f32[16,8,2176]{2,1,0:T(8,128)}), f32[16,8,2176]{2,1,0:T(8,128)S(1)}, u32[]{:S(2)}, u32[]{:S(2)}) %all-to-all-start) | async-done | bytes 1114144 | tf_op jit(solution)/shard_map/all_to_all | solution.py:305
  93.6 0.1 reduce_sum.9
  93.6 0.6 broadcast_multiply_fusion
  94.3 0.0 all-gather.5.cloned.1.call-update
  94.3 0.0 reduce-scatter.2.cloned.1.call-start
  94.3 47.3 %all_to_all.14 = f32[8,128,768]{2,1,0:T(8,128)S(1)} all-to-all(f32[8,128,768]{2,1,0:T(8,128)} %mask_rest.1), channel_id=1, replica_groups=mesh['row'=8,'col'=16] {'row'}, dimensions={0} | all-to-all | bytes 6291456 | tf_op jit(solution)/shard_map/all_to_all | solution.py:310
  141.6 15.7 %fusion.9 = f32[2048,768]{1,0:T(8,128)} fusion(f32[1024,2048]{1,0:T(8,128)} %all-gather.3.cloned.1.call-done, f32[1024,768]{1,0:T(8,128)S(1)} %bitcast.8), kind=kOutput, calls=%fused_computation.19 | convolution fusion | flops 9663676416 | bytes 17825792 | tf_op jit(solution)/shard_map/dot_general | solution.py:312
  157.4 11.2 %all-gather.5.cloned.1.call-done.packed_ref = f32[1024,2176]{1,0:T(8,128)} async-done(((f32[8,2176]{1,0:T(8,128)}), f32[1024,2176]{1,0:T(8,128)}) %all-gather.5.cloned.1.call-update) | async-done | bytes 8912912 | tf_op jit(solution)/shard_map/all_gather | solution.py:308
  168.6 0.0 reduce-scatter.2.cloned.1.call-update
  168.6 0.7 pad_add_fusion.place_ref
  169.3 94.2 %factor.1 = (f32[256,128]{1,0:T(8,128)}, f32[256,128]{1,0:T(8,128)}) custom-call(s32[2]{0:T(128)} %pad_add_fusion.place_ref, f32[1024,2176]{1,0:T(8,128)} %all-gather.5.cloned.1.call-done.packed_ref), custom_call_target="tpu_custom_call" | custom-call | flops 17179869184 | bytes 314572800 | tf_op jit(solution)/shard_map/factor/pallas_call | solution.py:215
  263.4 0.0 reduce-scatter.2.cloned.1.call-done
  263.5 1.1 constant_dynamic-slice_fusion.1
  264.5 5.3 %collective-permute-start = (f32[128,384]{1,0:T(8,128)S(1)}, f32[128,384]{1,0:T(8,128)S(1)}, u32[]{:S(2)}, u32[]{:S(2)}) collective-permute-start(f32[128,384]{1,0:T(8,128)S(1)} %get-tuple-element.24), channel_id=1, source_target_pairs={{0,0},{1,1},{2,16},{3,17},{4,32},{5,33},{6,48},{7,49},{8,64},{9,65... | collective-permute-start | bytes 589832 | tf_op jit(solution)/shard_map/ppermute | solution.py:325
  269.8 4.6 %collective-permute-start.1 = (f32[128,384]{1,0:T(8,128)S(1)}, f32[128,384]{1,0:T(8,128)S(1)}, u32[]{:S(2)}, u32[]{:S(2)}) collective-permute-start(f32[128,384]{1,0:T(8,128)S(1)} %get-tuple-element.25), channel_id=1, source_target_pairs={{0,1},{1,0},{2,17},{3,16},{4,33},{5,32},{6,49},{7,48},{8,65},{9,64... | collective-permute-start | bytes 589832 | tf_op jit(solution)/shard_map/ppermute | solution.py:326
  274.4 9.9 %collective-permute-done = f32[128,384]{1,0:T(8,128)S(1)} collective-permute-done((f32[128,384]{1,0:T(8,128)S(1)}, f32[128,384]{1,0:T(8,128)S(1)}, u32[]{:S(2)}, u32[]{:S(2)}) %collective-permute-start) | collective-permute-done | bytes 196640 | tf_op jit(solution)/shard_map/ppermute | solution.py:325
  284.3 3.6 %collective-permute-done.1 = f32[128,384]{1,0:T(8,128)S(1)} collective-permute-done((f32[128,384]{1,0:T(8,128)S(1)}, f32[128,384]{1,0:T(8,128)S(1)}, u32[]{:S(2)}, u32[]{:S(2)}) %collective-permute-start.1) | collective-permute-done | bytes 196640 | tf_op jit(solution)/shard_map/ppermute | solution.py:326
  287.9 1.8 pad_maximum_fusion
  (2 shorter events, 0.0 us)
Async XLA Ops:
  7.2 55.8 %all-gather.3.cloned.1.call-start = ((), (), s32[]{:S(2)}) async-start(), calls=%async_computation.3 | async-start | bytes 9437184 | tf_op jit(solution)/shard_map/all_gather | solution.py:295
  71.8 21.8 %all-to-all-start = ((f32[16,8,2176]{2,1,0:T(8,128)}), f32[16,8,2176]{2,1,0:T(8,128)S(1)}, u32[]{:S(2)}, u32[]{:S(2)}) async-start(f32[16,8,2176]{2,1,0:T(8,128)} %fusion.1), calls=%async_computation | async-start | bytes 2228224 | tf_op jit(solution)/shard_map/all_to_all | solution.py:305
  78.5 90.1 %all-gather.5.cloned.1.call-start = ((), (), s32[]{:S(2)}) async-start(), calls=%async_computation.4 | async-start | bytes 8982528 | tf_op jit(solution)/shard_map/all_gather | solution.py:308
  94.3 169.2 %reduce-scatter.2.cloned.1.call-start = ((), (), s32[]{:S(2)}) async-start(), calls=%async_computation.5 | async-start | bytes 6684672 | tf_op jit(solution)/shard_map/reduce_scatter | solution.py:314
  264.5 19.7 %collective-permute-start = (f32[128,384]{1,0:T(8,128)S(1)}, f32[128,384]{1,0:T(8,128)S(1)}, u32[]{:S(2)}, u32[]{:S(2)}) collective-permute-start(f32[128,384]{1,0:T(8,128)S(1)} %get-tuple-element.24), channel_id=1, source_target_pairs={{0,0},{1,1},{2,16},{3,17},{4,32},{5,33},{6,48},{7,49},{8,64},{9,65... | collective-permute-start | bytes 589832 | tf_op jit(solution)/shard_map/ppermute | solution.py:325
  269.8 18.1 %collective-permute-start.1 = (f32[128,384]{1,0:T(8,128)S(1)}, f32[128,384]{1,0:T(8,128)S(1)}, u32[]{:S(2)}, u32[]{:S(2)}) collective-permute-start(f32[128,384]{1,0:T(8,128)S(1)} %get-tuple-element.25), channel_id=1, source_target_pairs={{0,1},{1,0},{2,17},{3,16},{4,33},{5,32},{6,49},{7,48},{8,65},{9,64... | collective-permute-start | bytes 589832 | tf_op jit(solution)/shard_map/ppermute | solution.py:326
Sparse Core Ops, SparseCore 0:
  10.4 52.5 all-gather.2
  94.4 74.1 all-gather.4
  172.0 78.0 reduce-scatter.1

commit v5 on v4

--- a/solution.py
+++ b/solution.py
@@ -5,6 +5,7 @@
 from jax import lax
 from jax.experimental import pallas as pl
 from jax.experimental.pallas import tpu as pltpu
+from jax.sharding import Mesh
 from jax.sharding import PartitionSpec as P
 
 BLK = 128
@@ -92,44 +93,31 @@
     r = place_ref[0]
     c = place_ref[1]
 
-    copies = []
+    early, late = [], []
     for i in range(nb):
         src = min(i, nb - 1 - i)
         first = 0 if 2 * i >= nb else BLK * (nb - i)
-        copies.append(
-            pltpu.make_async_copy(
-                packed_ref.at[pl.ds(BLK * src, BLK), pl.ds(first, BLK * (i + 1))],
-                a_ref.at[pl.ds(BLK * i, BLK), pl.ds(0, BLK * (i + 1))],
-                sems.at[i],
-            )
-        )
-    for copy in copies:
+        for group, lo, hi in ((early, 0, min(2, i + 1)), (late, 2, i + 1)):
+            if hi > lo:
+                group.append(
+                    pltpu.make_async_copy(
+                        packed_ref.at[pl.ds(BLK * src, BLK), pl.ds(first + BLK * lo, BLK * (hi - lo))],
+                        a_ref.at[pl.ds(BLK * i, BLK), pl.ds(BLK * lo, BLK * (hi - lo))],
+                        sems.at[len(early) + len(late)],
+                    )
+                )
+    for copy in early + late:
         copy.start()
 
     def zero(i, _):
         at = pl.ds(pl.multiple_of(i * 256, 256), 256)
-        for L in Ls:
-            L[at, :] = jnp.zeros((256, n), L.dtype)
         Q[at, :] = jnp.zeros((256, 256), jnp.float32)
         return 0
 
     lax.fori_loop(0, np2, zero, 0)
     out_ref[...] = jnp.zeros(out_ref.shape, jnp.float32)
-    for copy in copies:
+    for copy in early:
         copy.wait()
-
-    for q in range(2):
-        i = 2 * r + q
-        rows_i = pl.multiple_of(i * BLK, BLK)
-        cols_c = pl.multiple_of(c * BLK, BLK)
-
-        @pl.when(c <= i)
-        def _():
-            band_ref[q * BLK:(q + 1) * BLK, :] = a_ref[pl.ds(rows_i, BLK), pl.ds(cols_c, BLK)]
-
-        @pl.when(c > i)
-        def _():
-            band_ref[q * BLK:(q + 1) * BLK, :] = a_ref[pl.ds(cols_c, BLK), pl.ds(rows_i, BLK)].T
 
     row_of = lax.broadcasted_iota(jnp.int32, (BLK, BLK), 0)
     col_of = lax.broadcasted_iota(jnp.int32, (BLK, BLK), 1)
@@ -149,6 +137,11 @@
                 P[at, :] = a_ref[at, :256]
                 return 0
             lax.fori_loop(0, n // BT, rows, 0)
+
+        @pl.when(jj == 1)
+        def _():
+            for copy in late:
+                copy.wait()
 
         @pl.when((h == 0) & (jj > 0))
         def _():
@@ -207,6 +200,19 @@
         return 0
     lax.fori_loop(0, n // 128, column, 0)
 
+    for q in range(2):
+        i = 2 * r + q
+        rows_i = pl.multiple_of(i * BLK, BLK)
+        cols_c = pl.multiple_of(c * BLK, BLK)
+
+        @pl.when(c <= i)
+        def _():
+            band_ref[q * BLK:(q + 1) * BLK, :] = a_ref[pl.ds(rows_i, BLK), pl.ds(cols_c, BLK)]
+
+        @pl.when(c > i)
+        def _():
+            band_ref[q * BLK:(q + 1) * BLK, :] = a_ref[pl.ds(cols_c, BLK), pl.ds(rows_i, BLK)].T
+
 
 def chol_piece(packed, place, n, rows, nparts=3):
     nb = n // BLK
@@ -219,7 +225,7 @@
         out_specs=(vmem, vmem),
         scratch_shapes=[pltpu.VMEM((n, n), jnp.float32)]
         + [pltpu.VMEM((n, n), jnp.bfloat16)] * nparts
-        + [pltpu.VMEM((n, 256), jnp.float32), pltpu.VMEM((n + 256, 256), jnp.float32), pltpu.VMEM((BLK, BLK), jnp.float32), pltpu.SemaphoreType.DMA((nb,))],
+        + [pltpu.VMEM((n, 256), jnp.float32), pltpu.VMEM((n + 256, 256), jnp.float32), pltpu.VMEM((BLK, BLK), jnp.float32), pltpu.SemaphoreType.DMA((2 * nb,))],
         compiler_params=pltpu.CompilerParams(vmem_limit_bytes=56 * 2**20),
         cost_estimate=pl.CostEstimate(flops=2 * n * n * n, bytes_accessed=300 * 2**20, transcendentals=n),
         name="factor",
@@ -281,59 +287,62 @@
 
 
 def shards(slab, block_mask):
-    ncols = lax.axis_size("col")
-    nrows = lax.axis_size("row")
-    r = lax.axis_index("row")
-    c = lax.axis_index("col")
-    pair = ncols // nrows
-    total_users = slab.shape[0] * ncols * nrows
+    z, k, y, x = (lax.axis_index(axis) for axis in ("z", "k", "y", "x"))
+    groups = lax.axis_size("y") * lax.axis_size("k")
+    ncols = lax.axis_size("z") * lax.axis_size("x")
+    g = lax.axis_size("k") * y + k
+    pair = ncols // groups
+    total_users = slab.shape[0] * ncols * groups
     high = dict(precision=lax.Precision.HIGH, preferred_element_type=jnp.float32)
     over_users = (((0,), (0,)), ((), ()))
 
     band = band_columns(slab, block_mask, ncols)
-    rest = other_columns(slab, block_mask, ncols, nrows)
-    bands = lax.all_gather(band, "row", axis=0, tiled=True)
-
-    upper = lax.dynamic_slice_in_dim(bands, BLK * r, BLK, 1)
-    lower = lax.dynamic_slice_in_dim(bands, BLK * (ncols - 1 - r), BLK, 1)
+    rest = other_columns(slab, block_mask, ncols, groups)
+    bands = lax.all_gather(band, ("y", "k"), axis=0, tiled=True)
+
+    upper = lax.dynamic_slice_in_dim(bands, BLK * g, BLK, 1)
+    lower = lax.dynamic_slice_in_dim(bands, BLK * (ncols - 1 - g), BLK, 1)
     both = lax.dot_general(jnp.concatenate([lower, upper], axis=1), bands, over_users, **high)
     padded = jnp.concatenate([jnp.zeros((BLK, BLK * ncols), jnp.float32), both[BLK:]], axis=1)
-    moved = lax.dynamic_slice_in_dim(padded, BLK * r, BLK * (ncols + 1), 1)
+    moved = lax.dynamic_slice_in_dim(padded, BLK * g, BLK * (ncols + 1), 1)
     long = jnp.concatenate([both[:BLK], jnp.zeros((BLK, BLK), jnp.float32)], axis=1)
     lane = lax.broadcasted_iota(jnp.int32, moved.shape, 1)
-    packed = jnp.where(lane < BLK * (ncols - r), long, moved)
-    pieces = lax.all_to_all(packed, "col", split_axis=0, concat_axis=0, tiled=True)
+    packed = jnp.where(lane < BLK * (ncols - g), long, moved)
+    pieces = lax.all_to_all(packed, ("z", "x"), split_axis=0, concat_axis=0, tiled=True)
     mine = jnp.sum(pieces.reshape(ncols, BLK // ncols, -1), axis=0) / total_users
     mine, rest = lax.optimization_barrier((mine, rest))
-    panel = lax.all_gather(mine, ("row", "col"), axis=0, tiled=True)
-
-    others = lax.all_to_all(rest, "row", split_axis=0, concat_axis=0, tiled=True)
+    panel = lax.all_gather(mine, ("y", "k", "z", "x"), axis=0, tiled=True)
+
+    others = lax.all_to_all(rest, ("y", "k"), split_axis=0, concat_axis=0, tiled=True)
     others = others.reshape(-1, others.shape[-1])
     partial = lax.dot_general(bands, others, over_users, **high)
     panel, partial = lax.optimization_barrier((panel, partial))
-    strip = lax.psum_scatter(partial, "col", scatter_dimension=0, tiled=True)
-
-    place = jnp.stack([r, c]).astype(jnp.int32)
+    strip = lax.psum_scatter(partial, ("z", "x"), scatter_dimension=0, tiled=True)
+
+    place = jnp.stack([lax.axis_size("k") * z + k, lax.axis_size("x") * y + x]).astype(jnp.int32)
     block, piece = chol_piece(panel, place, BLK * ncols, BLK * pair)
     strip, block, piece = lax.optimization_barrier((strip, block, piece))
     half = strip.shape[1] // pair
-    odd = c % 2
+    odd = x % 2
     own = lax.dynamic_slice_in_dim(strip, half * odd, half, 1)
     far = lax.dynamic_slice_in_dim(strip, half * (1 - odd), half, 1)
-    at = [(i, j) for i in range(nrows) for j in range(ncols)]
-    to = lambda i, j: i * ncols + j
-    own = lax.ppermute(own, ("row", "col"), [(to(i, j), to(j // 2, 2 * i + j % 2)) for i, j in at])
-    far = lax.ppermute(far, ("row", "col"), [(to(i, j), to(j // 2, 2 * i + 1 - j % 2)) for i, j in at])
+    nx = lax.axis_size("x")
+    at = [(i, j) for i in range(lax.axis_size("k")) for j in range(nx)]
+    to = lambda i, j: i * nx + j
+    own = lax.ppermute(own, ("k", "x"), [(to(i, j), to(j // 2, 2 * i + j % 2)) for i, j in at])
+    far = lax.ppermute(far, ("k", "x"), [(to(i, j), to(j // 2, 2 * i + 1 - j % 2)) for i, j in at])
     items = jnp.where(odd == 0, jnp.concatenate([own, far]), jnp.concatenate([far, own])) / total_users
     return (jnp.concatenate([block, items], axis=1), piece)
 
 
 def solution(mesh):
-    placed = (P(("row", "col"), None), P(("row", "col"), None))
+    rows, cols = mesh.devices.shape
+    axes = ("z", "k", "y", "x")
+    fine = Mesh(mesh.devices.reshape(rows // 2, 2, cols // 4, 4), axes)
     return jax.shard_map(
         shards,
-        mesh=mesh,
-        in_specs=placed,
-        out_specs=(P("row", "col"), P("row", "col")),
+        mesh=fine,
+        in_specs=(P(axes, None), P(axes, None)),
+        out_specs=(P(("z", "k"), ("y", "x")), P(("z", "k"), ("y", "x"))),
         check_vma=False,
     )

time: 298 us -> 284 us (0.953)
  waiting for transfers between devices: 86 us -> 79.9 us
  starting transfers between devices: 16.7 us -> 11.9 us
    ppermute x2, waiting for transfers between devices: 13.5 us -> 5.73 us  [the longest x1 3.73 us: shards(): lax.ppermute(own, ('k', 'x'), [(to(i, j), to(j // 2, 2 * i + j % 2)) for...]
    ppermute x2, starting transfers between devices: 9.86 us -> 5.11 us  [the longest x1 3.48 us: shards(): lax.ppermute(own, ('k', 'x'), [(to(i, j), to(j // 2, 2 * i + j % 2)) for...]
  transfers between devices with their start and end apart: 6 -> 6, of which waited for: 5 -> 5; matrix products, arithmetic and copies ran while one was open for 6% -> 6% of each run, Pallas kernels for 34% -> 35%
where the time goes in v5:
time: 284 us; the launch traced here: 282 us
  Pallas kernels  102 us (36%)
  waiting for transfers between devices  79.9 us (28%)
  blocking collectives  45.8 us (16%)
  matrix products  22 us (8%)
  between operations  13.9 us (5%)
  starting transfers between devices  11.9 us (4%)
  other arithmetic  4.29 us (2%)
    pallas_call x1, Pallas kernels, chol_piece(): pl.pallas_call(functools.partial(chol_kernel, nparts), out_shape=(flat, f...  92.2 us
    all_gather x1, waiting for transfers between devices, shards(): bands = lax.all_gather(band, ('y', 'k'), axis=0, tiled=True)  51.4 us
    all_to_all x1, blocking collectives, shards(): lax.all_to_all(rest, ('y', 'k'), split_axis=0, concat_axis=0, tiled=True)  45.8 us
    dot_general x1, matrix products, shards(): partial = lax.dot_general(bands, others, over_users, **high)  15.7 us
    all_gather x1, waiting for transfers between devices, shards(): panel = lax.all_gather(mine, ('y', 'k', 'z', 'x'), axis=0, tiled=True)  11.8 us
    all_to_all x1, waiting for transfers between devices, shards(): lax.all_to_all(packed, ('z', 'x'), split_axis=0, concat_axis=0, tiled=True)  10.9 us
    all_to_all x1, starting transfers between devices, shards(): lax.all_to_all(packed, ('z', 'x'), split_axis=0, concat_axis=0, tiled=True)  6.67 us
    pallas_call x1, Pallas kernels, other_columns(): pl.pallas_call(functools.partial(rest_kernel, pair), grid=(nrows,), out_s...  6.42 us
  transfers between devices with their start and end apart: 6, of which 5 were waited for; matrix products, arithmetic and copies ran while one was open for 6% of the time, Pallas kernels for 35%

profile of v5, /device:TPU:17, one launch (start us, length us, event | category | flops | bytes accessed | tf_op | source)
XLA Modules:
  0.0 281.9 jit_solution(6133120256770200655)
XLA Ops:
  7.2 0.0 all-gather.3.cloned.1.call-start
  7.2 3.0 %mask_band.1 = f32[128,2048]{1,0:T(8,128)} custom-call(s32[1,64]{1,0:T(1,128)} %keep_ref.3, f32[128,8192]{1,0:T(8,128)} %slab_ref.3), custom_call_target="tpu_custom_call" | custom-call | tf_op jit(solution)/shard_map/mask_band/pallas_call | solution.py:252
  10.3 0.0 all-gather.3.cloned.1.call-update
  10.3 51.4 %all-gather.3.cloned.1.call-done = f32[1024,2048]{1,0:T(8,128)} async-done(((f32[128,2048]{1,0:T(8,128)}), f32[1024,2048]{1,0:T(8,128)}) %all-gather.3.cloned.1.call-update) | async-done | bytes 8388624 | tf_op jit(solution)/shard_map/all_gather | solution.py:301
  61.7 1.3 constant_dynamic-slice_fusion.3
  63.0 6.2 %fusion.2 = f32[256,2048]{1,0:T(8,128)S(1)} fusion(f32[1024,2048]{1,0:T(8,128)} %all-gather.3.cloned.1.call-done, f32[1024,128]{1,0:T(8,128)S(1)} %get-tuple-element.21, f32[1024,128]{1,0:T(8,128)S(1)} %get-tuple-element.20), kind=kOutput, calls=%fused_computation.3 | convolution fusion | flops 3221487616 | bytes 11534336 | tf_op jit(solution)/shard_map/dot_general | solution.py:305
  69.2 0.1 fusion.8
  69.4 1.1 fusion.1
  70.5 6.7 %all-to-all-start = ((f32[16,8,2176]{2,1,0:T(8,128)}), f32[16,8,2176]{2,1,0:T(8,128)S(1)}, u32[]{:S(2)}, u32[]{:S(2)}) async-start(f32[16,8,2176]{2,1,0:T(8,128)} %fusion.1), calls=%async_computation | async-start | bytes 2228224 | tf_op jit(solution)/shard_map/all_to_all | solution.py:311
  77.2 0.0 all-gather.5.cloned.1.call-start
  77.2 6.4 %mask_rest.1 = f32[8,128,768]{2,1,0:T(8,128)} custom-call(s32[1,64]{1,0:T(1,128)} %keep_ref.3, f32[128,8192]{1,0:T(8,128)} %slab_ref.3), custom_call_target="tpu_custom_call" | custom-call | flops 1048576 | bytes 8388608 | tf_op jit(solution)/shard_map/mask_rest/pallas_call | solution.py:278
  83.6 10.9 %all-to-all-done = f32[16,8,2176]{2,1,0:T(8,128)S(1)} async-done(((f32[16,8,2176]{2,1,0:T(8,128)}), f32[16,8,2176]{2,1,0:T(8,128)S(1)}, u32[]{:S(2)}, u32[]{:S(2)}) %all-to-all-start) | async-done | bytes 1114144 | tf_op jit(solution)/shard_map/all_to_all | solution.py:311
  94.6 0.1 reduce_sum.9
  94.6 0.6 broadcast_multiply_fusion
  95.3 0.0 all-gather.5.cloned.1.call-update
  95.3 0.0 reduce-scatter.2.cloned.1.call-start
  95.3 45.8 %all_to_all.14 = f32[8,128,768]{2,1,0:T(8,128)S(1)} all-to-all(f32[8,128,768]{2,1,0:T(8,128)} %mask_rest.1), channel_id=1, replica_groups=mesh['z'=4,'k'=2,'y'=4,'x'=4] {'y','k'}, dimensions={0} | all-to-all | bytes 6291456 | tf_op jit(solution)/shard_map/all_to_all | solution.py:316
  141.1 15.7 %fusion.9 = f32[2048,768]{1,0:T(8,128)} fusion(f32[1024,2048]{1,0:T(8,128)} %all-gather.3.cloned.1.call-done, f32[1024,768]{1,0:T(8,128)S(1)} %bitcast.8), kind=kOutput, calls=%fused_computation.19 | convolution fusion | flops 9663676416 | bytes 17825792 | tf_op jit(solution)/shard_map/dot_general | solution.py:318
  156.9 11.8 %all-gather.5.cloned.1.call-done.packed_ref = f32[1024,2176]{1,0:T(8,128)} async-done(((f32[8,2176]{1,0:T(8,128)}), f32[1024,2176]{1,0:T(8,128)}) %all-gather.5.cloned.1.call-update) | async-done | bytes 8912912 | tf_op jit(solution)/shard_map/all_gather | solution.py:314
  168.7 0.0 reduce-scatter.2.cloned.1.call-update
  168.7 0.7 pad_add_fusion.place_ref
  169.4 92.2 %factor.1 = (f32[256,128]{1,0:T(8,128)}, f32[256,128]{1,0:T(8,128)}) custom-call(s32[2]{0:T(128)} %pad_add_fusion.place_ref, f32[1024,2176]{1,0:T(8,128)} %all-gather.5.cloned.1.call-done.packed_ref), custom_call_target="tpu_custom_call" | custom-call | flops 17179869184 | bytes 314572800 | tf_op jit(solution)/shard_map/factor/pallas_call | solution.py:221
  261.6 0.0 reduce-scatter.2.cloned.1.call-done
  261.6 1.1 constant_dynamic-slice_fusion.1
  262.7 3.5 %collective-permute-start = (f32[128,384]{1,0:T(8,128)S(1)}, f32[128,384]{1,0:T(8,128)S(1)}, u32[]{:S(2)}, u32[]{:S(2)}) collective-permute-start(f32[128,384]{1,0:T(8,128)S(1)} %get-tuple-element.24), channel_id=1, source_target_pairs={{0,0},{1,1},{2,16},{3,17},{16,2},{17,3},{18,18},{19,19},{4,4},{5,5... | collective-permute-start | bytes 589832 | tf_op jit(solution)/shard_map/ppermute | solution.py:332
  266.2 1.6 collective-permute-start.1
  267.8 3.7 %collective-permute-done = f32[128,384]{1,0:T(8,128)S(1)} collective-permute-done((f32[128,384]{1,0:T(8,128)S(1)}, f32[128,384]{1,0:T(8,128)S(1)}, u32[]{:S(2)}, u32[]{:S(2)}) %collective-permute-start) | collective-permute-done | bytes 196640 | tf_op jit(solution)/shard_map/ppermute | solution.py:332
  271.5 2.0 collective-permute-done.1
  273.6 1.8 pad_maximum_fusion
  (2 shorter events, 0.0 us)
Async XLA Ops:
  7.2 54.5 %all-gather.3.cloned.1.call-start = ((), (), s32[]{:S(2)}) async-start(), calls=%async_computation.3 | async-start | bytes 9437184 | tf_op jit(solution)/shard_map/all_gather | solution.py:301
  70.5 24.1 %all-to-all-start = ((f32[16,8,2176]{2,1,0:T(8,128)}), f32[16,8,2176]{2,1,0:T(8,128)S(1)}, u32[]{:S(2)}, u32[]{:S(2)}) async-start(f32[16,8,2176]{2,1,0:T(8,128)} %fusion.1), calls=%async_computation | async-start | bytes 2228224 | tf_op jit(solution)/shard_map/all_to_all | solution.py:311
  77.2 91.5 %all-gather.5.cloned.1.call-start = ((), (), s32[]{:S(2)}) async-start(), calls=%async_computation.4 | async-start | bytes 8982528 | tf_op jit(solution)/shard_map/all_gather | solution.py:314
  95.3 166.3 %reduce-scatter.2.cloned.1.call-start = ((), (), s32[]{:S(2)}) async-start(), calls=%async_computation.5 | async-start | bytes 6684672 | tf_op jit(solution)/shard_map/reduce_scatter | solution.py:320
  262.7 8.8 %collective-permute-start = (f32[128,384]{1,0:T(8,128)S(1)}, f32[128,384]{1,0:T(8,128)S(1)}, u32[]{:S(2)}, u32[]{:S(2)}) collective-permute-start(f32[128,384]{1,0:T(8,128)S(1)} %get-tuple-element.24), channel_id=1, source_target_pairs={{0,0},{1,1},{2,16},{3,17},{16,2},{17,3},{18,18},{19,19},{4,4},{5,5... | collective-permute-start | bytes 589832 | tf_op jit(solution)/shard_map/ppermute | solution.py:332
  266.2 7.4 %collective-permute-start.1 = (f32[128,384]{1,0:T(8,128)S(1)}, f32[128,384]{1,0:T(8,128)S(1)}, u32[]{:S(2)}, u32[]{:S(2)}) collective-permute-start(f32[128,384]{1,0:T(8,128)S(1)} %get-tuple-element.25), channel_id=1, source_target_pairs={{0,1},{1,0},{2,17},{3,16},{16,3},{17,2},{18,19},{19,18},{4,5},{5,4... | collective-permute-start | bytes 589832 | tf_op jit(solution)/shard_map/ppermute | solution.py:333
Sparse Core Ops, SparseCore 0:
  10.4 51.2 all-gather.2
  95.4 73.2 all-gather.4
  172.1 78.9 reduce-scatter.1

commit v6 on v5

--- a/solution.py
+++ b/solution.py
@@ -38,7 +38,7 @@
         for k in range(8):
             d = jnp.broadcast_to(D[k][k:k + 1], S)
             rs = lax.rsqrt(d)
-            inv = rs * rs
+            inv = 1.0 / d
             g = D[k] - onehot[k]
             xk = jnp.broadcast_to(X[k:k + 1], S)
             G = jnp.where(subl == k, xk * rs, G)
@@ -81,7 +81,27 @@
     y = jnp.concatenate([b[j] for _, j in pairs], axis=1)
     return lax.dot_general(x, y, (((1,), (1,)), ((), ())), preferred_element_type=jnp.float32)
 
-BT = 512
+def dot_nt_narrow(a, b):
+    rows = b[0].shape[0]
+    x = jnp.concatenate([a[0], a[1]], axis=1)
+    y = jnp.concatenate([jnp.concatenate([b[0], b[1]], axis=1), jnp.concatenate([b[1], b[0]], axis=1)], axis=0)
+    u = lax.dot_general(x, y, (((1,), (1,)), ((), ())), preferred_element_type=jnp.float32)
+    x = jnp.concatenate([a[0], a[2]], axis=1)
+    y = jnp.concatenate([b[2], b[0]], axis=1)
+    v = lax.dot_general(x, y, (((1,), (1,)), ((), ())), preferred_element_type=jnp.float32)
+    return u[:, :rows] + (u[:, rows:] + v)
+
+
+BT = 256
+
+
+def each_tile(first, n, body):
+    for f in range(n // BT):
+
+        @pl.when(first == f)
+        def _():
+            for i in range(f, n // BT):
+                body(i)
 
 
 def chol_kernel(nparts, place_ref, packed_ref, band_ref, out_ref, a_ref, *scratch):
@@ -132,11 +152,11 @@
 
         @pl.when(jj == 0)
         def _():
-            def rows(i, _):
-                at = pl.ds(pl.multiple_of(i * BT, BT), BT)
+            def rows(i):
+                at = pl.ds(i * BT, BT)
                 P[at, :] = a_ref[at, :256]
-                return 0
-            lax.fori_loop(0, n // BT, rows, 0)
+            for i in range(n // BT):
+                rows(i)
 
         @pl.when(jj == 1)
         def _():
@@ -146,21 +166,19 @@
         @pl.when((h == 0) & (jj > 0))
         def _():
             ks = pl.ds(pl.multiple_of(base - 256, 256), 256)
-            def rows(i, _):
-                at = pl.ds(pl.multiple_of(i * BT, BT), BT)
+            def rows(i):
+                at = pl.ds(i * BT, BT)
                 P[at, :] = a_ref[at, pl.ds(base, 256)] + Q[at, :] - dot_nt([L[at, ks] for L in Ls], [L[pl.ds(base, 256), ks] for L in Ls])
                 Q[at, :] = jnp.zeros((BT, 256), jnp.float32)
-                return 0
-            lax.fori_loop(first, n // BT, rows, 0)
+            each_tile(first, n, rows)
 
         @pl.when(h == 1)
         def _():
             prev = pl.ds(pl.multiple_of(here - 128, 128), 128)
-            def rows(i, _):
-                at = pl.ds(pl.multiple_of(i * BT, BT), BT)
-                P[at, :128] = P[at, 128:] - dot_nt([L[at, prev] for L in Ls], [L[pl.ds(here, 128), prev] for L in Ls])
-                return 0
-            lax.fori_loop(first, n // BT, rows, 0)
+            def rows(i):
+                at = pl.ds(i * BT, BT)
+                P[at, :128] = P[at, 128:] - dot_nt_narrow([L[at, prev] for L in Ls], [L[pl.ds(here, 128), prev] for L in Ls])
+            each_tile(first, n, rows)
 
         units = (np2 // 2 * (np2 // 2 - 1) + 1) // 2
         later = jnp.minimum(J2 + 1, np2 - 1)
@@ -181,14 +199,13 @@
         for s in range(16):
             W[8 * s:8 * s + 8, :] = ws[s]
         w = split(W[...], 3)
-        def rows(i, _):
-            at = pl.ds(pl.multiple_of(i * BT, BT), BT)
-            l = dot_nt(split(P[at, :128], 3), w)
+        def rows(i):
+            at = pl.ds(i * BT, BT)
+            l = dot_nt_narrow(split(P[at, :128], 3), w)
             for L, part in zip(Ls, split(l, nparts)):
                 L[at, pl.ds(here, 128)] = part
             P[at, :128] = l
-            return 0
-        lax.fori_loop(first, n // BT, rows, 0)
+        each_tile(first, n, rows)
 
         @pl.when(jj == c)
         def _():
@@ -299,6 +316,7 @@
     band = band_columns(slab, block_mask, ncols)
     rest = other_columns(slab, block_mask, ncols, groups)
     bands = lax.all_gather(band, ("y", "k"), axis=0, tiled=True)
+    bands, rest = lax.optimization_barrier((bands, rest))
 
     upper = lax.dynamic_slice_in_dim(bands, BLK * g, BLK, 1)
     lower = lax.dynamic_slice_in_dim(bands, BLK * (ncols - 1 - g), BLK, 1)
@@ -311,7 +329,7 @@
     pieces = lax.all_to_all(packed, ("z", "x"), split_axis=0, concat_axis=0, tiled=True)
     mine = jnp.sum(pieces.reshape(ncols, BLK // ncols, -1), axis=0) / total_users
     mine, rest = lax.optimization_barrier((mine, rest))
-    panel = lax.all_gather(mine, ("y", "k", "z", "x"), axis=0, tiled=True)
+    panel = lax.all_gather(lax.all_gather(mine, "x", axis=0, tiled=True), ("y", "k", "z"), axis=0, tiled=True)
 
     others = lax.all_to_all(rest, ("y", "k"), split_axis=0, concat_axis=0, tiled=True)
     others = others.reshape(-1, others.shape[-1])

time: 284 us -> 281 us (0.989)
  blocking collectives: 45.8 us -> 93.2 us
  waiting for transfers between devices: 79.9 us -> 54.5 us
  Pallas kernels: 102 us -> 83.7 us
  starting transfers between devices: 11.9 us -> 6.14 us
    all_to_all x0 -> x1, blocking collectives: none -> 23.8 us  [shards(): lax.all_to_all(packed, ('z', 'x'), split_axis=0, concat_axis=0, tiled=True)]
    pallas_call x1, Pallas kernels: 92.2 us -> 74.2 us  [chol_piece(): pl.pallas_call(functools.partial(chol_kernel, nparts), out_shape=(flat, f...]
    all_to_all x1, blocking collectives: 45.8 us -> 58.8 us  [shards(): lax.all_to_all(rest, ('y', 'k'), split_axis=0, concat_axis=0, tiled=True)]
    all_gather x1, waiting for transfers between devices: 11.8 us -> 0.01 us  [shards(): lax.all_gather(lax.all_gather(mine, 'x', axis=0, tiled=True), ('y', 'k',...]
    all_to_all x1 -> x0, waiting for transfers between devices: 10.9 us -> none  [shards(): lax.all_to_all(packed, ('z', 'x'), split_axis=0, concat_axis=0, tiled=True)]
    all_gather x0 -> x1, blocking collectives: none -> 10.5 us  [shards(): lax.all_gather(mine, 'x', axis=0, tiled=True)]
    all_to_all x1 -> x0, starting transfers between devices: 6.67 us -> none  [shards(): lax.all_to_all(packed, ('z', 'x'), split_axis=0, concat_axis=0, tiled=True)]
    all_gather x1, waiting for transfers between devices: 51.4 us -> 44.9 us  [shards(): bands = lax.all_gather(band, ('y', 'k'), axis=0, tiled=True)]
  transfers between devices with their start and end apart: 6 -> 5, of which waited for: 5 -> 4; matrix products, arithmetic and copies ran while one was open for 6% -> 6% of each run, Pallas kernels for 35% -> 29%
where the time goes in v6:
time: 281 us; the launch traced here: 280 us
  blocking collectives  93.2 us (33%)
  Pallas kernels  83.7 us (30%)
  waiting for transfers between devices  54.5 us (19%)
  matrix products  22.1 us (8%)
  between operations  13.9 us (5%)
  starting transfers between devices  6.14 us (2%)
  other arithmetic  3.86 us (1%)
    pallas_call x1, Pallas kernels, chol_piece(): pl.pallas_call(functools.partial(chol_kernel, nparts), out_shape=(flat, f...  74.2 us
    all_to_all x1, blocking collectives, shards(): lax.all_to_all(rest, ('y', 'k'), split_axis=0, concat_axis=0, tiled=True)  58.8 us
    all_gather x1, waiting for transfers between devices, shards(): bands = lax.all_gather(band, ('y', 'k'), axis=0, tiled=True)  44.9 us
    all_to_all x1, blocking collectives, shards(): lax.all_to_all(packed, ('z', 'x'), split_axis=0, concat_axis=0, tiled=True)  23.8 us
    dot_general x1, matrix products, shards(): partial = lax.dot_general(bands, others, over_users, **high)  15.9 us
    all_gather x1, blocking collectives, shards(): lax.all_gather(mine, 'x', axis=0, tiled=True)  10.5 us
    pallas_call x1, Pallas kernels, other_columns(): pl.pallas_call(functools.partial(rest_kernel, pair), grid=(nrows,), out_s...  6.41 us
    dot_general x1, matrix products, shards(): lax.dot_general(jnp.concatenate([lower, upper], axis=1), bands, over_user...  6.25 us
  transfers between devices with their start and end apart: 5, of which 4 were waited for; matrix products, arithmetic and copies ran while one was open for 6% of the time, Pallas kernels for 29%

profile of v6, /device:TPU:17, one launch (start us, length us, event | category | flops | bytes accessed | tf_op | source)
XLA Modules:
  0.0 279.8 jit_solution(17423244819062031292)
XLA Ops:
  7.2 0.0 all-gather.3.cloned.1.call-start
  7.2 3.0 %mask_band.1 = f32[128,2048]{1,0:T(8,128)} custom-call(s32[1,64]{1,0:T(1,128)} %keep_ref.3, f32[128,8192]{1,0:T(8,128)} %slab_ref.3), custom_call_target="tpu_custom_call" | custom-call | tf_op jit(solution)/shard_map/mask_band/pallas_call | solution.py:269
  10.3 0.0 all-gather.3.cloned.1.call-update
  10.3 0.0 all-gather.5.cloned.1.call-start
  10.3 6.4 %mask_rest.1 = f32[8,128,768]{2,1,0:T(8,128)} custom-call(s32[1,64]{1,0:T(1,128)} %keep_ref.3, f32[128,8192]{1,0:T(8,128)} %slab_ref.3), custom_call_target="tpu_custom_call" | custom-call | flops 1048576 | bytes 8388608 | tf_op jit(solution)/shard_map/mask_rest/pallas_call | solution.py:295
  16.8 44.9 %all-gather.3.cloned.1.call-done = f32[1024,2048]{1,0:T(8,128)} async-done(((f32[128,2048]{1,0:T(8,128)}), f32[1024,2048]{1,0:T(8,128)}) %all-gather.3.cloned.1.call-update) | async-done | bytes 8388624 | tf_op jit(solution)/shard_map/all_gather | solution.py:318
  61.7 1.3 constant_dynamic-slice_fusion.3
  63.0 6.3 %fusion.2 = f32[256,2048]{1,0:T(8,128)S(1)} fusion(f32[1024,2048]{1,0:T(8,128)} %all-gather.3.cloned.1.call-done, f32[1024,128]{1,0:T(8,128)S(1)} %get-tuple-element.25, f32[1024,128]{1,0:T(8,128)S(1)} %get-tuple-element.24), kind=kOutput, calls=%fused_computation.3 | convolution fusion | flops 3221487616 | bytes 11534336 | tf_op jit(solution)/shard_map/dot_general | solution.py:323
  69.2 0.1 fusion.8
  69.4 0.0 copy-start
  69.4 0.2 fusion.1
  69.5 23.8 %all_to_all.14 = f32[16,8,2176]{2,1,0:T(8,128)} all-to-all(f32[16,8,2176]{2,1,0:T(8,128)S(1)} %fusion.1), channel_id=1, replica_groups=mesh['z'=4,'k'=2,'y'=4,'x'=4] {'z','x'}, dimensions={0} | all-to-all | bytes 2228224 | tf_op jit(solution)/shard_map/all_to_all | solution.py:329
  93.4 1.3 reduce_sum.9
  94.7 10.5 %all_gather.10 = f32[32,2176]{1,0:T(8,128)} all-gather(f32[8,2176]{1,0:T(8,128)S(1)} %broadcast_multiply_fusion), channel_id=1, replica_groups=mesh['z'=4,'k'=2,'y'=4,'x'=4] {'x'}, dimensions={0}, use_global_device_ids=true | all-gather | bytes 348160 | tf_op jit(solution)/shard_map/all_gather | solution.py:332
  105.3 0.0 all-gather.5.cloned.1.call-update
  105.3 0.0 reduce-scatter.2.cloned.1.call-start
  105.3 0.0 copy-done
  105.3 58.8 %all_to_all.15 = f32[8,128,768]{2,1,0:T(8,128)S(1)} all-to-all(f32[8,128,768]{2,1,0:T(8,128)S(1)} %copy-done), channel_id=1, replica_groups=mesh['z'=4,'k'=2,'y'=4,'x'=4] {'y','k'}, dimensions={0} | all-to-all | bytes 6291456 | tf_op jit(solution)/shard_map/all_to_all | solution.py:334
  164.2 15.9 %fusion.9 = f32[2048,768]{1,0:T(8,128)} fusion(f32[1024,2048]{1,0:T(8,128)} %all-gather.3.cloned.1.call-done, f32[1024,768]{1,0:T(8,128)S(1)} %bitcast.8), kind=kOutput, calls=%fused_computation.19 | convolution fusion | flops 9663676416 | bytes 17825792 | tf_op jit(solution)/shard_map/dot_general | solution.py:336
  180.1 0.0 all-gather.5.cloned.1.call-done.packed_ref
  180.1 0.0 reduce-scatter.2.cloned.1.call-update
  180.1 0.6 pad_add_fusion.place_ref
  180.7 74.2 %factor.1 = (f32[256,128]{1,0:T(8,128)}, f32[256,128]{1,0:T(8,128)}) custom-call(s32[2]{0:T(128)} %pad_add_fusion.place_ref, f32[1024,2176]{1,0:T(8,128)} %all-gather.5.cloned.1.call-done.packed_ref), custom_call_target="tpu_custom_call" | custom-call | flops 17179869184 | bytes 314572800 | tf_op jit(solution)/shard_map/factor/pallas_call | solution.py:238
  254.9 3.2 %reduce-scatter.2.cloned.1.call-done = f32[128,768]{1,0:T(8,128)} async-done(((f32[2048,768]{1,0:T(8,128)}), f32[128,768]{1,0:T(8,128)}) %reduce-scatter.2.cloned.1.call-update) | async-done | bytes 393232 | tf_op jit(solution)/shard_map/reduce_scatter | solution.py:338
  258.1 1.0 constant_dynamic-slice_fusion.1
  259.2 5.9 %collective-permute-start = (f32[128,384]{1,0:T(8,128)S(1)}, f32[128,384]{1,0:T(8,128)S(1)}, u32[]{:S(2)}, u32[]{:S(2)}) collective-permute-start(f32[128,384]{1,0:T(8,128)S(1)} %get-tuple-element.28), channel_id=1, source_target_pairs={{0,0},{1,1},{2,16},{3,17},{16,2},{17,3},{18,18},{19,19},{4,4},{5,5... | collective-permute-start | bytes 589832 | tf_op jit(solution)/shard_map/ppermute | solution.py:350
  265.1 0.1 collective-permute-start.1
  265.2 3.2 %collective-permute-done = f32[128,384]{1,0:T(8,128)S(1)} collective-permute-done((f32[128,384]{1,0:T(8,128)S(1)}, f32[128,384]{1,0:T(8,128)S(1)}, u32[]{:S(2)}, u32[]{:S(2)}) %collective-permute-start) | collective-permute-done | bytes 196640 | tf_op jit(solution)/shard_map/ppermute | solution.py:350
  268.5 3.0 %collective-permute-done.1 = f32[128,384]{1,0:T(8,128)S(1)} collective-permute-done((f32[128,384]{1,0:T(8,128)S(1)}, f32[128,384]{1,0:T(8,128)S(1)}, u32[]{:S(2)}, u32[]{:S(2)}) %collective-permute-start.1) | collective-permute-done | bytes 196640 | tf_op jit(solution)/shard_map/ppermute | solution.py:351
  271.5 1.8 pad_maximum_fusion
  (3 shorter events, 0.0 us)
Async XLA Ops:
  7.2 54.5 %all-gather.3.cloned.1.call-start = ((), (), s32[]{:S(2)}) async-start(), calls=%async_computation.3 | async-start | bytes 9437184 | tf_op jit(solution)/shard_map/all_gather | solution.py:318
  10.3 169.8 %all-gather.5.cloned.1.call-start = ((), (), s32[]{:S(2)}) async-start(), calls=%async_computation.4 | async-start | bytes 9191424 | tf_op jit(solution)/shard_map/all_gather | solution.py:332
  69.4 36.0 %copy-start = (f32[8,128,768]{2,1,0:T(8,128)S(1)}, f32[8,128,768]{2,1,0:T(8,128)}, u32[]{:S(2)}) copy-start(f32[8,128,768]{2,1,0:T(8,128)} %mask_rest.1) | copy-start | bytes 9437188
  105.3 152.8 %reduce-scatter.2.cloned.1.call-start = ((), (), s32[]{:S(2)}) async-start(), calls=%async_computation.5 | async-start | bytes 6684672 | tf_op jit(solution)/shard_map/reduce_scatter | solution.py:338
  259.2 9.3 %collective-permute-start = (f32[128,384]{1,0:T(8,128)S(1)}, f32[128,384]{1,0:T(8,128)S(1)}, u32[]{:S(2)}, u32[]{:S(2)}) collective-permute-start(f32[128,384]{1,0:T(8,128)S(1)} %get-tuple-element.28), channel_id=1, source_target_pairs={{0,0},{1,1},{2,16},{3,17},{16,2},{17,3},{18,18},{19,19},{4,4},{5,5... | collective-permute-start | bytes 589832 | tf_op jit(solution)/shard_map/ppermute | solution.py:350
  265.1 6.4 %collective-permute-start.1 = (f32[128,384]{1,0:T(8,128)S(1)}, f32[128,384]{1,0:T(8,128)S(1)}, u32[]{:S(2)}, u32[]{:S(2)}) collective-permute-start(f32[128,384]{1,0:T(8,128)S(1)} %get-tuple-element.29), channel_id=1, source_target_pairs={{0,1},{1,0},{2,17},{3,16},{16,3},{17,2},{18,19},{19,18},{4,5},{5,4... | collective-permute-start | bytes 589832 | tf_op jit(solution)/shard_map/ppermute | solution.py:351
Sparse Core Ops, SparseCore 0:
  10.4 51.2 all-gather.2
  105.4 68.9 all-gather.4
  180.2 77.8 reduce-scatter.1

commit v7 on v6

--- a/solution.py
+++ b/solution.py
@@ -329,17 +329,17 @@
     pieces = lax.all_to_all(packed, ("z", "x"), split_axis=0, concat_axis=0, tiled=True)
     mine = jnp.sum(pieces.reshape(ncols, BLK // ncols, -1), axis=0) / total_users
     mine, rest = lax.optimization_barrier((mine, rest))
-    panel = lax.all_gather(lax.all_gather(mine, "x", axis=0, tiled=True), ("y", "k", "z"), axis=0, tiled=True)
+    panel = lax.all_gather(mine, ("y", "k", "z", "x"), axis=0, tiled=True)
 
     others = lax.all_to_all(rest, ("y", "k"), split_axis=0, concat_axis=0, tiled=True)
     others = others.reshape(-1, others.shape[-1])
     partial = lax.dot_general(bands, others, over_users, **high)
-    panel, partial = lax.optimization_barrier((panel, partial))
-    strip = lax.psum_scatter(partial, ("z", "x"), scatter_dimension=0, tiled=True)
+    parts = lax.all_to_all(partial, ("z", "x"), split_axis=0, concat_axis=0, tiled=True)
 
     place = jnp.stack([lax.axis_size("k") * z + k, lax.axis_size("x") * y + x]).astype(jnp.int32)
     block, piece = chol_piece(panel, place, BLK * ncols, BLK * pair)
-    strip, block, piece = lax.optimization_barrier((strip, block, piece))
+    parts, block, piece = lax.optimization_barrier((parts, block, piece))
+    strip = jnp.sum(parts.reshape(ncols, -1, parts.shape[1]), axis=0) / total_users
     half = strip.shape[1] // pair
     odd = x % 2
     own = lax.dynamic_slice_in_dim(strip, half * odd, half, 1)
@@ -349,7 +349,7 @@
     to = lambda i, j: i * nx + j
     own = lax.ppermute(own, ("k", "x"), [(to(i, j), to(j // 2, 2 * i + j % 2)) for i, j in at])
     far = lax.ppermute(far, ("k", "x"), [(to(i, j), to(j // 2, 2 * i + 1 - j % 2)) for i, j in at])
-    items = jnp.where(odd == 0, jnp.concatenate([own, far]), jnp.concatenate([far, own])) / total_users
+    items = jnp.where(odd == 0, jnp.concatenate([own, far]), jnp.concatenate([far, own]))
     return (jnp.concatenate([block, items], axis=1), piece)
 
 

time: 281 us -> 290 us (1.032)
  blocking collectives: 93.2 us -> 23.6 us
  waiting for transfers between devices: 54.5 us -> 115 us
  starting transfers between devices: 6.14 us -> 16.2 us
  local copies, waits for them, and re-layouts: 2.47 us -> 10.8 us
    all_to_all x1 -> x0, blocking collectives: 58.8 us -> none  [shards(): lax.all_to_all(rest, ('y', 'k'), split_axis=0, concat_axis=0, tiled=True)]
    all_gather x1, waiting for transfers between devices: 0.01 us -> 34.5 us  [shards(): panel = lax.all_gather(mine, ('y', 'k', 'z', 'x'), axis=0, tiled=True)]
    all_to_all x0 -> x2, waiting for transfers between devices: none -> 29.5 us  [the longest x1 29.4 us: shards(): lax.all_to_all(rest, ('y', 'k'), split_axis=0, concat_axis=0, tiled=True)]
    all_to_all x0 -> x2, starting transfers between devices: none -> 11.2 us  [the longest x1 6.53 us: shards(): lax.all_to_all(rest, ('y', 'k'), split_axis=0, concat_axis=0, tiled=True)]
    all_gather x1 -> x0, blocking collectives: 10.5 us -> none  [shards(): lax.all_gather(mine, 'x', axis=0, tiled=True)]
    dot_general x0 -> x1, local copies, waits for them, and re-layouts: none -> 9.35 us  [shards(): partial = lax.dot_general(bands, others, over_users, **high)]
    reduce_scatter x1 -> x0, waiting for transfers between devices: 3.21 us -> none  [shards(): lax.psum_scatter(partial, ('z', 'x'), scatter_dimension=0, tiled=True)]
    reduce_sum x0 -> x1, other arithmetic: none -> 3.2 us  [shards(): jnp.sum(parts.reshape(ncols, -1, parts.shape[1]), axis=0) / total_users]
  transfers between devices with their start and end apart: 5 -> 6, of which waited for: 4 -> 5; matrix products, arithmetic and copies ran while one was open for 6% -> 8% of each run, Pallas kernels for 29% -> 28%
where the time goes in v7:
time: 290 us
  waiting for transfers between devices  115 us (40%)
  Pallas kernels  83.7 us (29%)
  blocking collectives  23.6 us (8%)
  matrix products  20.6 us (7%)
  starting transfers between devices  16.2 us (6%)
  between operations  14.2 us (5%)
  local copies, waits for them, and re-layouts  10.8 us (4%)
  other arithmetic  5.65 us (2%)
    pallas_call x1, Pallas kernels, chol_piece(): pl.pallas_call(functools.partial(chol_kernel, nparts), out_shape=(flat, f...  74.2 us
    all_gather x1, waiting for transfers between devices, shards(): bands = lax.all_gather(band, ('y', 'k'), axis=0, tiled=True)  44.9 us
    all_gather x1, waiting for transfers between devices, shards(): panel = lax.all_gather(mine, ('y', 'k', 'z', 'x'), axis=0, tiled=True)  34.5 us
    all_to_all x1, waiting for transfers between devices, shards(): lax.all_to_all(rest, ('y', 'k'), split_axis=0, concat_axis=0, tiled=True)  29.4 us
    all_to_all x1, blocking collectives, shards(): lax.all_to_all(packed, ('z', 'x'), split_axis=0, concat_axis=0, tiled=True)  23.6 us
    dot_general x1, matrix products, shards(): partial = lax.dot_general(bands, others, over_users, **high)  14.3 us
    dot_general x1, local copies, waits for them, and re-layouts, shards(): partial = lax.dot_general(bands, others, over_users, **high)  9.35 us
    all_to_all x1, starting transfers between devices, shards(): lax.all_to_all(rest, ('y', 'k'), split_axis=0, concat_axis=0, tiled=True)  6.53 us
  transfers between devices with their start and end apart: 6, of which 5 were waited for; matrix products, arithmetic and copies ran while one was open for 8% of the time, Pallas kernels for 28%

profile of v7, /device:TPU:17, one launch (start us, length us, event | category | flops | bytes accessed | tf_op | source)
XLA Modules:
  0.0 289.6 jit_solution(14000953918151918372)
XLA Ops:
  7.2 0.0 all-gather.3.cloned.1.call-start
  7.2 3.1 %mask_band.1 = f32[128,2048]{1,0:T(8,128)} custom-call(s32[1,64]{1,0:T(1,128)} %keep_ref.3, f32[128,8192]{1,0:T(8,128)} %slab_ref.3), custom_call_target="tpu_custom_call" | custom-call | tf_op jit(solution)/shard_map/mask_band/pallas_call | solution.py:269
  10.3 0.0 all-gather.3.cloned.1.call-update
  10.3 0.0 all-gather.5.cloned.1.call-start
  10.4 6.4 %mask_rest.1 = f32[8,128,768]{2,1,0:T(8,128)} custom-call(s32[1,64]{1,0:T(1,128)} %keep_ref.3, f32[128,8192]{1,0:T(8,128)} %slab_ref.3), custom_call_target="tpu_custom_call" | custom-call | flops 1048576 | bytes 8388608 | tf_op jit(solution)/shard_map/mask_rest/pallas_call | solution.py:295
  16.8 44.9 %all-gather.3.cloned.1.call-done = f32[1024,2048]{1,0:T(8,128)} async-done(((f32[128,2048]{1,0:T(8,128)}), f32[1024,2048]{1,0:T(8,128)}) %all-gather.3.cloned.1.call-update) | async-done | bytes 8388624 | tf_op jit(solution)/shard_map/all_gather | solution.py:318
  61.7 1.3 constant_dynamic-slice_fusion.3
  63.0 6.3 %fusion.2 = f32[256,2048]{1,0:T(8,128)S(1)} fusion(f32[1024,2048]{1,0:T(8,128)} %all-gather.3.cloned.1.call-done, f32[1024,128]{1,0:T(8,128)S(1)} %get-tuple-element.21, f32[1024,128]{1,0:T(8,128)S(1)} %get-tuple-element.20), kind=kOutput, calls=%fused_computation.3 | convolution fusion | flops 3221487616 | bytes 11534336 | tf_op jit(solution)/shard_map/dot_general | solution.py:323
  69.2 0.1 fusion.7
  69.4 0.2 fusion.1
  69.5 23.6 %all_to_all.23 = f32[16,8,2176]{2,1,0:T(8,128)S(1)} all-to-all(f32[16,8,2176]{2,1,0:T(8,128)S(1)} %fusion.1), channel_id=1, replica_groups=mesh['z'=4,'k'=2,'y'=4,'x'=4] {'z','x'}, dimensions={0} | all-to-all | bytes 2228224 | tf_op jit(solution)/shard_map/all_to_all | solution.py:329
  93.2 0.1 reduce_sum.18
  93.2 0.6 broadcast_multiply_fusion.1
  93.9 0.0 all-gather.5.cloned.1.call-update
  93.9 6.5 %all-to-all-start.1 = ((f32[8,128,768]{2,1,0:T(8,128)}), f32[8,128,768]{2,1,0:T(8,128)S(1)}, u32[]{:S(2)}, u32[]{:S(2)}) async-start(f32[8,128,768]{2,1,0:T(8,128)} %mask_rest.1), calls=%async_computation.1 | async-start | bytes 6291456 | tf_op jit(solution)/shard_map/all_to_all | solution.py:334
  100.4 9.3 %copy.5 = f32[2048,1024]{1,0:T(8,128)} copy(f32[2048,1024]{0,1:T(8,128)} %bitcast.14) | data formatting | bytes 16777216 | tf_op jit(solution)/shard_map/dot_general | solution.py:336
  109.8 29.4 %all-to-all-done.1 = f32[8,128,768]{2,1,0:T(8,128)S(1)} async-done(((f32[8,128,768]{2,1,0:T(8,128)}), f32[8,128,768]{2,1,0:T(8,128)S(1)}, u32[]{:S(2)}, u32[]{:S(2)}) %all-to-all-start.1) | async-done | bytes 3145760 | tf_op jit(solution)/shard_map/all_to_all | solution.py:334
  139.2 14.3 %fusion.8 = f32[16,128,768]{2,1,0:T(8,128)} fusion(f32[16,128,1024]{2,1,0:T(8,128)} %bitcast.15, f32[1024,768,1]{1,0,2:T(8,128)S(1)} %bitcast.16), kind=kOutput, calls=%fused_computation.19 | convolution fusion | flops 9663676416 | bytes 17825792 | tf_op jit(solution)/shard_map/dot_general | solution.py:336
  153.6 4.6 %all-to-all-start.2 = ((f32[16,128,768]{2,1,0:T(8,128)}), f32[16,128,768]{2,1,0:T(8,128)}, u32[]{:S(2)}, u32[]{:S(2)}) async-start(f32[16,128,768]{2,1,0:T(8,128)} %fusion.8), calls=%async_computation.2 | async-start | bytes 12582912 | tf_op jit(solution)/shard_map/all_to_all | solution.py:337
  158.3 0.7 pad_add_fusion.place_ref
  158.9 34.5 %all-gather.5.cloned.1.call-done.packed_ref = f32[1024,2176]{1,0:T(8,128)} async-done(((f32[8,2176]{1,0:T(8,128)}), f32[1024,2176]{1,0:T(8,128)}) %all-gather.5.cloned.1.call-update) | async-done | bytes 8912912 | tf_op jit(solution)/shard_map/all_gather | solution.py:332
  193.4 74.2 %factor.1 = (f32[256,128]{1,0:T(8,128)}, f32[256,128]{1,0:T(8,128)}) custom-call(s32[2]{0:T(128)} %pad_add_fusion.place_ref, f32[1024,2176]{1,0:T(8,128)} %all-gather.5.cloned.1.call-done.packed_ref), custom_call_target="tpu_custom_call" | custom-call | flops 17179869184 | bytes 314572800 | tf_op jit(solution)/shard_map/factor/pallas_call | solution.py:238
  267.6 0.0 all-to-all-done.2
  267.6 0.0 copy-start
  267.7 3.2 %reduce_sum.19 = f32[128,768]{1,0:T(8,128)S(1)} reduce(f32[16,128,768]{2,1,0:T(8,128)} %bitcast.8, f32[]{:T(128)} %constant.49.clone.1), dimensions={0}, to_apply=%region_1.2 | reduce | flops 1474560 | bytes 6684676 | tf_op jit(solution)/shard_map/reduce_sum | solution.py:342
  270.9 2.7 collective-permute-start
  273.7 2.2 collective-permute-start.1
  275.8 5.1 %collective-permute-done = f32[128,384]{1,0:T(8,128)S(1)} collective-permute-done((f32[128,384]{1,0:T(8,128)S(1)}, f32[128,384]{1,0:T(8,128)S(1)}, u32[]{:S(2)}, u32[]{:S(2)}) %collective-permute-start) | collective-permute-done | bytes 196640 | tf_op jit(solution)/shard_map/ppermute | solution.py:350
  280.9 0.9 collective-permute-done.1
  281.9 0.0 copy-done
  281.9 0.9 pad_maximum_fusion
  (4 shorter events, 0.1 us)
Async XLA Ops:
  7.2 54.5 %all-gather.3.cloned.1.call-start = ((), (), s32[]{:S(2)}) async-start(), calls=%async_computation.3 | async-start | bytes 9437184 | tf_op jit(solution)/shard_map/all_gather | solution.py:318
  10.3 183.1 %all-gather.5.cloned.1.call-start = ((), (), s32[]{:S(2)}) async-start(), calls=%async_computation.4 | async-start | bytes 8982528 | tf_op jit(solution)/shard_map/all_gather | solution.py:332
  93.9 45.3 %all-to-all-start.1 = ((f32[8,128,768]{2,1,0:T(8,128)}), f32[8,128,768]{2,1,0:T(8,128)S(1)}, u32[]{:S(2)}, u32[]{:S(2)}) async-start(f32[8,128,768]{2,1,0:T(8,128)} %mask_rest.1), calls=%async_computation.1 | async-start | bytes 6291456 | tf_op jit(solution)/shard_map/all_to_all | solution.py:334
  153.6 114.1 %all-to-all-start.2 = ((f32[16,128,768]{2,1,0:T(8,128)}), f32[16,128,768]{2,1,0:T(8,128)}, u32[]{:S(2)}, u32[]{:S(2)}) async-start(f32[16,128,768]{2,1,0:T(8,128)} %fusion.8), calls=%async_computation.2 | async-start | bytes 12582912 | tf_op jit(solution)/shard_map/all_to_all | solution.py:337
  267.6 14.2 %copy-start = (f32[256,128]{1,0:T(8,128)S(1)}, f32[256,128]{1,0:T(8,128)}, u32[]{:S(2)}) copy-start(f32[256,128]{1,0:T(8,128)} %get-tuple-element.17) | copy-start | bytes 393220
  270.9 10.0 %collective-permute-start = (f32[128,384]{1,0:T(8,128)S(1)}, f32[128,384]{1,0:T(8,128)S(1)}, u32[]{:S(2)}, u32[]{:S(2)}) collective-permute-start(f32[128,384]{1,0:T(8,128)S(1)} %get-tuple-element.24), channel_id=1, source_target_pairs={{0,0},{1,1},{2,16},{3,17},{16,2},{17,3},{18,18},{19,19},{4,4},{5,5... | collective-permute-start | bytes 589832 | tf_op jit(solution)/shard_map/ppermute | solution.py:350
  273.7 8.2 %collective-permute-start.1 = (f32[128,384]{1,0:T(8,128)S(1)}, f32[128,384]{1,0:T(8,128)S(1)}, u32[]{:S(2)}, u32[]{:S(2)}) collective-permute-start(f32[128,384]{1,0:T(8,128)S(1)} %get-tuple-element.25), channel_id=1, source_target_pairs={{0,1},{1,0},{2,17},{3,16},{16,3},{17,2},{18,19},{19,18},{4,5},{5,4... | collective-permute-start | bytes 589832 | tf_op jit(solution)/shard_map/ppermute | solution.py:351
Sparse Core Ops, SparseCore 0:
  10.4 51.2 all-gather.2
  94.0 99.3 all-gather.4

commit v8 on v6

--- a/solution.py
+++ b/solution.py
@@ -329,7 +329,7 @@
     pieces = lax.all_to_all(packed, ("z", "x"), split_axis=0, concat_axis=0, tiled=True)
     mine = jnp.sum(pieces.reshape(ncols, BLK // ncols, -1), axis=0) / total_users
     mine, rest = lax.optimization_barrier((mine, rest))
-    panel = lax.all_gather(lax.all_gather(mine, "x", axis=0, tiled=True), ("y", "k", "z"), axis=0, tiled=True)
+    panel = lax.all_gather(mine, ("y", "k", "z", "x"), axis=0, tiled=True)
 
     others = lax.all_to_all(rest, ("y", "k"), split_axis=0, concat_axis=0, tiled=True)
     others = others.reshape(-1, others.shape[-1])

time: 281 us -> 274 us (0.975)
  blocking collectives: 93.2 us -> 68.9 us
  waiting for transfers between devices: 54.5 us -> 70.7 us
    all_to_all x1, blocking collectives: 58.8 us -> 45 us  [shards(): lax.all_to_all(rest, ('y', 'k'), split_axis=0, concat_axis=0, tiled=True)]
    all_gather x1, waiting for transfers between devices: 0.01 us -> 11.7 us  [shards(): panel = lax.all_gather(mine, ('y', 'k', 'z', 'x'), axis=0, tiled=True)]
    all_gather x1 -> x0, blocking collectives: 10.5 us -> none  [shards(): lax.all_gather(mine, 'x', axis=0, tiled=True)]
    reduce_scatter x1, waiting for transfers between devices: 3.21 us -> 7.7 us  [shards(): lax.psum_scatter(partial, ('z', 'x'), scatter_dimension=0, tiled=True)]
  transfers between devices with their start and end apart: 5 -> 5, of which waited for: 4 -> 5; matrix products, arithmetic and copies ran while one was open for 6% -> 6% of each run, Pallas kernels for 29% -> 30%
where the time goes in v8:
time: 274 us; the launch traced here: 272 us
  Pallas kernels  83.7 us (31%)
  waiting for transfers between devices  70.7 us (26%)
  blocking collectives  68.9 us (25%)
  matrix products  22 us (8%)
  between operations  13.9 us (5%)
  starting transfers between devices  6.1 us (2%)
  other arithmetic  4.49 us (2%)
    pallas_call x1, Pallas kernels, chol_piece(): pl.pallas_call(functools.partial(chol_kernel, nparts), out_shape=(flat, f...  74.2 us
    all_to_all x1, blocking collectives, shards(): lax.all_to_all(rest, ('y', 'k'), split_axis=0, concat_axis=0, tiled=True)  45 us
    all_gather x1, waiting for transfers between devices, shards(): bands = lax.all_gather(band, ('y', 'k'), axis=0, tiled=True)  44.9 us
    all_to_all x1, blocking collectives, shards(): lax.all_to_all(packed, ('z', 'x'), split_axis=0, concat_axis=0, tiled=True)  23.8 us
    dot_general x1, matrix products, shards(): partial = lax.dot_general(bands, others, over_users, **high)  15.7 us
    all_gather x1, waiting for transfers between devices, shards(): panel = lax.all_gather(mine, ('y', 'k', 'z', 'x'), axis=0, tiled=True)  11.7 us
    reduce_scatter x1, waiting for transfers between devices, shards(): lax.psum_scatter(partial, ('z', 'x'), scatter_dimension=0, tiled=True)  7.7 us
    pallas_call x1, Pallas kernels, other_columns(): pl.pallas_call(functools.partial(rest_kernel, pair), grid=(nrows,), out_s...  6.41 us
  transfers between devices with their start and end apart: 5, of which 5 were waited for; matrix products, arithmetic and copies ran while one was open for 6% of the time, Pallas kernels for 30%

profile of v8, /device:TPU:17, one launch (start us, length us, event | category | flops | bytes accessed | tf_op | source)
XLA Modules:
  0.0 272.1 jit_solution(11404298647624277594)
XLA Ops:
  7.2 0.0 all-gather.3.cloned.1.call-start
  7.2 3.0 %mask_band.1 = f32[128,2048]{1,0:T(8,128)} custom-call(s32[1,64]{1,0:T(1,128)} %keep_ref.3, f32[128,8192]{1,0:T(8,128)} %slab_ref.3), custom_call_target="tpu_custom_call" | custom-call | tf_op jit(solution)/shard_map/mask_band/pallas_call | solution.py:269
  10.3 0.0 all-gather.3.cloned.1.call-update
  10.3 0.0 all-gather.5.cloned.1.call-start
  10.3 6.4 %mask_rest.1 = f32[8,128,768]{2,1,0:T(8,128)} custom-call(s32[1,64]{1,0:T(1,128)} %keep_ref.3, f32[128,8192]{1,0:T(8,128)} %slab_ref.3), custom_call_target="tpu_custom_call" | custom-call | flops 1048576 | bytes 8388608 | tf_op jit(solution)/shard_map/mask_rest/pallas_call | solution.py:295
  16.8 44.9 %all-gather.3.cloned.1.call-done = f32[1024,2048]{1,0:T(8,128)} async-done(((f32[128,2048]{1,0:T(8,128)}), f32[1024,2048]{1,0:T(8,128)}) %all-gather.3.cloned.1.call-update) | async-done | bytes 8388624 | tf_op jit(solution)/shard_map/all_gather | solution.py:318
  61.7 1.3 constant_dynamic-slice_fusion.3
  63.0 6.3 %fusion.2 = f32[256,2048]{1,0:T(8,128)S(1)} fusion(f32[1024,2048]{1,0:T(8,128)} %all-gather.3.cloned.1.call-done, f32[1024,128]{1,0:T(8,128)S(1)} %get-tuple-element.25, f32[1024,128]{1,0:T(8,128)S(1)} %get-tuple-element.24), kind=kOutput, calls=%fused_computation.3 | convolution fusion | flops 3221487616 | bytes 11534336 | tf_op jit(solution)/shard_map/dot_general | solution.py:323
  69.2 0.1 fusion.8
  69.4 0.0 copy-start
  69.4 0.2 fusion.1
  69.5 23.8 %all_to_all.14 = f32[16,8,2176]{2,1,0:T(8,128)} all-to-all(f32[16,8,2176]{2,1,0:T(8,128)S(1)} %fusion.1), channel_id=1, replica_groups=mesh['z'=4,'k'=2,'y'=4,'x'=4] {'z','x'}, dimensions={0} | all-to-all | bytes 2228224 | tf_op jit(solution)/shard_map/all_to_all | solution.py:329
  93.4 1.3 reduce_sum.9
  94.7 0.6 broadcast_multiply_fusion
  95.3 0.0 all-gather.5.cloned.1.call-update
  95.4 0.0 reduce-scatter.2.cloned.1.call-start
  95.4 0.0 copy-done
  95.4 45.0 %all_to_all.15 = f32[8,128,768]{2,1,0:T(8,128)S(1)} all-to-all(f32[8,128,768]{2,1,0:T(8,128)S(1)} %copy-done), channel_id=1, replica_groups=mesh['z'=4,'k'=2,'y'=4,'x'=4] {'y','k'}, dimensions={0} | all-to-all | bytes 6291456 | tf_op jit(solution)/shard_map/all_to_all | solution.py:334
  140.4 15.7 %fusion.9 = f32[2048,768]{1,0:T(8,128)} fusion(f32[1024,2048]{1,0:T(8,128)} %all-gather.3.cloned.1.call-done, f32[1024,768]{1,0:T(8,128)S(1)} %bitcast.8), kind=kOutput, calls=%fused_computation.19 | convolution fusion | flops 9663676416 | bytes 17825792 | tf_op jit(solution)/shard_map/dot_general | solution.py:336
  156.2 11.7 %all-gather.5.cloned.1.call-done.packed_ref = f32[1024,2176]{1,0:T(8,128)} async-done(((f32[8,2176]{1,0:T(8,128)}), f32[1024,2176]{1,0:T(8,128)}) %all-gather.5.cloned.1.call-update) | async-done | bytes 8912912 | tf_op jit(solution)/shard_map/all_gather | solution.py:332
  167.9 0.0 reduce-scatter.2.cloned.1.call-update
  168.0 0.6 pad_add_fusion.place_ref
  168.5 74.2 %factor.1 = (f32[256,128]{1,0:T(8,128)}, f32[256,128]{1,0:T(8,128)}) custom-call(s32[2]{0:T(128)} %pad_add_fusion.place_ref, f32[1024,2176]{1,0:T(8,128)} %all-gather.5.cloned.1.call-done.packed_ref), custom_call_target="tpu_custom_call" | custom-call | flops 17179869184 | bytes 314572800 | tf_op jit(solution)/shard_map/factor/pallas_call | solution.py:238
  242.8 7.7 %reduce-scatter.2.cloned.1.call-done = f32[128,768]{1,0:T(8,128)} async-done(((f32[2048,768]{1,0:T(8,128)}), f32[128,768]{1,0:T(8,128)}) %reduce-scatter.2.cloned.1.call-update) | async-done | bytes 393232 | tf_op jit(solution)/shard_map/reduce_scatter | solution.py:338
  250.5 1.0 constant_dynamic-slice_fusion.1
  251.5 5.9 %collective-permute-start = (f32[128,384]{1,0:T(8,128)S(1)}, f32[128,384]{1,0:T(8,128)S(1)}, u32[]{:S(2)}, u32[]{:S(2)}) collective-permute-start(f32[128,384]{1,0:T(8,128)S(1)} %get-tuple-element.28), channel_id=1, source_target_pairs={{0,0},{1,1},{2,16},{3,17},{16,2},{17,3},{18,18},{19,19},{4,4},{5,5... | collective-permute-start | bytes 589832 | tf_op jit(solution)/shard_map/ppermute | solution.py:350
  257.4 0.1 collective-permute-start.1
  257.5 3.2 %collective-permute-done = f32[128,384]{1,0:T(8,128)S(1)} collective-permute-done((f32[128,384]{1,0:T(8,128)S(1)}, f32[128,384]{1,0:T(8,128)S(1)}, u32[]{:S(2)}, u32[]{:S(2)}) %collective-permute-start) | collective-permute-done | bytes 196640 | tf_op jit(solution)/shard_map/ppermute | solution.py:350
  260.8 3.0 %collective-permute-done.1 = f32[128,384]{1,0:T(8,128)S(1)} collective-permute-done((f32[128,384]{1,0:T(8,128)S(1)}, f32[128,384]{1,0:T(8,128)S(1)}, u32[]{:S(2)}, u32[]{:S(2)}) %collective-permute-start.1) | collective-permute-done | bytes 196640 | tf_op jit(solution)/shard_map/ppermute | solution.py:351
  263.8 1.8 pad_maximum_fusion
  (2 shorter events, 0.0 us)
Async XLA Ops:
  7.2 54.5 %all-gather.3.cloned.1.call-start = ((), (), s32[]{:S(2)}) async-start(), calls=%async_computation.3 | async-start | bytes 9437184 | tf_op jit(solution)/shard_map/all_gather | solution.py:318
  10.3 157.6 %all-gather.5.cloned.1.call-start = ((), (), s32[]{:S(2)}) async-start(), calls=%async_computation.4 | async-start | bytes 8982528 | tf_op jit(solution)/shard_map/all_gather | solution.py:332
  69.4 26.1 %copy-start = (f32[8,128,768]{2,1,0:T(8,128)S(1)}, f32[8,128,768]{2,1,0:T(8,128)}, u32[]{:S(2)}) copy-start(f32[8,128,768]{2,1,0:T(8,128)} %mask_rest.1) | copy-start | bytes 9437188
  95.4 155.1 %reduce-scatter.2.cloned.1.call-start = ((), (), s32[]{:S(2)}) async-start(), calls=%async_computation.5 | async-start | bytes 6684672 | tf_op jit(solution)/shard_map/reduce_scatter | solution.py:338
  251.5 9.2 %collective-permute-start = (f32[128,384]{1,0:T(8,128)S(1)}, f32[128,384]{1,0:T(8,128)S(1)}, u32[]{:S(2)}, u32[]{:S(2)}) collective-permute-start(f32[128,384]{1,0:T(8,128)S(1)} %get-tuple-element.28), channel_id=1, source_target_pairs={{0,0},{1,1},{2,16},{3,17},{16,2},{17,3},{18,18},{19,19},{4,4},{5,5... | collective-permute-start | bytes 589832 | tf_op jit(solution)/shard_map/ppermute | solution.py:350
  257.4 6.4 %collective-permute-start.1 = (f32[128,384]{1,0:T(8,128)S(1)}, f32[128,384]{1,0:T(8,128)S(1)}, u32[]{:S(2)}, u32[]{:S(2)}) collective-permute-start(f32[128,384]{1,0:T(8,128)S(1)} %get-tuple-element.29), channel_id=1, source_target_pairs={{0,1},{1,0},{2,17},{3,16},{16,3},{17,2},{18,19},{19,18},{4,5},{5,4... | collective-permute-start | bytes 589832 | tf_op jit(solution)/shard_map/ppermute | solution.py:351
Sparse Core Ops, SparseCore 0:
  10.4 51.2 all-gather.2
  95.5 72.3 all-gather.4
  171.3 79.0 reduce-scatter.1

commit v9 on v8

--- a/solution.py
+++ b/solution.py
@@ -249,7 +249,7 @@
     )(place, packed)
 
 
-def band_kernel(keep_ref, slab_ref, band_ref, got, sems):
+def band_kernel(scale, keep_ref, slab_ref, band_ref, got, sems):
     ncols = band_ref.shape[1] // BLK
     step = slab_ref.shape[1] // ncols
     copies = [
@@ -261,13 +261,13 @@
     for c, copy in enumerate(copies):
         copy.wait()
         at = slice(c * BLK, (c + 1) * BLK)
-        band_ref[:, at] = got[:, at] * keep_ref[0, c * step // BLK].astype(jnp.float32)
-
-
-def band_columns(slab, block_mask, ncols):
+        band_ref[:, at] = got[:, at] * (keep_ref[0, c * step // BLK].astype(jnp.float32) * scale)
+
+
+def band_columns(slab, block_mask, ncols, scale):
     users = slab.shape[0]
     return pl.pallas_call(
-        band_kernel,
+        functools.partial(band_kernel, scale),
         out_shape=jax.ShapeDtypeStruct((users, BLK * ncols), jnp.float32),
         in_specs=[pl.BlockSpec(memory_space=pltpu.SMEM), pl.BlockSpec(memory_space=pl.ANY)],
         out_specs=pl.BlockSpec(memory_space=pltpu.VMEM),
@@ -276,24 +276,24 @@
     )(block_mask, slab)
 
 
-def rest_kernel(pair, keep_ref, slab_ref, rest_ref):
+def rest_kernel(pair, scale, keep_ref, slab_ref, rest_ref):
     g = pl.program_id(0)
     blocks = slab_ref.shape[1] // BLK
     per = blocks // pair
     to = 0
     for b in range(blocks):
         if b % per:
-            keep = keep_ref[0, g * blocks + b].astype(jnp.float32)
+            keep = keep_ref[0, g * blocks + b].astype(jnp.float32) * scale
             rest_ref[0, :, to:to + BLK] = slab_ref[:, b * BLK:(b + 1) * BLK] * keep
             to += BLK
 
 
-def other_columns(slab, block_mask, ncols, nrows):
+def other_columns(slab, block_mask, ncols, nrows, scale):
     users, items = slab.shape
     pair = ncols // nrows
     other = items // nrows - pair * BLK
     return pl.pallas_call(
-        functools.partial(rest_kernel, pair),
+        functools.partial(rest_kernel, pair, scale),
         grid=(nrows,),
         out_shape=jax.ShapeDtypeStruct((nrows, users, other), jnp.float32),
         in_specs=[pl.BlockSpec(memory_space=pltpu.SMEM), pl.BlockSpec((users, items // nrows), lambda g: (0, g))],
@@ -313,8 +313,10 @@
     high = dict(precision=lax.Precision.HIGH, preferred_element_type=jnp.float32)
     over_users = (((0,), (0,)), ((), ()))
 
-    band = band_columns(slab, block_mask, ncols)
-    rest = other_columns(slab, block_mask, ncols, groups)
+    scale = 2.0 ** -(total_users.bit_length() // 2)
+    assert scale * scale * total_users == 1.0
+    band = band_columns(slab, block_mask, ncols, scale)
+    rest = other_columns(slab, block_mask, ncols, groups, scale)
     bands = lax.all_gather(band, ("y", "k"), axis=0, tiled=True)
     bands, rest = lax.optimization_barrier((bands, rest))
 
@@ -327,14 +329,13 @@
     lane = lax.broadcasted_iota(jnp.int32, moved.shape, 1)
     packed = jnp.where(lane < BLK * (ncols - g), long, moved)
     pieces = lax.all_to_all(packed, ("z", "x"), split_axis=0, concat_axis=0, tiled=True)
-    mine = jnp.sum(pieces.reshape(ncols, BLK // ncols, -1), axis=0) / total_users
+    mine = jnp.sum(pieces.reshape(ncols, BLK // ncols, -1), axis=0)
     mine, rest = lax.optimization_barrier((mine, rest))
     panel = lax.all_gather(mine, ("y", "k", "z", "x"), axis=0, tiled=True)
 
     others = lax.all_to_all(rest, ("y", "k"), split_axis=0, concat_axis=0, tiled=True)
     others = others.reshape(-1, others.shape[-1])
     partial = lax.dot_general(bands, others, over_users, **high)
-    panel, partial = lax.optimization_barrier((panel, partial))
     strip = lax.psum_scatter(partial, ("z", "x"), scatter_dimension=0, tiled=True)
 
     place = jnp.stack([lax.axis_size("k") * z + k, lax.axis_size("x") * y + x]).astype(jnp.int32)
@@ -349,7 +350,7 @@
     to = lambda i, j: i * nx + j
     own = lax.ppermute(own, ("k", "x"), [(to(i, j), to(j // 2, 2 * i + j % 2)) for i, j in at])
     far = lax.ppermute(far, ("k", "x"), [(to(i, j), to(j // 2, 2 * i + 1 - j % 2)) for i, j in at])
-    items = jnp.where(odd == 0, jnp.concatenate([own, far]), jnp.concatenate([far, own])) / total_users
+    items = jnp.where(odd == 0, jnp.concatenate([own, far]), jnp.concatenate([far, own]))
     return (jnp.concatenate([block, items], axis=1), piece)
 
 

time: 274 us -> 273 us (level)
  no operation moved by 1% of the time
where the time goes in v9:
time: 273 us; the launch traced here: 272 us
  Pallas kernels  83.7 us (31%)
  waiting for transfers between devices  70.4 us (26%)
  blocking collectives  68.9 us (25%)
  matrix products  22 us (8%)
  between operations  13.9 us (5%)
  starting transfers between devices  6.1 us (2%)
  other arithmetic  4.48 us (2%)
    pallas_call x1, Pallas kernels, chol_piece(): pl.pallas_call(functools.partial(chol_kernel, nparts), out_shape=(flat, f...  74.2 us
    all_to_all x1, blocking collectives, shards(): lax.all_to_all(rest, ('y', 'k'), split_axis=0, concat_axis=0, tiled=True)  45 us
    all_gather x1, waiting for transfers between devices, shards(): bands = lax.all_gather(band, ('y', 'k'), axis=0, tiled=True)  44.9 us
    all_to_all x1, blocking collectives, shards(): lax.all_to_all(packed, ('z', 'x'), split_axis=0, concat_axis=0, tiled=True)  23.9 us
    dot_general x1, matrix products, shards(): partial = lax.dot_general(bands, others, over_users, **high)  15.7 us
    all_gather x1, waiting for transfers between devices, shards(): panel = lax.all_gather(mine, ('y', 'k', 'z', 'x'), axis=0, tiled=True)  11.1 us
    reduce_scatter x1, waiting for transfers between devices, shards(): lax.psum_scatter(partial, ('z', 'x'), scatter_dimension=0, tiled=True)  8.1 us
    pallas_call x1, Pallas kernels, other_columns(): pl.pallas_call(functools.partial(rest_kernel, pair, scale), grid=(nrows,)...  6.42 us
  transfers between devices with their start and end apart: 5, of which 5 were waited for; matrix products, arithmetic and copies ran while one was open for 6% of the time, Pallas kernels for 30%

profile of v9, /device:TPU:17, one launch (start us, length us, event | category | flops | bytes accessed | tf_op | source)
XLA Modules:
  0.0 271.9 jit_solution(11853977754969961516)
XLA Ops:
  7.2 0.0 all-gather.3.cloned.1.call-start
  7.2 3.0 %mask_band.1 = f32[128,2048]{1,0:T(8,128)} custom-call(s32[1,64]{1,0:T(1,128)} %keep_ref.3, f32[128,8192]{1,0:T(8,128)} %slab_ref.3), custom_call_target="tpu_custom_call" | custom-call | tf_op jit(solution)/shard_map/mask_band/pallas_call | solution.py:269
  10.3 0.0 all-gather.3.cloned.1.call-update
  10.3 0.0 all-gather.5.cloned.1.call-start
  10.3 6.4 %mask_rest.1 = f32[8,128,768]{2,1,0:T(8,128)} custom-call(s32[1,64]{1,0:T(1,128)} %keep_ref.3, f32[128,8192]{1,0:T(8,128)} %slab_ref.3), custom_call_target="tpu_custom_call" | custom-call | flops 1048576 | bytes 8388608 | tf_op jit(solution)/shard_map/mask_rest/pallas_call | solution.py:295
  16.8 44.9 %all-gather.3.cloned.1.call-done = f32[1024,2048]{1,0:T(8,128)} async-done(((f32[128,2048]{1,0:T(8,128)}), f32[1024,2048]{1,0:T(8,128)}) %all-gather.3.cloned.1.call-update) | async-done | bytes 8388624 | tf_op jit(solution)/shard_map/all_gather | solution.py:320
  61.7 1.3 constant_dynamic-slice_fusion.3
  63.0 6.3 %fusion.2 = f32[256,2048]{1,0:T(8,128)S(1)} fusion(f32[1024,2048]{1,0:T(8,128)} %all-gather.3.cloned.1.call-done, f32[1024,128]{1,0:T(8,128)S(1)} %get-tuple-element.21, f32[1024,128]{1,0:T(8,128)S(1)} %get-tuple-element.20), kind=kOutput, calls=%fused_computation.3 | convolution fusion | flops 3221487616 | bytes 11534336 | tf_op jit(solution)/shard_map/dot_general | solution.py:325
  69.2 0.1 fusion.7
  69.4 0.0 copy-start
  69.4 0.2 fusion.1
  69.5 23.9 %all_to_all.14 = f32[16,8,2176]{2,1,0:T(8,128)} all-to-all(f32[16,8,2176]{2,1,0:T(8,128)S(1)} %fusion.1), channel_id=1, replica_groups=mesh['z'=4,'k'=2,'y'=4,'x'=4] {'z','x'}, dimensions={0} | all-to-all | bytes 2228224 | tf_op jit(solution)/shard_map/all_to_all | solution.py:331
  93.4 1.9 reduce_sum.9
  95.3 0.0 all-gather.5.cloned.1.call-update
  95.4 0.0 reduce-scatter.2.cloned.1.call-start
  95.4 0.0 copy-done
  95.4 45.0 %all_to_all.15 = f32[8,128,768]{2,1,0:T(8,128)S(1)} all-to-all(f32[8,128,768]{2,1,0:T(8,128)S(1)} %copy-done), channel_id=1, replica_groups=mesh['z'=4,'k'=2,'y'=4,'x'=4] {'y','k'}, dimensions={0} | all-to-all | bytes 6291456 | tf_op jit(solution)/shard_map/all_to_all | solution.py:336
  140.4 15.7 %fusion.8 = f32[2048,768]{1,0:T(8,128)} fusion(f32[1024,2048]{1,0:T(8,128)} %all-gather.3.cloned.1.call-done, f32[1024,768]{1,0:T(8,128)S(1)} %bitcast.8), kind=kOutput, calls=%fused_computation.17 | convolution fusion | flops 9663676416 | bytes 17825792 | tf_op jit(solution)/shard_map/dot_general | solution.py:338
  156.2 0.0 reduce-scatter.2.cloned.1.call-update
  156.2 0.6 pad_add_fusion.place_ref
  156.8 11.1 %all-gather.5.cloned.1.call-done.packed_ref = f32[1024,2176]{1,0:T(8,128)} async-done(((f32[8,2176]{1,0:T(8,128)}), f32[1024,2176]{1,0:T(8,128)}) %all-gather.5.cloned.1.call-update) | async-done | bytes 8912912 | tf_op jit(solution)/shard_map/all_gather | solution.py:334
  167.9 74.2 %factor.1 = (f32[256,128]{1,0:T(8,128)}, f32[256,128]{1,0:T(8,128)}) custom-call(s32[2]{0:T(128)} %pad_add_fusion.place_ref, f32[1024,2176]{1,0:T(8,128)} %all-gather.5.cloned.1.call-done.packed_ref), custom_call_target="tpu_custom_call" | custom-call | flops 17179869184 | bytes 314572800 | tf_op jit(solution)/shard_map/factor/pallas_call | solution.py:238
  242.1 8.1 %reduce-scatter.2.cloned.1.call-done = f32[128,768]{1,0:T(8,128)} async-done(((f32[2048,768]{1,0:T(8,128)}), f32[128,768]{1,0:T(8,128)}) %reduce-scatter.2.cloned.1.call-update) | async-done | bytes 393232 | tf_op jit(solution)/shard_map/reduce_scatter | solution.py:339
  250.2 1.0 constant_dynamic-slice_fusion.1
  251.3 5.9 %collective-permute-start = (f32[128,384]{1,0:T(8,128)S(1)}, f32[128,384]{1,0:T(8,128)S(1)}, u32[]{:S(2)}, u32[]{:S(2)}) collective-permute-start(f32[128,384]{1,0:T(8,128)S(1)} %get-tuple-element.24), channel_id=1, source_target_pairs={{0,0},{1,1},{2,16},{3,17},{16,2},{17,3},{18,18},{19,19},{4,4},{5,5... | collective-permute-start | bytes 589832 | tf_op jit(solution)/shard_map/ppermute | solution.py:351
  257.2 0.1 collective-permute-start.1
  257.3 3.2 %collective-permute-done = f32[128,384]{1,0:T(8,128)S(1)} collective-permute-done((f32[128,384]{1,0:T(8,128)S(1)}, f32[128,384]{1,0:T(8,128)S(1)}, u32[]{:S(2)}, u32[]{:S(2)}) %collective-permute-start) | collective-permute-done | bytes 196640 | tf_op jit(solution)/shard_map/ppermute | solution.py:351
  260.5 3.0 %collective-permute-done.1 = f32[128,384]{1,0:T(8,128)S(1)} collective-permute-done((f32[128,384]{1,0:T(8,128)S(1)}, f32[128,384]{1,0:T(8,128)S(1)}, u32[]{:S(2)}, u32[]{:S(2)}) %collective-permute-start.1) | collective-permute-done | bytes 196640 | tf_op jit(solution)/shard_map/ppermute | solution.py:352
  263.6 1.8 pad_maximum_fusion
  (2 shorter events, 0.0 us)
Async XLA Ops:
  7.2 54.5 %all-gather.3.cloned.1.call-start = ((), (), s32[]{:S(2)}) async-start(), calls=%async_computation.3 | async-start | bytes 9437184 | tf_op jit(solution)/shard_map/all_gather | solution.py:320
  10.3 157.6 %all-gather.5.cloned.1.call-start = ((), (), s32[]{:S(2)}) async-start(), calls=%async_computation.5 | async-start | bytes 8982528 | tf_op jit(solution)/shard_map/all_gather | solution.py:334
  69.4 26.1 %copy-start = (f32[8,128,768]{2,1,0:T(8,128)S(1)}, f32[8,128,768]{2,1,0:T(8,128)}, u32[]{:S(2)}) copy-start(f32[8,128,768]{2,1,0:T(8,128)} %mask_rest.1) | copy-start | bytes 9437188
  95.4 154.9 %reduce-scatter.2.cloned.1.call-start = ((), (), s32[]{:S(2)}) async-start(), calls=%async_computation.4 | async-start | bytes 6684672 | tf_op jit(solution)/shard_map/reduce_scatter | solution.py:339
  251.3 9.2 %collective-permute-start = (f32[128,384]{1,0:T(8,128)S(1)}, f32[128,384]{1,0:T(8,128)S(1)}, u32[]{:S(2)}, u32[]{:S(2)}) collective-permute-start(f32[128,384]{1,0:T(8,128)S(1)} %get-tuple-element.24), channel_id=1, source_target_pairs={{0,0},{1,1},{2,16},{3,17},{16,2},{17,3},{18,18},{19,19},{4,4},{5,5... | collective-permute-start | bytes 589832 | tf_op jit(solution)/shard_map/ppermute | solution.py:351
  257.2 6.4 %collective-permute-start.1 = (f32[128,384]{1,0:T(8,128)S(1)}, f32[128,384]{1,0:T(8,128)S(1)}, u32[]{:S(2)}, u32[]{:S(2)}) collective-permute-start(f32[128,384]{1,0:T(8,128)S(1)} %get-tuple-element.25), channel_id=1, source_target_pairs={{0,1},{1,0},{2,17},{3,16},{16,3},{17,2},{18,19},{19,18},{4,5},{5,4... | collective-permute-start | bytes 589832 | tf_op jit(solution)/shard_map/ppermute | solution.py:352
Sparse Core Ops, SparseCore 0:
  10.4 51.2 all-gather.2
  95.5 72.3 all-gather.4
  171.3 78.8 reduce-scatter.1

commit v10 on v9

--- a/solution.py
+++ b/solution.py
@@ -303,6 +303,57 @@
     )(block_mask, slab)
 
 
+def strips_kernel(k_ref, left_ref, own_ref, far_ref, out_ref, left, right):
+    depth = own_ref.shape[0]
+    x = pl.program_id(1)
+
+    @pl.when(x == 0)
+    def _():
+        for q in range(2):
+            at = jnp.where(q == 0, k_ref[0], 1 - k_ref[0]) * depth
+            high, low = split(left_ref[pl.ds(pl.multiple_of(at, depth), depth), :].T, 2)
+            for i, part in enumerate((high, high, low)):
+                left[q, :, depth * i:depth * (i + 1)] = part
+
+    @pl.when(pl.program_id(0) == 0)
+    def _():
+        for q, ref in enumerate((own_ref, far_ref)):
+            high, low = split(ref[...], 2)
+            for i, part in enumerate((high, low, high)):
+                right[x, q, depth * i:depth * (i + 1), :] = part
+
+    both = jnp.dot(left[0], right[x, 0], preferred_element_type=jnp.float32) + jnp.dot(
+        left[1], right[x, 1], preferred_element_type=jnp.float32
+    )
+    cols = out_ref.shape[-1]
+    for i in range(out_ref.shape[0]):
+        out_ref[i, 0] = both[:, cols * i:cols * (i + 1)]
+
+
+def strips(k, bands, own, far, nz, nx):
+    users, width = bands.shape
+    rows, cols = width // (2 * nz), own.shape[1] // nx
+    here = pl.BlockSpec((users // 2, 2 * cols), lambda z, x, k: (0, x))
+    out = pl.pallas_call(
+        strips_kernel,
+        out_shape=jax.ShapeDtypeStruct((nx, nz, rows, cols), jnp.float32),
+        grid_spec=pltpu.PrefetchScalarGridSpec(
+            num_scalar_prefetch=1,
+            grid=(nz, nx // 2),
+            in_specs=[pl.BlockSpec((users, rows), lambda z, x, k: (0, 2 * z + k[0])), here, here],
+            out_specs=pl.BlockSpec((2, 1, rows, cols), lambda z, x, k: (x, z, 0, 0)),
+            scratch_shapes=[
+                pltpu.VMEM((2, rows, 3 * users // 2), jnp.bfloat16),
+                pltpu.VMEM((nx // 2, 2, 3 * users // 2, 2 * cols), jnp.bfloat16),
+            ],
+        ),
+        compiler_params=pltpu.CompilerParams(vmem_limit_bytes=32 * 2**20),
+        cost_estimate=pl.CostEstimate(flops=6 * users * nz * rows * nx * cols, bytes_accessed=40 * 2**20, transcendentals=0),
+        name="strips",
+    )(k.reshape(1).astype(jnp.int32), bands, own, far)
+    return out.reshape(nx * nz * rows, cols)
+
+
 def shards(slab, block_mask):
     z, k, y, x = (lax.axis_index(axis) for axis in ("z", "k", "y", "x"))
     groups = lax.axis_size("y") * lax.axis_size("k")
@@ -316,8 +367,8 @@
     scale = 2.0 ** -(total_users.bit_length() // 2)
     assert scale * scale * total_users == 1.0
     band = band_columns(slab, block_mask, ncols, scale)
-    rest = other_columns(slab, block_mask, ncols, groups, scale)
-    bands = lax.all_gather(band, ("y", "k"), axis=0, tiled=True)
+    rest = other_columns(slab, block_mask, ncols, lax.axis_size("y"), scale)
+    bands = lax.all_gather(band, ("k", "y"), axis=0, tiled=True)
     bands, rest = lax.optimization_barrier((bands, rest))
 
     upper = lax.dynamic_slice_in_dim(bands, BLK * g, BLK, 1)
@@ -333,24 +384,15 @@
     mine, rest = lax.optimization_barrier((mine, rest))
     panel = lax.all_gather(mine, ("y", "k", "z", "x"), axis=0, tiled=True)
 
-    others = lax.all_to_all(rest, ("y", "k"), split_axis=0, concat_axis=0, tiled=True)
-    others = others.reshape(-1, others.shape[-1])
-    partial = lax.dot_general(bands, others, over_users, **high)
-    strip = lax.psum_scatter(partial, ("z", "x"), scatter_dimension=0, tiled=True)
+    own = lax.all_to_all(rest, "y", split_axis=0, concat_axis=0, tiled=True)
+    own = own.reshape(-1, own.shape[-1])
+    far = lax.ppermute(own, "k", [(0, 1), (1, 0)])
+    partial = strips(k, bands, own, far, lax.axis_size("z"), lax.axis_size("x"))
+    items = lax.psum_scatter(partial, ("x", "z"), scatter_dimension=0, tiled=True)
 
     place = jnp.stack([lax.axis_size("k") * z + k, lax.axis_size("x") * y + x]).astype(jnp.int32)
     block, piece = chol_piece(panel, place, BLK * ncols, BLK * pair)
-    strip, block, piece = lax.optimization_barrier((strip, block, piece))
-    half = strip.shape[1] // pair
-    odd = x % 2
-    own = lax.dynamic_slice_in_dim(strip, half * odd, half, 1)
-    far = lax.dynamic_slice_in_dim(strip, half * (1 - odd), half, 1)
-    nx = lax.axis_size("x")
-    at = [(i, j) for i in range(lax.axis_size("k")) for j in range(nx)]
-    to = lambda i, j: i * nx + j
-    own = lax.ppermute(own, ("k", "x"), [(to(i, j), to(j // 2, 2 * i + j % 2)) for i, j in at])
-    far = lax.ppermute(far, ("k", "x"), [(to(i, j), to(j // 2, 2 * i + 1 - j % 2)) for i, j in at])
-    items = jnp.where(odd == 0, jnp.concatenate([own, far]), jnp.concatenate([far, own]))
+    items, block, piece = lax.optimization_barrier((items, block, piece))
     return (jnp.concatenate([block, items], axis=1), piece)
 
 

time: 273 us -> 259 us (0.949)
  matrix products: 22 us -> 6.25 us
  Pallas kernels: 83.7 us -> 97.9 us
  waiting for transfers between devices: 70.4 us -> 59.2 us
  blocking collectives: 68.9 us -> 63.8 us
  local copies, waits for them, and re-layouts: 2.47 us -> 7.5 us
    pallas_call x0 -> x1, Pallas kernels: none -> 16.1 us  [strips(): pl.pallas_call(strips_kernel, out_shape=jax.ShapeDtypeStruct((nx, nz, row...]
    dot_general x1 -> x0, matrix products: 15.7 us -> none  [shards(): partial = lax.dot_general(bands, others, over_users, **high)]
    all_gather x1, waiting for transfers between devices: 11.1 us -> 0.01 us  [shards(): panel = lax.all_gather(mine, ('y', 'k', 'z', 'x'), axis=0, tiled=True)]
    unnamed x2 -> x6, local copies, waits for them, and re-layouts: 0.01 us -> 6.08 us
    all_to_all x1, blocking collectives: 45 us -> 39.9 us  [shards(): own = lax.all_to_all(rest, 'y', split_axis=0, concat_axis=0, tiled=True)]
    ppermute x2 -> x1, starting transfers between devices: 5.97 us -> 4.01 us  [shards(): far = lax.ppermute(own, 'k', [(0, 1), (1, 0)])]
    ppermute x2 -> x1, waiting for transfers between devices: 6.29 us -> 5.29 us  [shards(): far = lax.ppermute(own, 'k', [(0, 1), (1, 0)])]
  transfers between devices with their start and end apart: 5 -> 4, of which waited for: 5 -> 3; matrix products, arithmetic and copies ran while one was open for 6% -> 0% of each run, Pallas kernels for 30% -> 37%
where the time goes in v10:
time: 259 us; the launch traced here: 257 us
  Pallas kernels  97.9 us (38%)
  blocking collectives  63.8 us (25%)
  waiting for transfers between devices  59.2 us (23%)
  between operations  13.8 us (5%)
  local copies, waits for them, and re-layouts  7.5 us (3%)
  matrix products  6.25 us (2%)
  other arithmetic  4.53 us (2%)
  starting transfers between devices  4.14 us (2%)
    pallas_call x1, Pallas kernels, chol_piece(): pl.pallas_call(functools.partial(chol_kernel, nparts), out_shape=(flat, f...  74.2 us
    all_gather x1, waiting for transfers between devices, shards(): bands = lax.all_gather(band, ('k', 'y'), axis=0, tiled=True)  46.8 us
    all_to_all x1, blocking collectives, shards(): own = lax.all_to_all(rest, 'y', split_axis=0, concat_axis=0, tiled=True)  39.9 us
    all_to_all x1, blocking collectives, shards(): lax.all_to_all(packed, ('z', 'x'), split_axis=0, concat_axis=0, tiled=True)  23.9 us
    pallas_call x1, Pallas kernels, strips(): pl.pallas_call(strips_kernel, out_shape=jax.ShapeDtypeStruct((nx, nz, row...  16.1 us
    reduce_scatter x1, waiting for transfers between devices, shards(): lax.psum_scatter(partial, ('x', 'z'), scatter_dimension=0, tiled=True)  7.04 us
    dot_general x1, matrix products, shards(): lax.dot_general(jnp.concatenate([lower, upper], axis=1), bands, over_user...  6.25 us
    unnamed x6, local copies, waits for them, and re-layouts  6.08 us
  transfers between devices with their start and end apart: 4, of which 3 were waited for; matrix products, arithmetic and copies ran while one was open for 0% of the time, Pallas kernels for 37%

profile of v10, /device:TPU:17, one launch (start us, length us, event | category | flops | bytes accessed | tf_op | source)
XLA Modules:
  0.0 257.1 jit_solution(12188875754579973739)
XLA Ops:
  7.2 0.0 all-gather.3.cloned.1.call-start
  7.2 3.0 %mask_band.1 = f32[128,2048]{1,0:T(8,128)} custom-call(s32[1,64]{1,0:T(1,128)} %keep_ref.3, f32[128,8192]{1,0:T(8,128)} %slab_ref.3), custom_call_target="tpu_custom_call" | custom-call | tf_op jit(solution)/shard_map/mask_band/pallas_call | solution.py:269
  10.3 0.0 all-gather.3.cloned.1.call-update
  10.3 0.0 all-gather.5.cloned.1.call-start
  10.3 4.5 %mask_rest.1 = f32[4,128,1536]{2,1,0:T(8,128)} custom-call(s32[1,64]{1,0:T(1,128)} %keep_ref.3, f32[128,8192]{1,0:T(8,128)} %slab_ref.3), custom_call_target="tpu_custom_call" | custom-call | flops 1048576 | bytes 8388608 | tf_op jit(solution)/shard_map/mask_rest/pallas_call | solution.py:295
  14.9 46.8 %all-gather.3.cloned.1.call-done.left_ref = f32[1024,2048]{1,0:T(8,128)} async-done(((f32[128,2048]{1,0:T(8,128)}), f32[1024,2048]{1,0:T(8,128)}) %all-gather.3.cloned.1.call-update) | async-done | bytes 8388624 | tf_op jit(solution)/shard_map/all_gather | solution.py:371
  61.7 1.3 constant_dynamic-slice_fusion.1
  63.0 6.3 %fusion.2 = f32[256,2048]{1,0:T(8,128)S(1)} fusion(f32[1024,2048]{1,0:T(8,128)} %all-gather.3.cloned.1.call-done.left_ref, f32[1024,128]{1,0:T(8,128)S(1)} %get-tuple-element.21, f32[1024,128]{1,0:T(8,128)S(1)} %get-tuple-element.20), kind=kOutput, calls=%fused_computation.3 | convolution fusion | flops 3221487616 | bytes 11534336 | tf_op jit(solution)/shard_map/dot_general | solution.py:376
  69.2 0.1 fusion.7
  69.4 0.0 copy-start.2
  69.4 0.2 fusion.1
  69.5 23.9 %all_to_all.14 = f32[16,8,2176]{2,1,0:T(8,128)} all-to-all(f32[16,8,2176]{2,1,0:T(8,128)S(1)} %fusion.1), channel_id=1, replica_groups=mesh['z'=4,'k'=2,'y'=4,'x'=4] {'z','x'}, dimensions={0} | all-to-all | bytes 2228224 | tf_op jit(solution)/shard_map/all_to_all | solution.py:382
  93.4 1.9 reduce_sum.9
  95.3 0.0 all-gather.5.cloned.1.call-update
  95.4 0.0 reduce-scatter.2.cloned.1.call-start
  95.4 0.0 copy-done.2
  95.4 39.9 %all_to_all.15 = f32[4,128,1536]{2,1,0:T(8,128)S(1)} all-to-all(f32[4,128,1536]{2,1,0:T(8,128)S(1)} %copy-done.2), channel_id=1, replica_groups=mesh['z'=4,'k'=2,'y'=4,'x'=4] {'y'}, dimensions={0} | all-to-all | bytes 6291456 | tf_op jit(solution)/shard_map/all_to_all | solution.py:387
  135.3 4.0 %collective-permute-start = (f32[512,1536]{1,0:T(8,128)S(1)}, f32[512,1536]{1,0:T(8,128)S(1)}, u32[]{:S(2)}, u32[]{:S(2)}) collective-permute-start(f32[512,1536]{1,0:T(8,128)S(1)} %bitcast.9), channel_id=1, source_target_pairs={{0,16},{16,0},{1,17},{17,1},{2,18},{18,2},{3,19},{19,3},{4,20},{20... | collective-permute-start | bytes 9437192 | tf_op jit(solution)/shard_map/ppermute | solution.py:389
  139.3 5.3 %collective-permute-done.far_ref = f32[512,1536]{1,0:T(8,128)S(1)} collective-permute-done((f32[512,1536]{1,0:T(8,128)S(1)}, f32[512,1536]{1,0:T(8,128)S(1)}, u32[]{:S(2)}, u32[]{:S(2)}) %collective-permute-start) | collective-permute-done | bytes 3145760 | tf_op jit(solution)/shard_map/ppermute | solution.py:389
  144.6 0.0 copy-start
  144.6 3.4 %copy-done = f32[1024,2048]{1,0:T(8,128)S(1)} copy-done((f32[1024,2048]{1,0:T(8,128)S(1)}, f32[1024,2048]{1,0:T(8,128)}, u32[]{:S(2)}) %copy-start) | copy-done | bytes 8388632
  148.0 16.1 %strips.1 = f32[4,4,256,384]{3,2,1,0:T(8,128)S(1)} custom-call(s32[1]{0:T(128)} %bitcast.k_ref, f32[1024,2048]{1,0:T(8,128)S(1)} %copy-done, f32[512,1536]{1,0:T(8,128)S(1)} %bitcast.10, f32[512,1536]{1,0:T(8,128)S(1)} %collective-permute-done.far_ref), custom_call_target="tpu_custom_call" | custom-call | flops 9663676416 | bytes 41943040 | tf_op jit(solution)/shard_map/strips/pallas_call | solution.py:337
  164.2 0.0 copy-start.1
  164.2 2.7 %copy-done.1 = f32[4,4,256,384]{3,2,1,0:T(8,128)} copy-done((f32[4,4,256,384]{3,2,1,0:T(8,128)}, f32[4,4,256,384]{3,2,1,0:T(8,128)S(1)}, u32[]{:S(2)}) %copy-start.1) | copy-done | bytes 6291480
  166.9 0.0 reduce-scatter.2.cloned.1.call-update
  166.9 0.6 pad_add_fusion.place_ref
  167.5 0.0 all-gather.5.cloned.1.call-done.packed_ref
  167.5 74.2 %factor.1 = (f32[256,128]{1,0:T(8,128)}, f32[256,128]{1,0:T(8,128)}) custom-call(s32[2]{0:T(128)} %pad_add_fusion.place_ref, f32[1024,2176]{1,0:T(8,128)} %all-gather.5.cloned.1.call-done.packed_ref), custom_call_target="tpu_custom_call" | custom-call | flops 17179869184 | bytes 314572800 | tf_op jit(solution)/shard_map/factor/pallas_call | solution.py:238
  241.7 7.0 %reduce-scatter.2.cloned.1.call-done = f32[256,384]{1,0:T(8,128)} async-done(((f32[4096,384]{1,0:T(8,128)}), f32[256,384]{1,0:T(8,128)}) %reduce-scatter.2.cloned.1.call-update) | async-done | bytes 393232 | tf_op jit(solution)/shard_map/reduce_scatter | solution.py:391
  248.8 1.9 pad_maximum_fusion
  (1 shorter events, 0.0 us)
Async XLA Ops:
  7.2 54.5 %all-gather.3.cloned.1.call-start = ((), (), s32[]{:S(2)}) async-start(), calls=%async_computation.3 | async-start | bytes 9437184 | tf_op jit(solution)/shard_map/all_gather | solution.py:371
  10.3 157.2 %all-gather.5.cloned.1.call-start = ((), (), s32[]{:S(2)}) async-start(), calls=%async_computation.5 | async-start | bytes 8982528 | tf_op jit(solution)/shard_map/all_gather | solution.py:385
  69.4 26.1 %copy-start.2 = (f32[4,128,1536]{2,1,0:T(8,128)S(1)}, f32[4,128,1536]{2,1,0:T(8,128)}, u32[]{:S(2)}) copy-start(f32[4,128,1536]{2,1,0:T(8,128)} %mask_rest.1) | copy-start | bytes 9437188
  95.4 153.4 %reduce-scatter.2.cloned.1.call-start = ((), (), s32[]{:S(2)}) async-start(), calls=%async_computation.4 | async-start | bytes 6684672 | tf_op jit(solution)/shard_map/reduce_scatter | solution.py:391
  135.3 9.3 %collective-permute-start = (f32[512,1536]{1,0:T(8,128)S(1)}, f32[512,1536]{1,0:T(8,128)S(1)}, u32[]{:S(2)}, u32[]{:S(2)}) collective-permute-start(f32[512,1536]{1,0:T(8,128)S(1)} %bitcast.9), channel_id=1, source_target_pairs={{0,16},{16,0},{1,17},{17,1},{2,18},{18,2},{3,19},{19,3},{4,20},{20... | collective-permute-start | bytes 9437192 | tf_op jit(solution)/shard_map/ppermute | solution.py:389
  144.6 3.4 %copy-start = (f32[1024,2048]{1,0:T(8,128)S(1)}, f32[1024,2048]{1,0:T(8,128)}, u32[]{:S(2)}) copy-start(f32[1024,2048]{1,0:T(8,128)} %all-gather.3.cloned.1.call-done.left_ref) | copy-start | bytes 25165828
  164.2 2.7 %copy-start.1 = (f32[4,4,256,384]{3,2,1,0:T(8,128)}, f32[4,4,256,384]{3,2,1,0:T(8,128)S(1)}, u32[]{:S(2)}) copy-start(f32[4,4,256,384]{3,2,1,0:T(8,128)S(1)} %strips.1) | copy-start | bytes 18874372
Sparse Core Ops, SparseCore 0:
  10.4 51.2 all-gather.2
  95.5 70.9 all-gather.4
  170.0 78.7 reduce-scatter.1

commit v11 on v10

--- a/solution.py
+++ b/solution.py
@@ -17,15 +17,15 @@
     lane = lax.broadcasted_iota(jnp.int32, S, 1)
     subl = lax.broadcasted_iota(jnp.int32, S, 0)
     F = list(F)
-    Ws = []
-    onehot = [jnp.where(subl == k, 1.0, 0.0) for k in range(8)]
+    Ws, Us = [], []
     n = len(F)
     spread = lambda x, at: [jnp.broadcast_to(x[:, at + k:at + k + 1], S) for k in range(8)]
     D = spread(F[0], 0)
     for t in range(n):
         b = 8 * t
         inblk = (lane >= b) & (lane < b + 8)
-        X = jnp.where(inblk, jnp.where(lane - b == subl, 1.0, 0.0), F[t])
+        X = F[t]
+        Z = jnp.where(lane - b == subl, 1.0, 0.0)
         if t + 1 < n:
             first = spread(F[t + 1], b)
             B = list(first)
@@ -35,33 +35,43 @@
             for s in range(t + 2, n):
                 C[s, k] = jnp.broadcast_to(F[s][:, b + k:b + k + 1], S)
         G = jnp.zeros(S, jnp.float32)
+        H = jnp.zeros(S, jnp.float32)
+        scaled, f = [], {}
         for k in range(8):
             d = jnp.broadcast_to(D[k][k:k + 1], S)
             rs = lax.rsqrt(d)
             inv = 1.0 / d
-            g = D[k] - onehot[k]
+            g = jnp.where(subl > k, D[k], 0.0)
             xk = jnp.broadcast_to(X[k:k + 1], S)
+            zk = jnp.broadcast_to(Z[k:k + 1], S)
             G = jnp.where(subl == k, xk * rs, G)
+            H = jnp.where(subl == k, zk * rs, H)
             X = X - g * (xk * inv)
+            Z = Z - g * (zk * inv)
+            scaled.append(jnp.where(inblk, zk, xk) * inv)
             for m in range(k + 1, 8):
-                f = jnp.broadcast_to(D[m][k:k + 1], S) * inv
-                D[m] = D[m] - g * f
+                f[k, m] = jnp.broadcast_to(D[m][k:k + 1], S) * inv
+                D[m] = D[m] - g * f[k, m]
                 if t + 1 < n:
-                    B[m] = B[m] - B[k] * f
+                    B[m] = B[m] - B[k] * f[k, m]
             if t + 1 < n:
                 y = B[k] * inv
                 N = [N[m] - B[k] * jnp.broadcast_to(y[m:m + 1], S) for m in range(8)]
-        Ws.append(jnp.where(lane < b + 8, G, 0.0))
+        Ws.append(jnp.where(lane < b, G, jnp.where(inblk, H, 0.0)))
+        Us.append(jnp.where(lane >= b + subl, G, 0.0))
         if t + 1 < n:
-            V = [jnp.broadcast_to(X[k:k + 1], S) for k in range(8)]
+            V = list(scaled)
+            for m in range(7, 0, -1):
+                for k in range(m):
+                    V[k] = V[k] - f[k, m] * V[m]
             for s in range(t + 1, n):
-                f = jnp.where(inblk, 0.0, F[s])
+                row = jnp.where(inblk, 0.0, F[s])
                 for k in range(8):
-                    f = f - (first[k] if s == t + 1 else C[s, k]) * V[k]
-                F[s] = f
+                    row = row - (first[k] if s == t + 1 else C[s, k]) * V[k]
+                F[s] = row
             D = N
         beside(t)
-    return Ws
+    return Ws, Us
 
 
 def split(x, n):
@@ -106,7 +116,7 @@
 
 def chol_kernel(nparts, place_ref, packed_ref, band_ref, out_ref, a_ref, *scratch):
     Ls = scratch[:nparts]
-    P, Q, W, sems = scratch[nparts:]
+    P, Q, W, U, sems = scratch[nparts:]
     n = a_ref.shape[0]
     nb = n // BLK
     np2 = n // 256
@@ -195,10 +205,14 @@
             if t % 2 == 0 and t // 2 < units:
                 unit(t // 2)
         P[pl.ds(here, BLK), :BLK] += shift
-        ws = diag128([P[pl.ds(pl.multiple_of(here + 8 * s, 8), 8), :128] for s in range(16)], beside)
+        ws, us = diag128([P[pl.ds(pl.multiple_of(here + 8 * s, 8), 8), :128] for s in range(16)], beside)
         for s in range(16):
             W[8 * s:8 * s + 8, :] = ws[s]
-        w = split(W[...], 3)
+            U[8 * s:8 * s + 8, :] = us[s]
+        w = W[...]
+        off = jnp.where(row_of == col_of, 1.0, 0.0) - dot_nt_narrow(split(w, 3), split(U[...], 3))
+        w = w + jnp.dot(off.astype(jnp.bfloat16), w.astype(jnp.bfloat16), preferred_element_type=jnp.float32)
+        w = split(w, 3)
         def rows(i):
             at = pl.ds(i * BT, BT)
             l = dot_nt_narrow(split(P[at, :128], 3), w)
@@ -242,7 +256,7 @@
         out_specs=(vmem, vmem),
         scratch_shapes=[pltpu.VMEM((n, n), jnp.float32)]
         + [pltpu.VMEM((n, n), jnp.bfloat16)] * nparts
-        + [pltpu.VMEM((n, 256), jnp.float32), pltpu.VMEM((n + 256, 256), jnp.float32), pltpu.VMEM((BLK, BLK), jnp.float32), pltpu.SemaphoreType.DMA((2 * nb,))],
+        + [pltpu.VMEM((n, 256), jnp.float32), pltpu.VMEM((n + 256, 256), jnp.float32), pltpu.VMEM((BLK, BLK), jnp.float32), pltpu.VMEM((BLK, BLK), jnp.float32), pltpu.SemaphoreType.DMA((2 * nb,))],
         compiler_params=pltpu.CompilerParams(vmem_limit_bytes=56 * 2**20),
         cost_estimate=pl.CostEstimate(flops=2 * n * n * n, bytes_accessed=300 * 2**20, transcendentals=n),
         name="factor",
@@ -347,7 +361,7 @@
                 pltpu.VMEM((nx // 2, 2, 3 * users // 2, 2 * cols), jnp.bfloat16),
             ],
         ),
-        compiler_params=pltpu.CompilerParams(vmem_limit_bytes=32 * 2**20),
+        compiler_params=pltpu.CompilerParams(vmem_limit_bytes=56 * 2**20),
         cost_estimate=pl.CostEstimate(flops=6 * users * nz * rows * nx * cols, bytes_accessed=40 * 2**20, transcendentals=0),
         name="strips",
     )(k.reshape(1).astype(jnp.int32), bands, own, far)

time: 259 us -> 265 us (1.023)
  Pallas kernels: 97.9 us -> 114 us
  waiting for transfers between devices: 59.2 us -> 52.2 us
  local copies, waits for them, and re-layouts: 7.5 us -> 3.13 us
    pallas_call x1, Pallas kernels: 74.2 us -> 85.6 us  [chol_piece(): pl.pallas_call(functools.partial(chol_kernel, nparts), out_shape=(flat, f...]
    reduce_scatter x1, waiting for transfers between devices: 7.04 us -> 0.02 us  [shards(): lax.psum_scatter(partial, ('x', 'z'), scatter_dimension=0, tiled=True)]
    pallas_call x1, Pallas kernels: 16.1 us -> 21.1 us  [strips(): pl.pallas_call(strips_kernel, out_shape=jax.ShapeDtypeStruct((nx, nz, row...]
    unnamed x6, local copies, waits for them, and re-layouts: 6.08 us -> 1.71 us
  transfers between devices with their start and end apart: 4 -> 4, of which waited for: 3 -> 2; matrix products, arithmetic and copies ran while one was open for 0% -> 0% of each run, Pallas kernels for 37% -> 42%
where the time goes in v11:
time: 265 us; the launch traced here: 262 us
  Pallas kernels  114 us (43%)
  blocking collectives  63.8 us (24%)
  waiting for transfers between devices  52.2 us (20%)
  between operations  13.8 us (5%)
  matrix products  6.25 us (2%)
  other arithmetic  4.56 us (2%)
  starting transfers between devices  4.14 us (2%)
  local copies, waits for them, and re-layouts  3.13 us (1%)
    pallas_call x1, Pallas kernels, chol_piece(): pl.pallas_call(functools.partial(chol_kernel, nparts), out_shape=(flat, f...  85.6 us
    all_gather x1, waiting for transfers between devices, shards(): bands = lax.all_gather(band, ('k', 'y'), axis=0, tiled=True)  46.8 us
    all_to_all x1, blocking collectives, shards(): own = lax.all_to_all(rest, 'y', split_axis=0, concat_axis=0, tiled=True)  39.9 us
    all_to_all x1, blocking collectives, shards(): lax.all_to_all(packed, ('z', 'x'), split_axis=0, concat_axis=0, tiled=True)  23.9 us
    pallas_call x1, Pallas kernels, strips(): pl.pallas_call(strips_kernel, out_shape=jax.ShapeDtypeStruct((nx, nz, row...  21.1 us
    dot_general x1, matrix products, shards(): lax.dot_general(jnp.concatenate([lower, upper], axis=1), bands, over_user...  6.25 us
  transfers between devices with their start and end apart: 4, of which 2 were waited for; matrix products, arithmetic and copies ran while one was open for 0% of the time, Pallas kernels for 42%

profile of v11, /device:TPU:17, one launch (start us, length us, event | category | flops | bytes accessed | tf_op | source)
XLA Modules:
  0.0 262.1 jit_solution(12166667796519346981)
XLA Ops:
  7.2 0.0 all-gather.3.cloned.1.call-start
  7.2 3.0 %mask_band.1 = f32[128,2048]{1,0:T(8,128)} custom-call(s32[1,64]{1,0:T(1,128)} %keep_ref.3, f32[128,8192]{1,0:T(8,128)} %slab_ref.3), custom_call_target="tpu_custom_call" | custom-call | tf_op jit(solution)/shard_map/mask_band/pallas_call | solution.py:283
  10.3 0.0 all-gather.3.cloned.1.call-update
  10.3 0.0 all-gather.5.cloned.1.call-start
  10.3 4.5 %mask_rest.1 = f32[4,128,1536]{2,1,0:T(8,128)} custom-call(s32[1,64]{1,0:T(1,128)} %keep_ref.3, f32[128,8192]{1,0:T(8,128)} %slab_ref.3), custom_call_target="tpu_custom_call" | custom-call | flops 1048576 | bytes 8388608 | tf_op jit(solution)/shard_map/mask_rest/pallas_call | solution.py:309
  14.9 46.8 %all-gather.3.cloned.1.call-done.left_ref = f32[1024,2048]{1,0:T(8,128)} async-done(((f32[128,2048]{1,0:T(8,128)}), f32[1024,2048]{1,0:T(8,128)}) %all-gather.3.cloned.1.call-update) | async-done | bytes 8388624 | tf_op jit(solution)/shard_map/all_gather | solution.py:385
  61.7 1.3 constant_dynamic-slice_fusion.1
  63.0 6.3 %fusion.2 = f32[256,2048]{1,0:T(8,128)S(1)} fusion(f32[1024,2048]{1,0:T(8,128)} %all-gather.3.cloned.1.call-done.left_ref, f32[1024,128]{1,0:T(8,128)S(1)} %get-tuple-element.21, f32[1024,128]{1,0:T(8,128)S(1)} %get-tuple-element.20), kind=kOutput, calls=%fused_computation.3 | convolution fusion | flops 3221487616 | bytes 11534336 | tf_op jit(solution)/shard_map/dot_general | solution.py:390
  69.2 0.1 fusion.7
  69.4 0.0 copy-start
  69.4 0.2 fusion.1
  69.5 23.9 %all_to_all.14 = f32[16,8,2176]{2,1,0:T(8,128)} all-to-all(f32[16,8,2176]{2,1,0:T(8,128)S(1)} %fusion.1), channel_id=1, replica_groups=mesh['z'=4,'k'=2,'y'=4,'x'=4] {'z','x'}, dimensions={0} | all-to-all | bytes 2228224 | tf_op jit(solution)/shard_map/all_to_all | solution.py:396
  93.4 1.9 reduce_sum.9
  95.3 0.0 all-gather.5.cloned.1.call-update
  95.4 0.0 reduce-scatter.2.cloned.1.call-start
  95.4 0.0 copy-done
  95.4 39.9 %all_to_all.15 = f32[4,128,1536]{2,1,0:T(8,128)S(1)} all-to-all(f32[4,128,1536]{2,1,0:T(8,128)S(1)} %copy-done), channel_id=1, replica_groups=mesh['z'=4,'k'=2,'y'=4,'x'=4] {'y'}, dimensions={0} | all-to-all | bytes 6291456 | tf_op jit(solution)/shard_map/all_to_all | solution.py:401
  135.3 0.0 copy-start.1
  135.3 4.0 %collective-permute-start = (f32[512,1536]{1,0:T(8,128)S(1)}, f32[512,1536]{1,0:T(8,128)S(1)}, u32[]{:S(2)}, u32[]{:S(2)}) collective-permute-start(f32[512,1536]{1,0:T(8,128)S(1)} %bitcast.9), channel_id=1, source_target_pairs={{0,16},{16,0},{1,17},{17,1},{2,18},{18,2},{3,19},{19,3},{4,20},{20... | collective-permute-start | bytes 9437192 | tf_op jit(solution)/shard_map/ppermute | solution.py:403
  139.3 5.3 %collective-permute-done.far_ref = f32[512,1536]{1,0:T(8,128)S(1)} collective-permute-done((f32[512,1536]{1,0:T(8,128)S(1)}, f32[512,1536]{1,0:T(8,128)S(1)}, u32[]{:S(2)}, u32[]{:S(2)}) %collective-permute-start) | collective-permute-done | bytes 3145760 | tf_op jit(solution)/shard_map/ppermute | solution.py:403
  144.6 0.0 copy-start.2
  144.6 0.0 copy-done.1
  144.6 1.7 copy-done.2
  146.3 21.1 %strips.1 = f32[4,4,256,384]{3,2,1,0:T(8,128)} custom-call(s32[1]{0:T(128)} %bitcast.k_ref, f32[1024,2048]{1,0:T(8,128)} %all-gather.3.cloned.1.call-done.left_ref, f32[512,1536]{1,0:T(8,128)} %bitcast.10, f32[512,1536]{1,0:T(8,128)} %copy-done.2), custom_call_target="tpu_custom_call" | custom-call | flops 9663676416 | bytes 41943040 | tf_op jit(solution)/shard_map/strips/pallas_call | solution.py:351
  167.4 0.0 reduce-scatter.2.cloned.1.call-update
  167.4 0.6 pad_add_fusion.place_ref
  168.0 0.0 all-gather.5.cloned.1.call-done.packed_ref
  168.0 85.6 %factor.1 = (f32[256,128]{1,0:T(8,128)}, f32[256,128]{1,0:T(8,128)}) custom-call(s32[2]{0:T(128)} %pad_add_fusion.place_ref, f32[1024,2176]{1,0:T(8,128)} %all-gather.5.cloned.1.call-done.packed_ref), custom_call_target="tpu_custom_call" | custom-call | flops 17179869184 | bytes 314572800 | tf_op jit(solution)/shard_map/factor/pallas_call | solution.py:252
  253.6 0.0 reduce-scatter.2.cloned.1.call-done
  253.7 1.9 pad_maximum_fusion
  (1 shorter events, 0.0 us)
Async XLA Ops:
  7.2 54.5 %all-gather.3.cloned.1.call-start = ((), (), s32[]{:S(2)}) async-start(), calls=%async_computation.3 | async-start | bytes 9437184 | tf_op jit(solution)/shard_map/all_gather | solution.py:385
  10.3 157.7 %all-gather.5.cloned.1.call-start = ((), (), s32[]{:S(2)}) async-start(), calls=%async_computation.5 | async-start | bytes 8982528 | tf_op jit(solution)/shard_map/all_gather | solution.py:399
  69.4 26.1 %copy-start = (f32[4,128,1536]{2,1,0:T(8,128)S(1)}, f32[4,128,1536]{2,1,0:T(8,128)}, u32[]{:S(2)}) copy-start(f32[4,128,1536]{2,1,0:T(8,128)} %mask_rest.1) | copy-start | bytes 9437188
  95.4 158.3 %reduce-scatter.2.cloned.1.call-start = ((), (), s32[]{:S(2)}) async-start(), calls=%async_computation.4 | async-start | bytes 6684672 | tf_op jit(solution)/shard_map/reduce_scatter | solution.py:405
  135.3 9.3 %copy-start.1 = (f32[4,128,1536]{2,1,0:T(8,128)}, f32[4,128,1536]{2,1,0:T(8,128)S(1)}, u32[]{:S(2)}) copy-start(f32[4,128,1536]{2,1,0:T(8,128)S(1)} %all_to_all.15) | copy-start | bytes 9437188
  135.3 9.3 %collective-permute-start = (f32[512,1536]{1,0:T(8,128)S(1)}, f32[512,1536]{1,0:T(8,128)S(1)}, u32[]{:S(2)}, u32[]{:S(2)}) collective-permute-start(f32[512,1536]{1,0:T(8,128)S(1)} %bitcast.9), channel_id=1, source_target_pairs={{0,16},{16,0},{1,17},{17,1},{2,18},{18,2},{3,19},{19,3},{4,20},{20... | collective-permute-start | bytes 9437192 | tf_op jit(solution)/shard_map/ppermute | solution.py:403
  144.6 1.7 copy-start.2
Sparse Core Ops, SparseCore 0:
  10.4 51.2 all-gather.2
  95.5 70.9 all-gather.4
  170.0 78.8 reduce-scatter.1

commit v12 on v11

--- a/solution.py
+++ b/solution.py
@@ -201,14 +201,27 @@
             dst = pl.multiple_of(jnp.where(real, i, np2) * 256, 256)
             ks = pl.ds(pl.multiple_of(jnp.where(real, at % deep, 0) * 256, 256), 256)
             Q[pl.ds(dst, 256), :] -= dot_nt([L[pl.ds(src, 256), ks] for L in Ls], [L[pl.ds(pl.multiple_of(later * 256, 256), 256), ks] for L in Ls])
-        def beside(t):
-            if t % 2 == 0 and t // 2 < units:
-                unit(t // 2)
+        def block_inverse(some):
+            def beside(t):
+                if some and t % 2 == 0 and t // 2 < units:
+                    unit(t // 2)
+
+            ws, us = diag128([P[pl.ds(pl.multiple_of(here + 8 * s, 8), 8), :128] for s in range(16)], beside)
+            for s in range(16):
+                W[8 * s:8 * s + 8, :] = ws[s]
+                U[8 * s:8 * s + 8, :] = us[s]
+
         P[pl.ds(here, BLK), :BLK] += shift
-        ws, us = diag128([P[pl.ds(pl.multiple_of(here + 8 * s, 8), 8), :128] for s in range(16)], beside)
-        for s in range(16):
-            W[8 * s:8 * s + 8, :] = ws[s]
-            U[8 * s:8 * s + 8, :] = us[s]
+        none = J2 * (np2 - 1 - J2) == 0
+
+        @pl.when(none)
+        def _():
+            block_inverse(False)
+
+        @pl.when(jnp.logical_not(none))
+        def _():
+            block_inverse(True)
+
         w = W[...]
         off = jnp.where(row_of == col_of, 1.0, 0.0) - dot_nt_narrow(split(w, 3), split(U[...], 3))
         w = w + jnp.dot(off.astype(jnp.bfloat16), w.astype(jnp.bfloat16), preferred_element_type=jnp.float32)

time: 265 us -> 259 us (0.977)
  Pallas kernels: 114 us -> 108 us
    pallas_call x1, Pallas kernels: 85.6 us -> 79.5 us  [chol_piece(): pl.pallas_call(functools.partial(chol_kernel, nparts), out_shape=(flat, f...]
  transfers between devices with their start and end apart: 4 -> 4, of which waited for: 2 -> 3; matrix products, arithmetic and copies ran while one was open for 0% -> 0% of each run, Pallas kernels for 42% -> 41%
where the time goes in v12:
time: 259 us; the launch traced here: 257 us
  Pallas kernels  108 us (42%)
  blocking collectives  63.8 us (25%)
  waiting for transfers between devices  53.6 us (21%)
  between operations  13.8 us (5%)
  matrix products  6.25 us (2%)
  other arithmetic  4.55 us (2%)
  starting transfers between devices  4.14 us (2%)
  local copies, waits for them, and re-layouts  3.13 us (1%)
    pallas_call x1, Pallas kernels, chol_piece(): pl.pallas_call(functools.partial(chol_kernel, nparts), out_shape=(flat, f...  79.5 us
    all_gather x1, waiting for transfers between devices, shards(): bands = lax.all_gather(band, ('k', 'y'), axis=0, tiled=True)  46.8 us
    all_to_all x1, blocking collectives, shards(): own = lax.all_to_all(rest, 'y', split_axis=0, concat_axis=0, tiled=True)  39.9 us
    all_to_all x1, blocking collectives, shards(): lax.all_to_all(packed, ('z', 'x'), split_axis=0, concat_axis=0, tiled=True)  23.9 us
    pallas_call x1, Pallas kernels, strips(): pl.pallas_call(strips_kernel, out_shape=jax.ShapeDtypeStruct((nx, nz, row...  21.1 us
    dot_general x1, matrix products, shards(): lax.dot_general(jnp.concatenate([lower, upper], axis=1), bands, over_user...  6.25 us
    ppermute x1, waiting for transfers between devices, shards(): far = lax.ppermute(own, 'k', [(0, 1), (1, 0)])  5.29 us
  transfers between devices with their start and end apart: 4, of which 3 were waited for; matrix products, arithmetic and copies ran while one was open for 0% of the time, Pallas kernels for 41%

profile of v12, /device:TPU:17, one launch (start us, length us, event | category | flops | bytes accessed | tf_op | source)
XLA Modules:
  0.0 257.3 jit_solution(1061059981935349884)
XLA Ops:
  7.2 0.0 all-gather.3.cloned.1.call-start
  7.2 3.0 %mask_band.1 = f32[128,2048]{1,0:T(8,128)} custom-call(s32[1,64]{1,0:T(1,128)} %keep_ref.3, f32[128,8192]{1,0:T(8,128)} %slab_ref.3), custom_call_target="tpu_custom_call" | custom-call | tf_op jit(solution)/shard_map/mask_band/pallas_call | solution.py:296
  10.3 0.0 all-gather.3.cloned.1.call-update
  10.3 0.0 all-gather.5.cloned.1.call-start
  10.3 4.5 %mask_rest.1 = f32[4,128,1536]{2,1,0:T(8,128)} custom-call(s32[1,64]{1,0:T(1,128)} %keep_ref.3, f32[128,8192]{1,0:T(8,128)} %slab_ref.3), custom_call_target="tpu_custom_call" | custom-call | flops 1048576 | bytes 8388608 | tf_op jit(solution)/shard_map/mask_rest/pallas_call | solution.py:322
  14.9 46.8 %all-gather.3.cloned.1.call-done.left_ref = f32[1024,2048]{1,0:T(8,128)} async-done(((f32[128,2048]{1,0:T(8,128)}), f32[1024,2048]{1,0:T(8,128)}) %all-gather.3.cloned.1.call-update) | async-done | bytes 8388624 | tf_op jit(solution)/shard_map/all_gather | solution.py:398
  61.7 1.3 constant_dynamic-slice_fusion.1
  63.0 6.3 %fusion.2 = f32[256,2048]{1,0:T(8,128)S(1)} fusion(f32[1024,2048]{1,0:T(8,128)} %all-gather.3.cloned.1.call-done.left_ref, f32[1024,128]{1,0:T(8,128)S(1)} %get-tuple-element.21, f32[1024,128]{1,0:T(8,128)S(1)} %get-tuple-element.20), kind=kOutput, calls=%fused_computation.3 | convolution fusion | flops 3221487616 | bytes 11534336 | tf_op jit(solution)/shard_map/dot_general | solution.py:403
  69.2 0.1 fusion.7
  69.4 0.0 copy-start
  69.4 0.2 fusion.1
  69.5 23.9 %all_to_all.14 = f32[16,8,2176]{2,1,0:T(8,128)} all-to-all(f32[16,8,2176]{2,1,0:T(8,128)S(1)} %fusion.1), channel_id=1, replica_groups=mesh['z'=4,'k'=2,'y'=4,'x'=4] {'z','x'}, dimensions={0} | all-to-all | bytes 2228224 | tf_op jit(solution)/shard_map/all_to_all | solution.py:409
  93.4 1.9 reduce_sum.9
  95.3 0.0 all-gather.5.cloned.1.call-update
  95.4 0.0 reduce-scatter.2.cloned.1.call-start
  95.4 0.0 copy-done
  95.4 39.9 %all_to_all.15 = f32[4,128,1536]{2,1,0:T(8,128)S(1)} all-to-all(f32[4,128,1536]{2,1,0:T(8,128)S(1)} %copy-done), channel_id=1, replica_groups=mesh['z'=4,'k'=2,'y'=4,'x'=4] {'y'}, dimensions={0} | all-to-all | bytes 6291456 | tf_op jit(solution)/shard_map/all_to_all | solution.py:414
  135.3 0.0 copy-start.1
  135.3 4.0 %collective-permute-start = (f32[512,1536]{1,0:T(8,128)S(1)}, f32[512,1536]{1,0:T(8,128)S(1)}, u32[]{:S(2)}, u32[]{:S(2)}) collective-permute-start(f32[512,1536]{1,0:T(8,128)S(1)} %bitcast.9), channel_id=1, source_target_pairs={{0,16},{16,0},{1,17},{17,1},{2,18},{18,2},{3,19},{19,3},{4,20},{20... | collective-permute-start | bytes 9437192 | tf_op jit(solution)/shard_map/ppermute | solution.py:416
  139.3 5.3 %collective-permute-done.far_ref = f32[512,1536]{1,0:T(8,128)S(1)} collective-permute-done((f32[512,1536]{1,0:T(8,128)S(1)}, f32[512,1536]{1,0:T(8,128)S(1)}, u32[]{:S(2)}, u32[]{:S(2)}) %collective-permute-start) | collective-permute-done | bytes 3145760 | tf_op jit(solution)/shard_map/ppermute | solution.py:416
  144.6 0.0 copy-start.2
  144.6 0.0 copy-done.1
  144.6 1.7 copy-done.2
  146.3 21.1 %strips.1 = f32[4,4,256,384]{3,2,1,0:T(8,128)} custom-call(s32[1]{0:T(128)} %bitcast.k_ref, f32[1024,2048]{1,0:T(8,128)} %all-gather.3.cloned.1.call-done.left_ref, f32[512,1536]{1,0:T(8,128)} %bitcast.10, f32[512,1536]{1,0:T(8,128)} %copy-done.2), custom_call_target="tpu_custom_call" | custom-call | flops 9663676416 | bytes 41943040 | tf_op jit(solution)/shard_map/strips/pallas_call | solution.py:364
  167.4 0.0 reduce-scatter.2.cloned.1.call-update
  167.4 0.6 pad_add_fusion.place_ref
  168.0 0.0 all-gather.5.cloned.1.call-done.packed_ref
  168.0 79.5 %factor.1 = (f32[256,128]{1,0:T(8,128)}, f32[256,128]{1,0:T(8,128)}) custom-call(s32[2]{0:T(128)} %pad_add_fusion.place_ref, f32[1024,2176]{1,0:T(8,128)} %all-gather.5.cloned.1.call-done.packed_ref), custom_call_target="tpu_custom_call" | custom-call | flops 17179869184 | bytes 314572800 | tf_op jit(solution)/shard_map/factor/pallas_call | solution.py:265
  247.5 1.4 reduce-scatter.2.cloned.1.call-done
  249.0 1.9 pad_maximum_fusion
  (1 shorter events, 0.0 us)
Async XLA Ops:
  7.2 54.5 %all-gather.3.cloned.1.call-start = ((), (), s32[]{:S(2)}) async-start(), calls=%async_computation.3 | async-start | bytes 9437184 | tf_op jit(solution)/shard_map/all_gather | solution.py:398
  10.3 157.7 %all-gather.5.cloned.1.call-start = ((), (), s32[]{:S(2)}) async-start(), calls=%async_computation.5 | async-start | bytes 8982528 | tf_op jit(solution)/shard_map/all_gather | solution.py:412
  69.4 26.1 %copy-start = (f32[4,128,1536]{2,1,0:T(8,128)S(1)}, f32[4,128,1536]{2,1,0:T(8,128)}, u32[]{:S(2)}) copy-start(f32[4,128,1536]{2,1,0:T(8,128)} %mask_rest.1) | copy-start | bytes 9437188
  95.4 153.6 %reduce-scatter.2.cloned.1.call-start = ((), (), s32[]{:S(2)}) async-start(), calls=%async_computation.4 | async-start | bytes 6684672 | tf_op jit(solution)/shard_map/reduce_scatter | solution.py:418
  135.3 9.3 %copy-start.1 = (f32[4,128,1536]{2,1,0:T(8,128)}, f32[4,128,1536]{2,1,0:T(8,128)S(1)}, u32[]{:S(2)}) copy-start(f32[4,128,1536]{2,1,0:T(8,128)S(1)} %all_to_all.15) | copy-start | bytes 9437188
  135.3 9.3 %collective-permute-start = (f32[512,1536]{1,0:T(8,128)S(1)}, f32[512,1536]{1,0:T(8,128)S(1)}, u32[]{:S(2)}, u32[]{:S(2)}) collective-permute-start(f32[512,1536]{1,0:T(8,128)S(1)} %bitcast.9), channel_id=1, source_target_pairs={{0,16},{16,0},{1,17},{17,1},{2,18},{18,2},{3,19},{19,3},{4,20},{20... | collective-permute-start | bytes 9437192 | tf_op jit(solution)/shard_map/ppermute | solution.py:416
  144.6 1.7 copy-start.2
Sparse Core Ops, SparseCore 0:
  10.4 51.2 all-gather.2
  95.5 70.9 all-gather.4
  170.0 78.9 reduce-scatter.1
